TPU v7x, 32 devices: a whole 2x2x4 slice. The times are simulated.
32 devices in a mesh: comp: 8 (over z, y), band: 4 (over x, core).
Axes of the slice: x: 2, y: 2, z: 4, core: 2. Of those that a mesh axis runs over, the one named last changes fastest.
Arguments:
- spectra: bfloat16 [32, 36, 16, 1440], P('comp', None, 'band'), may hold values from 0 to 6, as said below
- depth_class: int32 [16, 1440], P('band'), may hold values from 0 to 63
- group_speed: float32 [64, 32], replicated, may hold values from 0.15 to 0.5
- current: float32 [2, 16, 1440], P(None, 'band'), may hold values from -0.3 to 0.3
- depth_slope: float32 [2, 16, 1440], P(None, 'band'), may hold values from -4 to 4
- wind: float32 [2, 16, 1440], P(None, 'band'), may hold values from -32 to 32
- land_mask: int32 [16, 1440], P('band'), may hold values from 0 to 1, as said below
- block_counts: int32 [4, 8], P('band'), may hold values from 210 to 630, as said below
Outputs:
- spectra_out: bfloat16 [1152, 20160], P(None, ('comp', 'band'))
Inputs may be any that keep to these rules, and one draw needn't show every extreme that they name: `spectra`: nonnegative densities. `land_mask`: band b's rows hold exactly as many sea cells as row b of block_counts sums to. `block_counts`: in every band one block has exactly 630 sea points.
All inputs are finite; a program needn't handle non-finite values.
Results may differ from a plain program's by a relative error of at most 0.0004.
Values may be sent and summed in bfloat16 or wider, within the bound.
No kernel may reach another device: no remote copies, remote signals or barrier semaphores. Data moves between devices by JAX's collectives and lax.ppermute only.
A program may use at most 64 MiB of HBM per device.

v0:
```python
import math

import jax
import jax.numpy as jnp
from jax import lax
from jax.sharding import PartitionSpec as P

GROWTH_RATE = 0.05
DAMPING = 1.5
TURNING_SCALE = 0.5


def extended(x, sides, width):
    for axis, dim in sides:
        size, length = (lax.axis_size(axis), x.shape[dim])
        up = [(i, (i + 1) % size) for i in range(size - 1)]
        down = [(j, i) for i, j in up]
        last = lax.slice_in_dim(x, length - width, length, axis=dim)
        initial = lax.slice_in_dim(x, 0, width, axis=dim)
        before = lax.ppermute(last, axis, up)
        after = lax.ppermute(initial, axis, down)
        x = jnp.concatenate([before, x, after], axis=dim)
    return x


def upwind(far_behind, behind, centre, ahead, far_ahead, celerity):
    forward = (2.0 * ahead + 3.0 * centre - 6.0 * behind + far_behind) / 6.0
    backward = (-far_ahead + 6.0 * ahead - 3.0 * centre - 2.0 * behind) / 6.0
    return celerity * jnp.where(celerity > 0, forward, backward)


def wrapped(values, celerity, axis):
    return upwind(
        jnp.roll(values, 2, axis),
        jnp.roll(values, 1, axis),
        values,
        jnp.roll(values, -1, axis),
        jnp.roll(values, -2, axis),
        celerity,
    )


def frequencies(count):
    angular = 2.0 * math.pi * 0.0418 * jnp.power(1.1, jnp.arange(count, dtype=jnp.float32))
    return (angular / angular[-1], 9.81 / angular)


def angles(count):
    heading = jnp.arange(count, dtype=jnp.float32) * (2.0 * math.pi / count)
    return (jnp.cos(heading), jnp.sin(heading))


def block_lists(band_mask, block_sizes, slot_count):
    sea_flag = (band_mask.reshape(-1) == 0).astype(jnp.int32)
    cell_count = sea_flag.shape[0]
    running = jnp.cumsum(sea_flag)
    starts = jnp.cumsum(block_sizes) - block_sizes
    slot_ids = jnp.arange(slot_count, dtype=jnp.int32)
    wanted = starts[:, None] + slot_ids[None, :] + 1
    found = jnp.searchsorted(running, wanted.reshape(-1), side="left")
    found = jnp.minimum(found, cell_count - 1).reshape(wanted.shape)
    return jnp.where(slot_ids[None, :] < block_sizes[:, None], found, -1)


def sources(values, mean_sq, wind_u, wind_v, ratio, phase, cos_t, sin_t):
    strength = jnp.sqrt(mean_sq + 1e-06)
    wind_along = (
        wind_u[None, None, :] * cos_t[None, :, None] + wind_v[None, None, :] * sin_t[None, :, None]
    )
    growth = (
        GROWTH_RATE
        * ratio[:, None, None]
        * jnp.maximum(wind_along / phase[:, None, None] - 1.0, 0.0)
    )
    decay = DAMPING * ratio[:, None, None] * strength[None, None, :]
    return values * jnp.exp(growth - decay)


def body(spectra, depth_class, group_speed, current, depth_slope, wind, land_mask, block_counts):
    freq_dev, dir_count, row_count, lon_count = spectra.shape
    depth_count, total_freqs = group_speed.shape
    groups = lax.axis_size("comp")
    slot_count = row_count * lon_count * 7 // (8 * groups)
    comp_index = lax.axis_index("comp")
    band_index = lax.axis_index("band")
    total_rows = row_count * lax.axis_size("band")
    sea_flag = (land_mask == 0).astype(jnp.float32)
    cos_t, sin_t = angles(dir_count)
    ratio, phase = frequencies(total_freqs)
    selector = (
        depth_class.reshape(1, -1) == jnp.arange(depth_count, dtype=jnp.int32)[:, None]
    ).astype(jnp.float32)
    speeds = jnp.dot(group_speed.T, selector, precision=lax.Precision.HIGHEST).reshape(
        total_freqs, row_count, lon_count
    )
    celerity = lax.dynamic_slice_in_dim(speeds, comp_index * freq_dev, freq_dev, 0)[:, None]
    row_ids = (band_index * row_count + jnp.arange(row_count, dtype=jnp.int32)).astype(jnp.float32)
    latitude = (-60.0 + 120.0 * (row_ids + 0.5) / total_rows) * (math.pi / 180.0)
    stretch = 1.0 / jnp.cos(latitude)
    masked = spectra * sea_flag.astype(jnp.bfloat16)
    padded = extended(masked, (("band", 2),), 2).astype(jnp.float32)
    density = padded[:, :, 2:-2]
    speed_x = celerity * cos_t[None, :, None, None] * stretch[None, None, :, None] + current[0]
    speed_y = celerity * sin_t[None, :, None, None] + current[1]
    across = upwind(
        padded[:, :, :-4],
        padded[:, :, 1:-3],
        density,
        padded[:, :, 3:-1],
        padded[:, :, 4:],
        speed_y,
    )
    advected = (density - wrapped(density, speed_x, 3) - across) * sea_flag
    turning = (
        TURNING_SCALE
        * celerity
        * (
            sin_t[None, :, None, None] * depth_slope[0]
            - cos_t[None, :, None, None] * depth_slope[1]
        )
    )
    refracted = (advected - wrapped(advected, turning, 1)) * sea_flag
    slot_cells = block_lists(land_mask, block_counts[0], slot_count)
    own_cells = lax.dynamic_index_in_dim(slot_cells, comp_index, 0, keepdims=False)
    occupied = (own_cells >= 0).astype(jnp.float32)
    all_cells = jnp.maximum(slot_cells, 0).reshape(-1)
    wind_east = wind[0].reshape(-1)
    wind_north = wind[1].reshape(-1)
    flattened = refracted.reshape(freq_dev * dir_count, row_count * lon_count)
    picked = jnp.take(flattened, all_cells, axis=1).reshape(
        freq_dev * dir_count, groups, slot_count
    )
    arrived = lax.all_to_all(picked, "comp", split_axis=1, concat_axis=0, tiled=True)
    values = arrived.reshape(total_freqs, dir_count, slot_count)
    mean_sq = jnp.mean(values * values, axis=(0, 1))
    safe_cells = jnp.maximum(own_cells, 0)
    finished = sources(
        values,
        mean_sq,
        jnp.take(wind_east, safe_cells),
        jnp.take(wind_north, safe_cells),
        ratio,
        phase,
        cos_t,
        sin_t,
    )
    result = (
        (finished * occupied[None, None, :])
        .astype(jnp.bfloat16)
        .reshape(total_freqs * dir_count, slot_count)
    )
    return result


def solution(mesh):
    return jax.shard_map(
        body,
        mesh=mesh,
        in_specs=(
            P("comp", None, "band", None),
            P("band", None),
            P(),
            P(None, "band", None),
            P(None, "band", None),
            P(None, "band", None),
            P("band", None),
            P("band", None),
        ),
        out_specs=P(None, ("comp", "band")),
        check_vma=False,
    )
```

profile of v0, /device:TPU:1, one launch (start us, length us, event | category | flops | bytes accessed | tf_op | source)
XLA Modules:
  0.0 548.4 jit_solution(7798837147033370381)
XLA Ops:
  4.1 4.5 collective-permute-start
  16.0 372.4 %while.24 = (s32[]{:T(128)}, u32[5040]{0:T(1024)S(1)}, u32[5040]{0:T(1024)S(1)}, s32[5760]{0:T(1024)S(1)}, s32[8]{0:T(128)S(1)}, /*index=5*/s32[]{:T(128)}, s32[]{:T(128)}, s32[]{}) while((s32[]{:T(128)}, u32[5040]{0:T(1024)S(1)}, u32[5040]{0:T(1024)S(1)}, s32[5760]{0:T(1024)S(1)}, s32[8]{0:T(128)S(1)}, /*index=5*/s32[]{:T(128)}, ...), condition=%wide.region_4.5_spmd.clone, body=%wide.region_3.4_spmd.clone.sunk | while | flops 105924 | bytes 433901 | solution.py:60
  16.2 28.4 %gather_fusion = s32[5040]{0:T(1024)S(1)} fusion(s32[5760]{0:T(1024)S(1)} %get-tuple-element.195, u32[5120]{0:T(1024)S(1)} %pad_clamp_fusion.4), kind=kCustom, calls=%fused_computation.clone.clone.1 | custom fusion | bytes 60480 | tf_op jit(solution)/shard_map/jit(searchsorted)/jit(_searchsorted_scan_impl)/vmap(jit(_searchsorted_scan_impl))/while/body/eval_jaxpr/gather | solution.py:60
  44.8 28.4 %gather_fusion = s32[5040]{0:T(1024)S(1)} fusion(s32[5760]{0:T(1024)S(1)} %get-tuple-element.195, u32[5120]{0:T(1024)S(1)} %pad_clamp_fusion.4), kind=kCustom, calls=%fused_computation.clone.clone.1 | custom fusion | bytes 60480 | tf_op jit(solution)/shard_map/jit(searchsorted)/jit(_searchsorted_scan_impl)/vmap(jit(_searchsorted_scan_impl))/while/body/eval_jaxpr/gather | solution.py:60
  73.4 28.4 %gather_fusion = s32[5040]{0:T(1024)S(1)} fusion(s32[5760]{0:T(1024)S(1)} %get-tuple-element.195, u32[5120]{0:T(1024)S(1)} %pad_clamp_fusion.4), kind=kCustom, calls=%fused_computation.clone.clone.1 | custom fusion | bytes 60480 | tf_op jit(solution)/shard_map/jit(searchsorted)/jit(_searchsorted_scan_impl)/vmap(jit(_searchsorted_scan_impl))/while/body/eval_jaxpr/gather | solution.py:60
  102.1 28.4 %gather_fusion = s32[5040]{0:T(1024)S(1)} fusion(s32[5760]{0:T(1024)S(1)} %get-tuple-element.195, u32[5120]{0:T(1024)S(1)} %pad_clamp_fusion.4), kind=kCustom, calls=%fused_computation.clone.clone.1 | custom fusion | bytes 60480 | tf_op jit(solution)/shard_map/jit(searchsorted)/jit(_searchsorted_scan_impl)/vmap(jit(_searchsorted_scan_impl))/while/body/eval_jaxpr/gather | solution.py:60
  130.7 28.4 %gather_fusion = s32[5040]{0:T(1024)S(1)} fusion(s32[5760]{0:T(1024)S(1)} %get-tuple-element.195, u32[5120]{0:T(1024)S(1)} %pad_clamp_fusion.4), kind=kCustom, calls=%fused_computation.clone.clone.1 | custom fusion | bytes 60480 | tf_op jit(solution)/shard_map/jit(searchsorted)/jit(_searchsorted_scan_impl)/vmap(jit(_searchsorted_scan_impl))/while/body/eval_jaxpr/gather | solution.py:60
  159.3 28.4 %gather_fusion = s32[5040]{0:T(1024)S(1)} fusion(s32[5760]{0:T(1024)S(1)} %get-tuple-element.195, u32[5120]{0:T(1024)S(1)} %pad_clamp_fusion.4), kind=kCustom, calls=%fused_computation.clone.clone.1 | custom fusion | bytes 60480 | tf_op jit(solution)/shard_map/jit(searchsorted)/jit(_searchsorted_scan_impl)/vmap(jit(_searchsorted_scan_impl))/while/body/eval_jaxpr/gather | solution.py:60
  187.9 28.4 %gather_fusion = s32[5040]{0:T(1024)S(1)} fusion(s32[5760]{0:T(1024)S(1)} %get-tuple-element.195, u32[5120]{0:T(1024)S(1)} %pad_clamp_fusion.4), kind=kCustom, calls=%fused_computation.clone.clone.1 | custom fusion | bytes 60480 | tf_op jit(solution)/shard_map/jit(searchsorted)/jit(_searchsorted_scan_impl)/vmap(jit(_searchsorted_scan_impl))/while/body/eval_jaxpr/gather | solution.py:60
  216.6 28.4 %gather_fusion = s32[5040]{0:T(1024)S(1)} fusion(s32[5760]{0:T(1024)S(1)} %get-tuple-element.195, u32[5120]{0:T(1024)S(1)} %pad_clamp_fusion.4), kind=kCustom, calls=%fused_computation.clone.clone.1 | custom fusion | bytes 60480 | tf_op jit(solution)/shard_map/jit(searchsorted)/jit(_searchsorted_scan_impl)/vmap(jit(_searchsorted_scan_impl))/while/body/eval_jaxpr/gather | solution.py:60
  245.2 28.4 %gather_fusion = s32[5040]{0:T(1024)S(1)} fusion(s32[5760]{0:T(1024)S(1)} %get-tuple-element.195, u32[5120]{0:T(1024)S(1)} %pad_clamp_fusion.4), kind=kCustom, calls=%fused_computation.clone.clone.1 | custom fusion | bytes 60480 | tf_op jit(solution)/shard_map/jit(searchsorted)/jit(_searchsorted_scan_impl)/vmap(jit(_searchsorted_scan_impl))/while/body/eval_jaxpr/gather | solution.py:60
  273.8 28.4 %gather_fusion = s32[5040]{0:T(1024)S(1)} fusion(s32[5760]{0:T(1024)S(1)} %get-tuple-element.195, u32[5120]{0:T(1024)S(1)} %pad_clamp_fusion.4), kind=kCustom, calls=%fused_computation.clone.clone.1 | custom fusion | bytes 60480 | tf_op jit(solution)/shard_map/jit(searchsorted)/jit(_searchsorted_scan_impl)/vmap(jit(_searchsorted_scan_impl))/while/body/eval_jaxpr/gather | solution.py:60
  302.5 28.4 %gather_fusion = s32[5040]{0:T(1024)S(1)} fusion(s32[5760]{0:T(1024)S(1)} %get-tuple-element.195, u32[5120]{0:T(1024)S(1)} %pad_clamp_fusion.4), kind=kCustom, calls=%fused_computation.clone.clone.1 | custom fusion | bytes 60480 | tf_op jit(solution)/shard_map/jit(searchsorted)/jit(_searchsorted_scan_impl)/vmap(jit(_searchsorted_scan_impl))/while/body/eval_jaxpr/gather | solution.py:60
  331.1 28.4 %gather_fusion = s32[5040]{0:T(1024)S(1)} fusion(s32[5760]{0:T(1024)S(1)} %get-tuple-element.195, u32[5120]{0:T(1024)S(1)} %pad_clamp_fusion.4), kind=kCustom, calls=%fused_computation.clone.clone.1 | custom fusion | bytes 60480 | tf_op jit(solution)/shard_map/jit(searchsorted)/jit(_searchsorted_scan_impl)/vmap(jit(_searchsorted_scan_impl))/while/body/eval_jaxpr/gather | solution.py:60
  359.7 28.4 %gather_fusion = s32[5040]{0:T(1024)S(1)} fusion(s32[5760]{0:T(1024)S(1)} %get-tuple-element.195, u32[5120]{0:T(1024)S(1)} %pad_clamp_fusion.4), kind=kCustom, calls=%fused_computation.clone.clone.1 | custom fusion | bytes 60480 | tf_op jit(solution)/shard_map/jit(searchsorted)/jit(_searchsorted_scan_impl)/vmap(jit(_searchsorted_scan_impl))/while/body/eval_jaxpr/gather | solution.py:60
  394.6 4.5 fusion.40
  402.5 6.9 %fusion.11 = f32[4,36,4,1440]{3,1,2,0:T(8,128)S(1)} fusion(f32[4,36,8,1440]{3,1,2,0:T(8,128)S(1)} %maximum_convert_fusion, f32[4,36,4,1438]{3,1,2,0:T(8,128)S(1)} %copy-done.3, f32[4,36,4,2]{3,1,2,0:T(8,128)S(1)} %get-tuple-element.128, f32[4,36,4,2]{3,1,2,0:T(8,128)S(1)} %get-tuple-element.127, f32[4,36,4,1438]{3,1,2,0:T(8,128)S(1)} %copy-done.2, ...), kind=kLoop, calls=%fused_computation.23 | loop fusion | flops 37324800 | bytes 33339184 | tf_op jit(solution)/shard_map/mul | solution.py:113
  411.6 4.5 fusion.3
  422.3 5.7 %copy.17 = f32[144,5760]{0,1:T(8,128)} copy(f32[144,5760]{1,0:T(8,128)} %reshape.273) | data formatting | bytes 6635520 | tf_op jit(solution)/shard_map/reshape | solution.py:129
  428.1 22.7 %gather_fusion.1 = f32[5040,144]{1,0:T(8,128)} fusion(f32[144,5760]{0,1:T(8,128)} %copy.17, s32[5120]{0:T(1024)S(1)} %copy-done.7), kind=kCustom, calls=%fused_computation.3 | custom fusion | bytes 5826240 | tf_op jit(solution)/shard_map/jit(_take)/gather | solution.py:130
  450.8 5.6 %copy.18 = f32[144,5040]{1,0:T(8,128)} copy(f32[144,5040]{0,1:T(8,128)} %bitcast.33) | data formatting | bytes 5806080 | tf_op jit(solution)/shard_map/jit(_take)/gather | solution.py:130
  462.2 5.7 %all-to-all-start = ((f32[144,8,630]{2,0,1:T(8,128)}), f32[144,8,630]{2,0,1:T(8,128)S(1)}, u32[]{:S(2)}, u32[]{:S(2)}) async-start(f32[144,8,630]{2,0,1:T(8,128)} %copy.19), calls=%async_computation | async-start | bytes 5898240 | tf_op jit(solution)/shard_map/all_to_all | solution.py:133
  484.7 49.4 %all-to-all-done = f32[144,8,630]{2,0,1:T(8,128)S(1)} async-done(((f32[144,8,630]{2,0,1:T(8,128)}), f32[144,8,630]{2,0,1:T(8,128)S(1)}, u32[]{:S(2)}, u32[]{:S(2)}) %all-to-all-start) | async-done | bytes 2903072 | tf_op jit(solution)/shard_map/all_to_all | solution.py:133
  540.5 4.4 fusion.32
  (204 shorter events, 64.4 us)
Async XLA Ops:
  0.0 10.7 %copy-start = (f32[64,32]{0,1:T(8,128)S(1)}, f32[64,32]{0,1:T(8,128)}, u32[]{:S(2)}) copy-start(f32[64,32]{0,1:T(8,128)} %param.14) | copy-start | bytes 24580
  0.0 10.6 %copy-start.13 = (s32[4,1440]{1,0:T(4,128)S(1)}, s32[4,1440]{1,0:T(4,128)}, u32[]{:S(2)}) copy-start(s32[4,1440]{1,0:T(4,128)} %param.13) | copy-start | bytes 69124
  2.6 12.3 %copy-start.8 = (f32[2,4,1440]{2,1,0:T(4,128)S(1)}, f32[2,4,1440]{2,1,0:T(4,128)}, u32[]{:S(2)}) copy-start(f32[2,4,1440]{2,1,0:T(4,128)} %param.15) | copy-start | bytes 138244
  2.6 13.1 %copy-start.18 = (s32[1,8]{1,0:T(1,128)S(1)}, s32[1,8]{1,0:T(1,128)}, u32[]{:S(2)}) copy-start(s32[1,8]{1,0:T(1,128)} %param.19) | copy-start | bytes 100
  4.1 387.2 %collective-permute-start = (bf16[4,36,2,1440]{3,1,2,0:T(8,128)(2,1)}, bf16[4,36,2,1440]{3,1,2,0:T(8,128)(2,1)S(1)}, u32[]{:S(2)}, u32[]{:S(2)}) collective-permute-start(bf16[4,36,2,1440]{3,1,2,0:T(8,128)(2,1)} %get-tuple-element.129), channel_id=1, source_target_pairs={{0,1},{1,2},{2,3},{4,5},{5,6},{6,7},{8,9},{9,10},{10,11},{12,13},{... | collective-permute-start | bytes 2488328 | tf_op jit(solution)/shard_map/ppermute | solution.py:20
  8.6 382.7 %collective-permute-start.1 = (bf16[4,36,2,1440]{3,1,2,0:T(8,128)(2,1)}, bf16[4,36,2,1440]{3,1,2,0:T(8,128)(2,1)}, u32[]{:S(2)}, u32[]{:S(2)}) collective-permute-start(bf16[4,36,2,1440]{3,1,2,0:T(8,128)(2,1)} %get-tuple-element.130), channel_id=1, source_target_pairs={{1,0},{2,1},{3,2},{5,4},{6,5},{7,6},{9,8},{10,9},{11,10},{13,12},{... | collective-permute-start | bytes 2488328 | tf_op jit(solution)/shard_map/ppermute | solution.py:21
  10.6 388.8 %copy-start.14 = (f32[36]{0:T(128)}, f32[36]{0:T(128)S(1)}, u32[]{:S(2)}) copy-start(f32[36]{0:T(128)S(1)} %get-tuple-element.139) | copy-start | bytes 436
  10.6 388.8 %copy-start.16 = (f32[36]{0:T(128)}, f32[36]{0:T(128)S(1)}, u32[]{:S(2)}) copy-start(f32[36]{0:T(128)S(1)} %get-tuple-element.140) | copy-start | bytes 436
  16.0 374.2 %copy-start.9 = (f32[2,4,1440]{2,1,0:T(4,128)S(1)}, f32[2,4,1440]{2,1,0:T(4,128)}, u32[]{:S(2)}) copy-start(f32[2,4,1440]{2,1,0:T(4,128)} %param.16) | copy-start | bytes 138244
  388.3 4.8 copy-start.4
  388.4 80.4 %copy-start.11 = (pred[8,630]{1,0:T(8,128)(4,1)}, pred[8,630]{1,0:T(8,128)(4,1)S(1)}, u32[]{:S(2)}) copy-start(pred[8,630]{1,0:T(8,128)(4,1)S(1)} %iota_compare_fusion.2) | copy-start | bytes 15124
  399.2 2.1 copy-start.2
  399.2 3.3 copy-start.3
  410.4 1.2 copy-start.6
  422.3 5.7 %copy-start.7 = (s32[5120]{0:T(1024)S(1)}, s32[5120]{0:T(1024)}, u32[]{:S(2)}) copy-start(s32[5120]{0:T(1024)} %pad_clamp_fusion.1) | copy-start | bytes 61444
  462.2 6.3 %copy-start.5 = (u32[5040]{0:T(1024)S(1)}, u32[5040]{0:T(1024)}, u32[]{:S(2)}) copy-start(u32[5040]{0:T(1024)} %copy-done.4) | copy-start | bytes 60484
  462.2 6.4 %copy-start.10 = (f32[2,4,1440]{2,1,0:T(4,128)S(1)}, f32[2,4,1440]{2,1,0:T(4,128)}, u32[]{:S(2)}) copy-start(f32[2,4,1440]{2,1,0:T(4,128)} %param.17) | copy-start | bytes 138244
  462.2 71.8 %all-to-all-start = ((f32[144,8,630]{2,0,1:T(8,128)}), f32[144,8,630]{2,0,1:T(8,128)S(1)}, u32[]{:S(2)}, u32[]{:S(2)}) async-start(f32[144,8,630]{2,0,1:T(8,128)} %copy.19), calls=%async_computation | async-start | bytes 5898240 | tf_op jit(solution)/shard_map/all_to_all | solution.py:133
  468.9 7.8 %copy-start.15 = (f32[36]{0:T(128)S(1)}, f32[36]{0:T(128)}, u32[]{:S(2)}) copy-start(f32[36]{0:T(128)} %copy-done.14) | copy-start | bytes 436
  468.9 7.8 %copy-start.17 = (f32[36]{0:T(128)S(1)}, f32[36]{0:T(128)}, u32[]{:S(2)}) copy-start(f32[36]{0:T(128)} %copy-done.16) | copy-start | bytes 436
  478.6 5.3 copy-start.12
  540.5 8.0 %copy-start.1 = (f32[64,32]{0,1:T(8,128)S(1)}, f32[64,32]{0,1:T(8,128)}, u32[]{:S(2)}) copy-start(f32[64,32]{0,1:T(8,128)} %param.14) | copy-start | bytes 24580
where the time goes:
time: 549 us; the launch traced here: 548 us
  local copies, waits for them, and re-layouts  456 us (83%)
  waiting for transfers between devices  49.4 us (9%)
  other arithmetic  27.5 us (5%)
  starting transfers between devices  12.1 us (2%)
    gather x13, local copies, waits for them, and re-layouts, block_lists(): found = jnp.searchsorted(running, wanted.reshape(-1), side='left')  369 us
    all_to_all x1, waiting for transfers between devices, body(): lax.all_to_all(picked, 'comp', split_axis=1, concat_axis=0, tiled=True)  49.4 us
    gather x3, local copies, waits for them, and re-layouts, body(): jnp.take(flattened, all_cells, axis=1)  31.8 us
  transfers between devices with their start and end apart: 3, of which 1 were waited for; matrix products, arithmetic and copies ran while one was open for 72% of the time, Pallas kernels for 0%

commit v1 on v0

v1 whole, which is shorter than its diff:
```python
import functools
import math

import jax
import jax.numpy as jnp
import numpy as np
from jax import lax
from jax.experimental import pallas as pl
from jax.experimental.pallas import tpu as pltpu
from jax.sharding import PartitionSpec as P

GROWTH_RATE = 0.05
DAMPING = 1.5
TURNING_SCALE = 0.5

LANES = 128
SUBLANES = 8
UNIT = 9
WORDS = 5
STEP_COUNT = 65500.0
EXPONENT_ZERO = 99
WINDOW = 4
VMEM_BYTES = 32 * 1024 * 1024

F32 = jnp.float32
I32 = jnp.int32


def call(kernel, out_shape, cost, **options):
    flops, moved = cost
    return pl.pallas_call(
        kernel,
        out_shape=out_shape,
        cost_estimate=pl.CostEstimate(flops=flops, bytes_accessed=moved, transcendentals=0),
        compiler_params=pltpu.CompilerParams(vmem_limit_bytes=VMEM_BYTES),
        **options,
    )


def iota(shape, axis):
    return lax.broadcasted_iota(I32, shape, axis)


def upwind(speed, far_behind, behind, centre, ahead, far_ahead):
    positive = speed > 0
    near = jnp.where(positive, behind, ahead)
    after = jnp.where(positive, ahead, behind)
    far = jnp.where(positive, far_behind, far_ahead)
    return jnp.abs(speed) * (2.0 * after + far + 3.0 * (centre - 2.0 * near))


def arrange_kernel(x_ref, sea_ref, top_ref, bottom_ref, scratch):
    freqs, parts, step, rows, lon = x_ref.shape
    chunks = scratch.shape[1]
    tail = lon - (chunks - 1) * LANES
    filler = jnp.zeros((rows, LANES - tail), F32)
    lane = iota((SUBLANES * rows, LANES), 1)
    for j in range(step):
        for f in range(freqs):
            for h in range(parts):
                place = pl.ds(f * parts + h, rows, stride=SUBLANES)
                for k in range(chunks):
                    if k < chunks - 1:
                        piece = x_ref[f, h, j, :, k * LANES : (k + 1) * LANES].astype(F32)
                    else:
                        piece = x_ref[f, h, j, :, k * LANES : lon].astype(F32)
                        piece = jnp.concatenate([piece, filler], axis=1)
                    scratch[j, k, place, :] = piece
        initial = None
        for k in range(chunks):
            span = slice(k * LANES, (k + 1) * LANES)
            piece = scratch[j, k] * sea_ref[:, span]
            if k == 0:
                initial = piece
            if k == chunks - 1:
                wrapped = jnp.where(
                    lane < tail + 2,
                    pltpu.roll(initial, tail, axis=1),
                    pltpu.roll(piece, LANES - tail, axis=1),
                )
                piece = jnp.where(lane < tail, piece, wrapped)
            piece = piece.astype(jnp.bfloat16)
            top_ref[j, :, span] = piece[: 2 * SUBLANES]
            bottom_ref[j, :, span] = piece[2 * SUBLANES :]


def index_kernel(land_ref, counts_ref, cells_ref, ranges_ref):
    chunks = land_ref.shape[0]
    groups, _, slots = cells_ref.shape
    spans = slots // LANES
    sea = (land_ref[...] == 0).astype(jnp.bfloat16)
    square = (LANES, LANES)
    ones_before = (iota(square, 1) <= iota(square, 0)).astype(jnp.bfloat16)
    ranks = lax.dot_general(ones_before, sea, (((1,), (1,)), ((), ())), preferred_element_type=F32)
    totals = jnp.dot(sea, jnp.ones(square, jnp.bfloat16), preferred_element_type=F32)
    chunk_square = (chunks, chunks)
    chunks_before = (iota(chunk_square, 1) <= iota(chunk_square, 0)).astype(jnp.bfloat16)
    through = jnp.dot(chunks_before, totals.astype(jnp.bfloat16), preferred_element_type=F32)
    through_column = through[:, :1]
    total_column = totals[:, :1]
    ranks = ranks.astype(jnp.bfloat16)
    chunk_ids = iota((chunks, slots), 0)
    slot_ids = iota((1, slots), 1)
    span_lane = iota((1, LANES), 1)
    start = jnp.int32(0)
    for c in range(groups):
        count = counts_ref[0, c]
        number = (slot_ids + start).astype(F32)
        passed = (through_column <= number).astype(F32)
        chunk_of = jnp.sum(passed, axis=0, keepdims=True)
        before = jnp.sum(passed * total_column, axis=0, keepdims=True)
        chunk_of = chunk_of.astype(I32)
        chosen = (chunk_ids == chunk_of).astype(jnp.bfloat16)
        inside = jnp.dot(ranks, chosen, preferred_element_type=F32)
        lane = jnp.sum((inside <= number - before).astype(F32), axis=0, keepdims=True)
        valid = slot_ids < count
        found = jnp.where(valid, chunk_of * LANES + lane.astype(I32), -1)
        cells_ref[c] = jnp.broadcast_to(found, (SUBLANES, slots))
        bounds = jnp.zeros((1, LANES), I32)
        for m in range(spans):
            span = slice(m * LANES, (m + 1) * LANES)
            own = chunk_of[:, span].astype(F32)
            low = jnp.min(jnp.where(valid[:, span], own, float(chunks)), axis=1, keepdims=True)
            high = jnp.max(jnp.where(valid[:, span], own, -1.0), axis=1, keepdims=True)
            bounds = jnp.where(span_lane == m, low.astype(I32), bounds)
            bounds = jnp.where(span_lane == m + spans, high.astype(I32), bounds)
        ranges_ref[c : c + 1, :] = bounds
        start = start + count


def advect_kernel(
    top_ref, bottom_ref, table_ref, depth_ref, fields_ref, stretch_ref, trig_ref, out_ref, coef_ref, scratch
):
    turns, _, padded = top_ref.shape
    rows = depth_ref.shape[0]
    chunks = padded // LANES
    table = table_ref[...]
    for r in range(rows):
        place = slice(r * SUBLANES, (r + 1) * SUBLANES)
        for k in range(chunks):
            span = slice(k * LANES, (k + 1) * LANES)

            def field(n):
                return jnp.broadcast_to(fields_ref[n, r : r + 1, span], (SUBLANES, LANES))

            classes = jnp.broadcast_to(depth_ref[r : r + 1, span], (SUBLANES, LANES))
            sixth = jnp.take_along_axis(table, classes, axis=1, mode="promise_in_bounds") * (1.0 / 6.0)
            coef_ref[0, place, span] = sixth
            coef_ref[1, place, span] = field(1) * (1.0 / 6.0)
            coef_ref[2, place, span] = sixth * TURNING_SCALE * field(2)
            coef_ref[3, place, span] = sixth * TURNING_SCALE * field(3)
            scratch[0, place, span] = sixth * stretch_ref[r]
            scratch[1, place, span] = field(0) * (1.0 / 6.0)

    width = LANES * (4 if chunks % 4 == 0 else 1)

    def window(ref, j, low, high):
        parts = []
        if low < LANES:
            parts.append(ref[j, :, padded - LANES :])
            parts.append(ref[j, :, : min(high + LANES, padded)])
        else:
            parts.append(ref[j, :, low - LANES : min(high + LANES, padded)])
        if high + LANES > padded:
            parts.append(ref[j, :, :LANES])
        return jnp.concatenate([part.astype(F32) for part in parts], axis=1)

    def one_turn(j, carry):
        sin = trig_ref[0, j][:, :1]
        cos = trig_ref[1, j][:, :1]
        for low in range(0, padded, width):
            high = low + width
            centres, shifted = [], []
            for ref in (top_ref, bottom_ref):
                wide = window(ref, j, low, high)
                moved = [
                    pltpu.roll(wide, shift % wide.shape[1], axis=1)[:, LANES : LANES + width] for shift in (2, 1, -1, -2)
                ]
                for half in (slice(0, SUBLANES), slice(SUBLANES, 2 * SUBLANES)):
                    centres.append(wide[half, LANES : LANES + width])
                    shifted.append([one[half] for one in moved])
            for r in range(rows):
                place = slice(r * SUBLANES, (r + 1) * SUBLANES)
                span = slice(low, high)
                speed_x = scratch[0, place, span] * cos + scratch[1, place, span]
                speed_y = coef_ref[0, place, span] * sin + coef_ref[1, place, span]
                near = [centres[n] if 0 <= n < rows else 0.0 for n in range(r - 2, r + 3)]
                far_behind, behind, ahead, far_ahead = shifted[r]
                along = upwind(speed_x, far_behind, behind, centres[r], ahead, far_ahead)
                across = upwind(speed_y, *near)
                out_ref[j, place, span] = centres[r] - along - across
        return carry

    lax.fori_loop(0, turns, one_turn, 0)


def pack_kernel(
    group,
    freqs,
    adv_ref,
    above_ref,
    below_ref,
    coef_ref,
    trig_ref,
    scale_ref,
    cells_ref,
    ranges_ref,
    out_ref,
    packed,
):
    turns, height, padded = adv_ref.shape
    rows = height // SUBLANES
    chunks = padded // LANES
    parts = SUBLANES // freqs
    shape = (SUBLANES, LANES)
    part = iota(shape, 0) % parts
    scale = scale_ref[0]
    first = group * UNIT

    def turned(value, by):
        if by == 0:
            return value
        if by > 0:
            return jnp.where(
                part == parts - 1, pltpu.roll(value, parts - 1, axis=0), pltpu.roll(value, SUBLANES - 1, axis=0)
            )
        return jnp.where(part == 0, pltpu.roll(value, SUBLANES - parts + 1, axis=0), pltpu.roll(value, 1, axis=0))

    for r in range(rows):
        place = slice(r * SUBLANES, (r + 1) * SUBLANES)

        def one_chunk(k, carry):
            span = pl.ds(pl.multiple_of(k * LANES, LANES), LANES)
            sixth, current_y, turn_x, turn_y = [coef_ref[n, place, span] for n in range(4)]
            known = {}

            def advected(j):
                j = j % turns
                if j not in known:
                    speed = sixth * trig_ref[0, j] + current_y
                    positive = speed > 0
                    ref = above_ref if r < 2 else below_ref
                    outer = ref[j, :, span].astype(F32)
                    low, high = outer[:SUBLANES], outer[SUBLANES:]
                    if r == 0:
                        share = jnp.where(positive, low - 6.0 * high, 2.0 * high)
                    elif r == 1:
                        share = jnp.where(positive, high, 0.0)
                    elif r == rows - 2:
                        share = jnp.where(positive, 0.0, low)
                    else:
                        share = jnp.where(positive, 2.0 * low, high - 6.0 * low)
                    known[j] = adv_ref[j, place, span] - jnp.abs(speed) * share
                return known[j]

            around = {j: turned(advected(j), j // turns) for j in range(first - 2, first + UNIT + 2)}
            values = []
            for j in range(first, first + UNIT):
                speed = trig_ref[0, j] * turn_x - trig_ref[1, j] * turn_y
                values.append(around[j] - upwind(speed, *[around[n] for n in range(j - 2, j + 3)]))
            largest = functools.reduce(jnp.maximum, [jnp.abs(value) for value in values])
            level = jnp.ceil(jnp.log2(jnp.maximum(largest, 2.0**-98)))
            level = jnp.minimum(level, 28.0).astype(I32) + EXPONENT_ZERO
            level = jnp.maximum(level, 1)
            inverse = jnp.take_along_axis(scale, level, axis=1, mode="promise_in_bounds")
            codes = [(value * inverse + 65536.5).astype(I32) for value in values]
            chunk = r * chunks + k
            rest = codes[8] | (level << 17)
            for n in range(4):
                even, odd = codes[2 * n], codes[2 * n + 1]
                packed[chunk, n * SUBLANES : (n + 1) * SUBLANES, :] = even | (odd << 17)
                rest = rest | ((odd >> 15) << (24 + 2 * n))
            packed[chunk, 4 * SUBLANES :, :] = rest
            return carry

        lax.fori_loop(0, chunks, one_chunk, 0)

    groups, _, slots = out_ref.shape
    spans = slots // LANES
    last = rows * chunks - 1

    def one_block(c, carry):
        for m in range(spans):
            span = slice(m * LANES, (m + 1) * LANES)
            cells = cells_ref[c, :, span]
            low, high = ranges_ref[c, m], ranges_ref[c, m + spans]

            def merged(chunk, sums):
                lane = cells - chunk * LANES
                here = (lane >= 0) & (lane < LANES)
                lane = lane & (LANES - 1)
                return tuple(
                    jnp.where(
                        here,
                        jnp.take_along_axis(
                            packed[chunk, n * SUBLANES : (n + 1) * SUBLANES, :],
                            lane,
                            axis=1,
                            mode="promise_in_bounds",
                        ),
                        sums[n],
                    )
                    for n in range(WORDS)
                )

            sums = tuple(jnp.zeros(shape, I32) for _ in range(WORDS))
            for t in range(WINDOW):
                sums = merged(jnp.minimum(low + t, last), sums)
            for n in range(WORDS):
                out_ref[c, n * SUBLANES : (n + 1) * SUBLANES, span] = sums[n]

            @pl.when(high >= low + WINDOW)
            def _():
                again = tuple(out_ref[c, n * SUBLANES : (n + 1) * SUBLANES, span] for n in range(WORDS))
                again = lax.fori_loop(low + WINDOW, high + 1, merged, again)
                for n in range(WORDS):
                    out_ref[c, n * SUBLANES : (n + 1) * SUBLANES, span] = again[n]

        return carry

    lax.fori_loop(0, groups, one_block, 0)


def finish_kernel(units, *refs):
    arrived = refs[:units]
    wind_ref, count_ref, trig_ref, scale_ref, rate_ref, out_ref, values, ordered = refs[units:]
    groups = arrived[0].shape[0]
    turns = values.shape[1]
    shape = (SUBLANES, LANES)
    scale = scale_ref[1]

    def decode(source, sums):
        for unit in range(units):
            words = [arrived[unit][source, n * SUBLANES : (n + 1) * SUBLANES, :] for n in range(WORDS)]
            rest = words[4]
            level = lax.shift_right_logical(rest, 17) & 127
            size = jnp.take_along_axis(scale, level, axis=1, mode="promise_in_bounds")
            offset = size * 65536.0
            for n in range(UNIT):
                if n == 8:
                    code = rest & 0x1FFFF
                elif n % 2 == 0:
                    code = words[n // 2] & 0x1FFFF
                else:
                    code = lax.shift_right_logical(words[n // 2], 17) | (
                        lax.shift_right_logical(rest, 9 + n - 1) & 0x18000
                    )
                value = code.astype(F32) * size - offset
                values[source, unit * UNIT + n] = value
                sums = sums + value * value
        return sums

    sums = lax.fori_loop(0, groups, decode, jnp.zeros(shape, F32))
    mean_sq = jnp.sum(sums, axis=0, keepdims=True) / float(groups * turns * SUBLANES)
    strength = jnp.broadcast_to(jnp.sqrt(mean_sq + 1e-06), shape)
    east = jnp.broadcast_to(wind_ref[0:1, :], shape)
    north = jnp.broadcast_to(wind_ref[1:2, :], shape)
    occupied = (pl.program_id(0) * LANES + iota(shape, 1)) < count_ref[0]

    def weigh(source, carry):
        decay = rate_ref[0, source] * strength
        slope, threshold = rate_ref[1, source], rate_ref[2, source]
        for j in range(turns):
            along = east * trig_ref[1, j] + north * trig_ref[0, j]
            growth = jnp.maximum(along * slope - threshold, 0.0)
            value = values[source, j] * jnp.exp(growth - decay)
            ordered[pl.ds(source * (turns * SUBLANES) + j, SUBLANES, stride=turns), :] = jnp.where(occupied, value, 0.0)
        return carry

    lax.fori_loop(0, groups, weigh, 0)
    square = (LANES, LANES)
    unit_matrix = (iota(square, 0) == iota(square, 1)).astype(jnp.bfloat16)
    turned = lax.dot_general(
        unit_matrix,
        ordered[...].astype(jnp.bfloat16),
        (((1,), (1,)), ((), ())),
        preferred_element_type=F32,
    )
    out_ref[...] = turned.astype(jnp.bfloat16)


def body(spectra, depth_class, group_speed, current, depth_slope, wind, land_mask, block_counts):
    freqs, directions, rows, lon = spectra.shape
    depths, total_freqs = group_speed.shape
    groups = lax.axis_size("comp")
    bands = lax.axis_size("band")
    comp = lax.axis_index("comp")
    band = lax.axis_index("band")
    slot_count = rows * lon * 7 // (8 * groups)
    slots = -(-slot_count // LANES) * LANES
    parts = SUBLANES // freqs
    turns = directions // parts
    units = turns // UNIT
    chunks = -(-lon // LANES)
    padded = chunks * LANES
    height = rows * SUBLANES
    spare = ((0, 0), (0, padded - lon))
    hbm = 2 * turns * height * padded

    heading = 2.0 * math.pi / directions * (
        np.arange(parts)[None, None, :] * turns + np.arange(turns)[:, None, None]
    )
    heading = np.broadcast_to(heading, (turns, freqs, parts)).reshape(turns, SUBLANES, 1)
    trig = np.stack([np.sin(heading), np.cos(heading)])
    trig = jnp.asarray(np.broadcast_to(trig, (2, turns, SUBLANES, LANES)).astype(np.float32))
    angular = 2.0 * math.pi * 0.0418 * 1.1 ** np.arange(total_freqs)
    ratio = angular / angular[-1]
    phase = 9.81 / angular
    rates = np.stack([DAMPING * ratio, GROWTH_RATE * ratio / phase, GROWTH_RATE * ratio])
    rates = np.repeat(rates.reshape(3, groups, freqs), parts, axis=2)[..., None]
    rates = jnp.asarray(np.broadcast_to(rates, (3, groups, SUBLANES, LANES)).astype(np.float32))
    powers = 2.0 ** (np.arange(LANES) - EXPONENT_ZERO)
    scale = np.stack([STEP_COUNT / powers, powers / STEP_COUNT])[:, None, :]
    scale = jnp.asarray(np.broadcast_to(scale, (2, SUBLANES, LANES)).astype(np.float32))
    latitude = (-60.0 + 120.0 * (np.arange(rows * bands) + 0.5) / (rows * bands)) * (math.pi / 180.0)
    stretch = jnp.asarray((1.0 / np.cos(latitude)).astype(np.float32))
    stretch = lax.dynamic_slice_in_dim(stretch, band * rows, rows, 0)

    land = jnp.pad(land_mask, spare, constant_values=1)
    sea = jnp.repeat((land == 0).astype(F32), SUBLANES, axis=0)
    smem = pl.BlockSpec(memory_space=pltpu.SMEM)
    vmem = pl.BlockSpec(memory_space=pltpu.VMEM)

    step = 3
    half = jax.ShapeDtypeStruct((turns, height // 2, padded), jnp.bfloat16)
    half_spec = pl.BlockSpec((step, height // 2, padded), lambda i: (i, 0, 0))
    top, bottom = call(
        arrange_kernel,
        [half, half],
        (4 * hbm, 2 * hbm),
        grid=(turns // step,),
        in_specs=[
            pl.BlockSpec((freqs, parts, step, rows, lon), lambda i: (0, 0, i, 0, 0)),
            pl.BlockSpec((height, padded), lambda i: (0, 0)),
        ],
        out_specs=[half_spec, half_spec],
        scratch_shapes=[pltpu.VMEM((step, chunks, height, LANES), F32)],
    )(spectra.reshape(freqs, parts, turns, rows, lon), sea)
    down = [(i, i + 1) for i in range(bands - 1)]
    above = lax.ppermute(bottom, "band", down)
    below = lax.ppermute(top, "band", [(j, i) for i, j in down])

    cells, ranges = call(
        index_kernel,
        [jax.ShapeDtypeStruct((groups, SUBLANES, slots), I32), jax.ShapeDtypeStruct((groups, LANES), I32)],
        (100 * groups * slots, 8 * groups * slots),
        in_specs=[vmem, smem],
        out_specs=[vmem, vmem],
    )(land.reshape(rows * chunks, LANES), block_counts)

    table = lax.dynamic_slice_in_dim(group_speed.T, comp * freqs, freqs, 0)
    table = jnp.pad(jnp.repeat(table, parts, axis=0), ((0, 0), (0, LANES - depths)))
    fields = jnp.pad(jnp.concatenate([current, depth_slope]), ((0, 0),) + spare)
    depth = jnp.pad(depth_class, spare)
    advected, coefs = call(
        advect_kernel,
        [
            jax.ShapeDtypeStruct((turns, height, padded), F32),
            jax.ShapeDtypeStruct((4, height, padded), F32),
        ],
        (50 * hbm, 4 * hbm),
        in_specs=[vmem, vmem, vmem, vmem, vmem, smem, vmem],
        out_specs=[vmem, vmem],
        scratch_shapes=[pltpu.VMEM((2, height, padded), F32)],
    )(top, bottom, table, depth, fields, stretch, trig)

    arrived = []
    for unit in range(units):
        sent = call(
            functools.partial(pack_kernel, unit, freqs),
            jax.ShapeDtypeStruct((groups, WORDS * SUBLANES, slots), I32),
            (30 * hbm, 4 * hbm),
            in_specs=[vmem] * 7 + [smem],
            out_specs=vmem,
            scratch_shapes=[pltpu.VMEM((rows * chunks, WORDS * SUBLANES, LANES), I32)],
        )(advected, above, below, coefs, trig, scale, cells, ranges)
        arrived.append(lax.all_to_all(sent, "comp", split_axis=0, concat_axis=0, tiled=True))

    own = jnp.maximum(lax.dynamic_index_in_dim(cells, comp, 0, keepdims=False)[0], 0)
    winds = jnp.pad(wind, ((0, 0),) + spare).reshape(2, rows * padded)
    winds = jnp.stack([jnp.take(winds[0], own), jnp.take(winds[1], own)])
    own_count = lax.dynamic_slice_in_dim(block_counts[0], comp, 1, 0)

    total = total_freqs * directions
    result = call(
        functools.partial(finish_kernel, units),
        jax.ShapeDtypeStruct((slot_count, total), jnp.bfloat16),
        (50 * total * slots, 6 * total * slots),
        grid=(slots // LANES,),
        in_specs=[pl.BlockSpec((groups, WORDS * SUBLANES, LANES), lambda i: (0, 0, i))] * units
        + [
            pl.BlockSpec((2, LANES), lambda i: (0, i)),
            smem,
            pl.BlockSpec((2, turns, SUBLANES, LANES), lambda i: (0, 0, 0, 0)),
            pl.BlockSpec((2, SUBLANES, LANES), lambda i: (0, 0, 0)),
            pl.BlockSpec((3, groups, SUBLANES, LANES), lambda i: (0, 0, 0, 0)),
        ],
        out_specs=pl.BlockSpec((LANES, total), lambda i: (i, 0)),
        scratch_shapes=[
            pltpu.VMEM((groups, turns, SUBLANES, LANES), F32),
            pltpu.VMEM((total, LANES), F32),
        ],
    )(*arrived, winds, own_count, trig, scale, rates)
    return result.T


def solution(mesh):
    return jax.shard_map(
        body,
        mesh=mesh,
        in_specs=(
            P("comp", None, "band", None),
            P("band", None),
            P(),
            P(None, "band", None),
            P(None, "band", None),
            P(None, "band", None),
            P("band", None),
            P("band", None),
        ),
        out_specs=P(None, ("comp", "band")),
        check_vma=False,
    )
```

time: 549 us -> 104 us (0.19)
  local copies, waits for them, and re-layouts: 456 us -> 23.2 us
  Pallas kernels: 0 us -> 46.6 us
  waiting for transfers between devices: 49.4 us -> 14.2 us
  other arithmetic: 27.5 us -> 1.62 us
    gather x18 -> x2, local copies, waits for them, and re-layouts: 408 us -> 7.72 us  [body(): winds = jnp.stack([jnp.take(winds[0], own), jnp.take(winds[1], own)])]
    pallas_call x0 -> x6, Pallas kernels: none -> 46.6 us  [the longest x2 25 us: body(): call(functools.partial(pack_kernel, unit, freqs), jax.ShapeDtypeStruct((g...]
    all_to_all x1 -> x2, waiting for transfers between devices: 49.4 us -> 14.2 us  [body(): lax.all_to_all(sent, 'comp', split_axis=0, concat_axis=0, tiled=True)]
    mul x8 -> x0, other arithmetic: 15.6 us -> none  [the longest x1 6.94 us: body(): advected = (density - wrapped(density, speed_x, 3) - across) * sea_flag]
    reshape x4 -> x2, local copies, waits for them, and re-layouts: 12.6 us -> 0.03 us  [the longest x1 0.02 us: body(): land.reshape(rows * chunks, LANES)]
    unnamed x38 -> x56, local copies, waits for them, and re-layouts: 3.11 us -> 12.8 us
    slice x9 -> x1, local copies, waits for them, and re-layouts: 10.1 us -> 0.77 us  [body(): winds = jnp.stack([jnp.take(winds[0], own), jnp.take(winds[1], own)])]
    div x4 -> x0, local copies, waits for them, and re-layouts: 6.34 us -> none  [sources(): wind_along / phase[:, None, None] - 1.0]
  transfers between devices with their start and end apart: 3 -> 4, of which waited for: 1 -> 2; matrix products, arithmetic and copies ran while one was open for 72% -> 11% of each run, Pallas kernels for 0% -> 22%
where the time goes in v1:
time: 104 us; the launch traced here: 101 us
  Pallas kernels  46.6 us (45%)
  local copies, waits for them, and re-layouts  23.2 us (22%)
  starting transfers between devices  15.5 us (15%)
  waiting for transfers between devices  14.2 us (14%)
  other arithmetic  1.62 us (2%)
    pallas_call x2, Pallas kernels, body(): call(functools.partial(pack_kernel, unit, freqs), jax.ShapeDtypeStruct((g...  25 us
    all_to_all x2, waiting for transfers between devices, body(): lax.all_to_all(sent, 'comp', split_axis=0, concat_axis=0, tiled=True)  14.2 us
    unnamed x56, local copies, waits for them, and re-layouts  12.8 us
    all_to_all x2, starting transfers between devices, body(): lax.all_to_all(sent, 'comp', split_axis=0, concat_axis=0, tiled=True)  9.1 us
    pallas_call x1, Pallas kernels, body(): call(functools.partial(finish_kernel, units), jax.ShapeDtypeStruct((slot_...  8.96 us
    pallas_call x1, Pallas kernels, body(): call(advect_kernel, [jax.ShapeDtypeStruct((turns, height, padded), F32),...  7.9 us
    gather x2, local copies, waits for them, and re-layouts, body(): winds = jnp.stack([jnp.take(winds[0], own), jnp.take(winds[1], own)])  7.72 us
    ppermute x1, starting transfers between devices, body(): above = lax.ppermute(bottom, 'band', down)  4.5 us
  transfers between devices with their start and end apart: 4, of which 2 were waited for; matrix products, arithmetic and copies ran while one was open for 11% of the time, Pallas kernels for 22%

profile of v1, /device:TPU:1, one launch (start us, length us, event | category | flops | bytes accessed | tf_op | source)
XLA Modules:
  0.0 101.5 jit_solution(1809997647840024995)
XLA Ops:
  0.1 0.8 compare_convert_fusion
  0.9 1.5 %copy-done.8 = bf16[4,36,4,1440]{3,2,1,0:T(4,128)(2,1)S(1)} copy-done((bf16[4,36,4,1440]{3,2,1,0:T(4,128)(2,1)S(1)}, bf16[4,36,4,1440]{3,2,1,0:T(4,128)(2,1)}, u32[]{:S(2)}) %copy-start.8) | copy-done | bytes 1658904
  2.4 3.2 %shard_map.118 = (bf16[18,16,1536]{2,1,0:T(8,128)(2,1)}, bf16[18,16,1536]{2,1,0:T(8,128)(2,1)}) custom-call(bf16[4,2,18,4,1440]{4,3,2,1,0:T(4,128)(2,1)S(1)} %bitcast.8, f32[32,1536]{1,0:T(8,128)S(1)} %broadcast_bitcast_fusion.sea_ref), custom_call_target="tpu_custom_call" | custom-call | flops 7077888 | bytes 3538944 | tf_op jit(solution)/shard_map/pallas_call | solution.py:427
  5.5 4.5 %collective-permute-start = (bf16[18,16,1536]{2,1,0:T(8,128)(2,1)}, bf16[18,16,1536]{2,1,0:T(8,128)(2,1)}, u32[]{:S(2)}, u32[]{:S(2)}) collective-permute-start(bf16[18,16,1536]{2,1,0:T(8,128)(2,1)} %get-tuple-element.13.bottom_ref), channel_id=1, source_target_pairs={{0,1},{1,2},{2,3},{4,5},{5,6},{6,7},{8,9},{9,10},{10,11},{12,13},{... | collective-permute-start | bytes 2654216 | tf_op jit(solution)/shard_map/ppermute | solution.py:440
  10.0 1.9 %collective-permute-start.1 = (bf16[18,16,1536]{2,1,0:T(8,128)(2,1)}, bf16[18,16,1536]{2,1,0:T(8,128)(2,1)}, u32[]{:S(2)}, u32[]{:S(2)}) collective-permute-start(bf16[18,16,1536]{2,1,0:T(8,128)(2,1)} %get-tuple-element.12.top_ref), channel_id=1, source_target_pairs={{1,0},{2,1},{3,2},{5,4},{6,5},{7,6},{9,8},{10,9},{11,10},{13,12},{... | collective-permute-start | bytes 2654216 | tf_op jit(solution)/shard_map/ppermute | solution.py:441
  12.0 1.6 %shard_map.120 = (s32[8,8,640]{2,1,0:T(8,128)S(1)}, s32[8,128]{1,0:T(8,128)S(1)}) custom-call(s32[48,128]{1,0:T(8,128)S(1)} %reshape.30.land_ref, s32[1,8]{1,0:T(1,128)S(1)} %copy-done.21), custom_call_target="tpu_custom_call" | custom-call | flops 512000 | bytes 40960 | tf_op jit(solution)/shard_map/pallas_call | solution.py:443
  16.3 0.9 copy-done.5
  18.6 7.9 %shard_map.119 = (f32[18,32,1536]{2,1,0:T(8,128)S(1)}, f32[4,32,1536]{2,1,0:T(8,128)S(1)}) custom-call(bf16[18,16,1536]{2,1,0:T(8,128)(2,1)} %get-tuple-element.12.top_ref, bf16[18,16,1536]{2,1,0:T(8,128)(2,1)} %get-tuple-element.13.bottom_ref, f32[8,128]{1,0:T(8,128)S(1)} %copy-done.20, s32[4,1536]{1,0:T(4,128)S(1)} %copy-done.12, ...), custom_call_target="tpu_custom_call" | custom-call | flops 88473600 | bytes 7077888 | tf_op jit(solution)/shard_map/pallas_call | solution.py:455
  27.2 12.5 %shard_map.121 = s32[8,40,640]{2,1,0:T(8,128)S(1)} custom-call(f32[18,32,1536]{2,1,0:T(8,128)S(1)} %get-tuple-element.14.adv_ref, bf16[18,16,1536]{2,1,0:T(8,128)(2,1)} %collective-permute-done.above_ref, bf16[18,16,1536]{2,1,0:T(8,128)(2,1)} %collective-permute-done.1.below_ref, f32[4,32,1536]{2,1,0:T(8,128)S(1)} %get-tuple-element.15.coef_ref, ...), custom_call_target="tpu_custom_call" | custom-call | flops 53084160 | bytes 7077888 | tf_op jit(solution)/shard_map/pallas_call | solution.py:469
  39.7 0.9 copy-done.2
  40.6 0.9 copy-done.3
  41.5 5.6 %all-to-all-start = ((s32[8,40,640]{2,1,0:T(8,128)}), s32[8,40,640]{2,1,0:T(8,128)}, u32[]{:S(2)}, u32[]{:S(2)}) async-start(s32[8,40,640]{2,1,0:T(8,128)} %copy-done.2), calls=%async_computation | async-start | bytes 1638400 | tf_op jit(solution)/shard_map/all_to_all | solution.py:477
  47.1 1.1 %copy-done.4 = f32[4,32,1536]{2,1,0:T(8,128)S(1)} copy-done((f32[4,32,1536]{2,1,0:T(8,128)S(1)}, f32[4,32,1536]{2,1,0:T(8,128)}, u32[]{:S(2)}) %copy-start.4) | copy-done | bytes 786456
  48.2 0.9 copy-done.6
  49.1 0.9 copy-done.11
  51.4 12.5 %shard_map.122 = s32[8,40,640]{2,1,0:T(8,128)S(1)} custom-call(f32[18,32,1536]{2,1,0:T(8,128)S(1)} %get-tuple-element.14.adv_ref, bf16[18,16,1536]{2,1,0:T(8,128)(2,1)} %collective-permute-done.above_ref, bf16[18,16,1536]{2,1,0:T(8,128)(2,1)} %collective-permute-done.1.below_ref, f32[4,32,1536]{2,1,0:T(8,128)S(1)} %copy-done.4, ...), custom_call_target="tpu_custom_call" | custom-call | flops 53084160 | bytes 7077888 | tf_op jit(solution)/shard_map/pallas_call | solution.py:469
  63.9 0.9 copy-done.1
  64.8 3.7 %all-to-all-done.refs_0_ = s32[8,40,640]{2,1,0:T(8,128)} async-done(((s32[8,40,640]{2,1,0:T(8,128)}), s32[8,40,640]{2,1,0:T(8,128)}, u32[]{:S(2)}, u32[]{:S(2)}) %all-to-all-start) | async-done | bytes 819232 | tf_op jit(solution)/shard_map/all_to_all | solution.py:477
  68.5 3.5 %all-to-all-start.1 = ((s32[8,40,640]{2,1,0:T(8,128)}), s32[8,40,640]{2,1,0:T(8,128)S(1)}, u32[]{:S(2)}, u32[]{:S(2)}) async-start(s32[8,40,640]{2,1,0:T(8,128)} %copy-done.1), calls=%async_computation.1 | async-start | bytes 1638400 | tf_op jit(solution)/shard_map/all_to_all | solution.py:477
  72.0 0.8 pad_slice_fusion
  74.2 3.9 %gather_fusion = f32[640]{0:T(1024)S(1)} fusion(f32[6144]{0:T(1024)S(1)} %squeeze.10, s32[1024]{0:T(1024)S(1)} %pad_clamp_fusion), kind=kCustom, calls=%fused_computation.clone | custom fusion | bytes 7680 | tf_op jit(solution)/shard_map/jit(_take)/gather | solution.py:481
  78.1 3.9 %gather_fusion.1 = f32[640]{0:T(1024)S(1)} fusion(f32[6144]{0:T(1024)S(1)} %squeeze.11, s32[1024]{0:T(1024)S(1)} %pad_clamp_fusion), kind=kCustom, calls=%fused_computation.1.clone | custom fusion | bytes 7680 | tf_op jit(solution)/shard_map/jit(_take)/gather | solution.py:481
  82.0 10.5 %all-to-all-done.1.refs_1_ = s32[8,40,640]{2,1,0:T(8,128)S(1)} async-done(((s32[8,40,640]{2,1,0:T(8,128)}), s32[8,40,640]{2,1,0:T(8,128)S(1)}, u32[]{:S(2)}, u32[]{:S(2)}) %all-to-all-start.1) | async-done | bytes 819232 | tf_op jit(solution)/shard_map/all_to_all | solution.py:477
  92.5 9.0 %shard_map.123 = bf16[630,1152]{1,0:T(8,128)(2,1)} custom-call(s32[8,40,640]{2,1,0:T(8,128)} %all-to-all-done.refs_0_, s32[8,40,640]{2,1,0:T(8,128)S(1)} %all-to-all-done.1.refs_1_, f32[2,640]{1,0:T(2,128)S(1)} %pad_maximum_fusion.refs_2_, s32[1]{0:T(128)} %bitcast.4.refs_3_, f32[2,18,8,128]{3,2,1,0:T(8,128)S(1)} %copy-done.7, f32[2,8,128]{2,1,0:T(8,128)S(1)} %copy-done.16, ...), custom_call_target="tpu_custom_call" | custom-call | flops 36864000 | bytes 4423680 | tf_op jit(solution)/shard_map/pallas_call | solution.py:485
  (70 shorter events, 7.6 us)
Async XLA Ops:
  0.0 15.6 %copy-start = (f32[64,32]{0,1:T(8,128)S(1)}, f32[64,32]{0,1:T(8,128)}, u32[]{:S(2)}) copy-start(f32[64,32]{0,1:T(8,128)} %param.16) | copy-start | bytes 24580
  0.0 16.1 %copy-start.27 = (f32[16]{0:T(128)S(1)}, f32[16]{0:T(128)}, u32[]{:S(2)}) copy-start(f32[16]{0:T(128)} %constant.51.clone) | copy-start | bytes 196
  0.0 12.0 %copy-start.23 = (s32[4,1440]{1,0:T(4,128)S(1)}, s32[4,1440]{1,0:T(4,128)}, u32[]{:S(2)}) copy-start(s32[4,1440]{1,0:T(4,128)} %param.20) | copy-start | bytes 69124
  0.0 12.0 %copy-start.21 = (s32[1,8]{1,0:T(1,128)S(1)}, s32[1,8]{1,0:T(1,128)}, u32[]{:S(2)}) copy-start(s32[1,8]{1,0:T(1,128)} %counts_ref.1) | copy-start | bytes 100
  0.0 14.9 %copy-start.26 = (s32[4,1440]{1,0:T(4,128)S(1)}, s32[4,1440]{1,0:T(4,128)}, u32[]{:S(2)}) copy-start(s32[4,1440]{1,0:T(4,128)} %param.15) | copy-start | bytes 69124
  0.0 16.2 %copy-start.24 = (f32[2,4,1440]{2,1,0:T(4,128)S(1)}, f32[2,4,1440]{2,1,0:T(4,128)}, u32[]{:S(2)}) copy-start(f32[2,4,1440]{2,1,0:T(4,128)} %param.18) | copy-start | bytes 138244
  0.0 16.2 %copy-start.25 = (f32[2,4,1440]{2,1,0:T(4,128)S(1)}, f32[2,4,1440]{2,1,0:T(4,128)}, u32[]{:S(2)}) copy-start(f32[2,4,1440]{2,1,0:T(4,128)} %param.17) | copy-start | bytes 138244
  0.9 1.5 %copy-start.8 = (bf16[4,36,4,1440]{3,2,1,0:T(4,128)(2,1)S(1)}, bf16[4,36,4,1440]{3,2,1,0:T(4,128)(2,1)}, u32[]{:S(2)}) copy-start(bf16[4,36,4,1440]{3,2,1,0:T(4,128)(2,1)} %param.14) | copy-start | bytes 4976644
  5.5 21.0 %collective-permute-start = (bf16[18,16,1536]{2,1,0:T(8,128)(2,1)}, bf16[18,16,1536]{2,1,0:T(8,128)(2,1)}, u32[]{:S(2)}, u32[]{:S(2)}) collective-permute-start(bf16[18,16,1536]{2,1,0:T(8,128)(2,1)} %get-tuple-element.13.bottom_ref), channel_id=1, source_target_pairs={{0,1},{1,2},{2,3},{4,5},{5,6},{6,7},{8,9},{9,10},{10,11},{12,13},{... | collective-permute-start | bytes 2654216 | tf_op jit(solution)/shard_map/ppermute | solution.py:440
  10.0 16.5 %collective-permute-start.1 = (bf16[18,16,1536]{2,1,0:T(8,128)(2,1)}, bf16[18,16,1536]{2,1,0:T(8,128)(2,1)}, u32[]{:S(2)}, u32[]{:S(2)}) collective-permute-start(bf16[18,16,1536]{2,1,0:T(8,128)(2,1)} %get-tuple-element.12.top_ref), channel_id=1, source_target_pairs={{1,0},{2,1},{3,2},{5,4},{6,5},{7,6},{9,8},{10,9},{11,10},{13,12},{... | collective-permute-start | bytes 2654216 | tf_op jit(solution)/shard_map/ppermute | solution.py:441
  16.2 10.4 %copy-start.10 = (s32[8,8,640]{2,1,0:T(8,128)S(1)}, s32[8,8,640]{2,1,0:T(8,128)}, u32[]{:S(2)}) copy-start(s32[8,8,640]{2,1,0:T(8,128)} %copy-done.9) | copy-start | bytes 491524
  16.2 10.4 %copy-start.18 = (s32[8,128]{1,0:T(8,128)S(1)}, s32[8,128]{1,0:T(8,128)}, u32[]{:S(2)}) copy-start(s32[8,128]{1,0:T(8,128)} %copy-done.17) | copy-start | bytes 12292
  16.3 0.9 copy-start.5
  39.7 0.9 copy-start.2
  41.5 27.0 %all-to-all-start = ((s32[8,40,640]{2,1,0:T(8,128)}), s32[8,40,640]{2,1,0:T(8,128)}, u32[]{:S(2)}, u32[]{:S(2)}) async-start(s32[8,40,640]{2,1,0:T(8,128)} %copy-done.2), calls=%async_computation | async-start | bytes 1638400 | tf_op jit(solution)/shard_map/all_to_all | solution.py:477
  47.0 1.1 %copy-start.4 = (f32[4,32,1536]{2,1,0:T(8,128)S(1)}, f32[4,32,1536]{2,1,0:T(8,128)}, u32[]{:S(2)}) copy-start(f32[4,32,1536]{2,1,0:T(8,128)} %copy-done.3) | copy-start | bytes 2359300
  48.2 0.9 copy-start.6
  49.1 0.9 copy-start.11
  63.9 0.9 copy-start.1
  64.8 8.1 %copy-start.22 = (s32[1,8]{1,0:T(1,128)S(1)}, s32[1,8]{1,0:T(1,128)}, u32[]{:S(2)}) copy-start(s32[1,8]{1,0:T(1,128)} %counts_ref.1) | copy-start | bytes 100
  68.5 24.0 %all-to-all-start.1 = ((s32[8,40,640]{2,1,0:T(8,128)}), s32[8,40,640]{2,1,0:T(8,128)S(1)}, u32[]{:S(2)}, u32[]{:S(2)}) async-start(s32[8,40,640]{2,1,0:T(8,128)} %copy-done.1), calls=%async_computation.1 | async-start | bytes 1638400 | tf_op jit(solution)/shard_map/all_to_all | solution.py:477
  78.1 14.5 %copy-start.7 = (f32[2,18,8,128]{3,2,1,0:T(8,128)S(1)}, f32[2,18,8,128]{3,2,1,0:T(8,128)}, u32[]{:S(2)}) copy-start(f32[2,18,8,128]{3,2,1,0:T(8,128)} %constant.48.clone.trig_ref.refs_4_) | copy-start | bytes 442372
  78.1 14.4 %copy-start.13 = (f32[3,8,8,128]{3,2,1,0:T(8,128)S(1)}, f32[3,8,8,128]{3,2,1,0:T(8,128)}, u32[]{:S(2)}) copy-start(f32[3,8,8,128]{3,2,1,0:T(8,128)} %constant.49.clone.refs_6_) | copy-start | bytes 294916
  78.1 14.4 %copy-start.16 = (f32[2,8,128]{2,1,0:T(8,128)S(1)}, f32[2,8,128]{2,1,0:T(8,128)}, u32[]{:S(2)}) copy-start(f32[2,8,128]{2,1,0:T(8,128)} %constant.50.clone.scale_ref.refs_5_) | copy-start | bytes 24580
  (8 other events, 5.6 us)

commit v2 on v1

v2 whole, which is shorter than its diff:
```python
import functools
import math

import jax
import jax.numpy as jnp
import numpy as np
from jax import lax
from jax.experimental import pallas as pl
from jax.experimental.pallas import tpu as pltpu
from jax.sharding import PartitionSpec as P

GROWTH_RATE = 0.05
DAMPING = 1.5
TURNING_SCALE = 0.5

LANES = 128
SUBLANES = 8
UNIT = 9
WORDS = 5
STEP_COUNT = 65500.0
EXPONENT_ZERO = 99
WINDOW = 4
VMEM_BYTES = 16 * 1024 * 1024

F32 = jnp.float32
I32 = jnp.int32


def call(kernel, out_shape, cost, **options):
    flops, moved = cost
    return pl.pallas_call(
        kernel,
        out_shape=out_shape,
        cost_estimate=pl.CostEstimate(flops=flops, bytes_accessed=moved, transcendentals=0),
        compiler_params=pltpu.CompilerParams(vmem_limit_bytes=VMEM_BYTES),
        **options,
    )


def iota(shape, axis):
    return lax.broadcasted_iota(I32, shape, axis)


def upwind(speed, far_behind, behind, centre, ahead, far_ahead):
    positive = speed > 0
    near = jnp.where(positive, behind, ahead)
    after = jnp.where(positive, ahead, behind)
    far = jnp.where(positive, far_behind, far_ahead)
    return jnp.abs(speed) * (2.0 * after + far + 3.0 * (centre - 2.0 * near))


def signs(part, parts, turns, directions, j):
    sin, cos = None, None
    for h in range(parts):
        angle = 2.0 * math.pi * (h * turns + j) / directions
        if h == 0:
            sin = jnp.full(part.shape, math.sin(angle), F32)
            cos = jnp.full(part.shape, math.cos(angle), F32)
        else:
            sin = jnp.where(part == h, math.sin(angle), sin)
            cos = jnp.where(part == h, math.cos(angle), cos)
    return sin, cos


def power_table(start, sign):
    lane = iota((SUBLANES, LANES), 1)
    table = jnp.full((SUBLANES, LANES), start, F32)
    for bit in range(7):
        factor = 2.0 ** (sign * 2**bit)
        table = jnp.where((lane & (1 << bit)) != 0, table * factor, table)
    return table


def arrange_kernel(x_ref, land_ref, top_ref, bottom_ref, scratch):
    freqs, parts, step, rows, lon = x_ref.shape
    chunks = scratch.shape[1]
    tail = lon - (chunks - 1) * LANES
    filler = jnp.zeros((rows, LANES - tail), F32)
    lane = iota((SUBLANES * rows, LANES), 1)
    for j in range(step):
        for f in range(freqs):
            for h in range(parts):
                place = pl.ds(f * parts + h, rows, stride=SUBLANES)
                for k in range(chunks):
                    if k < chunks - 1:
                        piece = x_ref[f, h, j, :, k * LANES : (k + 1) * LANES].astype(F32)
                    else:
                        piece = x_ref[f, h, j, :, k * LANES : lon].astype(F32)
                        piece = jnp.concatenate([piece, filler], axis=1)
                    scratch[j, k, place, :] = piece
    initial = [None] * step
    for k in range(chunks):
        span = slice(k * LANES, (k + 1) * LANES)
        land = land_ref[:, k * LANES : min((k + 1) * LANES, lon)]
        if k == chunks - 1:
            land = jnp.concatenate([land, jnp.ones((rows, LANES - tail), I32)], axis=1)
        sea = (land == 0).astype(F32)
        sea = jnp.concatenate([jnp.broadcast_to(sea[r : r + 1], (SUBLANES, LANES)) for r in range(rows)], axis=0)
        for j in range(step):
            piece = scratch[j, k] * sea
            if k == 0:
                initial[j] = piece
            if k == chunks - 1:
                wrapped = jnp.where(
                    lane < tail + 2,
                    pltpu.roll(initial[j], tail, axis=1),
                    pltpu.roll(piece, LANES - tail, axis=1),
                )
                piece = jnp.where(lane < tail, piece, wrapped)
            piece = piece.astype(jnp.bfloat16)
            top_ref[j, :, span] = piece[: 2 * SUBLANES]
            bottom_ref[j, :, span] = piece[2 * SUBLANES :]


def index_kernel(land_ref, counts_ref, cells_ref, ranges_ref, flat):
    chunks = flat.shape[0]
    rows, lon = land_ref.shape
    per_row = chunks // rows
    tail = lon - (per_row - 1) * LANES
    flat[...] = jnp.ones(flat.shape, I32)
    for r in range(rows):
        for k in range(per_row):
            size = LANES if k < per_row - 1 else tail
            piece = land_ref[r : r + 1, k * LANES : k * LANES + size]
            flat[r * per_row + k : r * per_row + k + 1, :size] = piece
    groups, _, slots = cells_ref.shape
    spans = slots // LANES
    sea = (flat[...] == 0).astype(jnp.bfloat16)
    square = (LANES, LANES)
    ones_before = (iota(square, 1) <= iota(square, 0)).astype(jnp.bfloat16)
    ranks = lax.dot_general(ones_before, sea, (((1,), (1,)), ((), ())), preferred_element_type=F32)
    totals = jnp.dot(sea, jnp.ones(square, jnp.bfloat16), preferred_element_type=F32)
    chunk_square = (chunks, chunks)
    chunks_before = (iota(chunk_square, 1) <= iota(chunk_square, 0)).astype(jnp.bfloat16)
    through = jnp.dot(chunks_before, totals.astype(jnp.bfloat16), preferred_element_type=F32)
    through_column = through[:, :1]
    total_column = totals[:, :1]
    ranks = ranks.astype(jnp.bfloat16)
    chunk_ids = iota((chunks, slots), 0)
    slot_ids = iota((1, slots), 1)
    span_lane = iota((1, LANES), 1)
    start = jnp.int32(0)
    longest = jnp.zeros((1, 1), F32)
    for c in range(groups):
        count = counts_ref[0, c]
        number = (slot_ids + start).astype(F32)
        passed = (through_column <= number).astype(F32)
        chunk_of = jnp.sum(passed, axis=0, keepdims=True)
        before = jnp.sum(passed * total_column, axis=0, keepdims=True)
        chunk_of = chunk_of.astype(I32)
        chosen = (chunk_ids == chunk_of).astype(jnp.bfloat16)
        inside = jnp.dot(ranks, chosen, preferred_element_type=F32)
        lane = jnp.sum((inside <= number - before).astype(F32), axis=0, keepdims=True)
        valid = slot_ids < count
        found = jnp.where(valid, chunk_of * LANES + lane.astype(I32), -1)
        cells_ref[c] = jnp.broadcast_to(found, (SUBLANES, slots))
        bounds = jnp.zeros((1, LANES), I32)
        for m in range(spans):
            span = slice(m * LANES, (m + 1) * LANES)
            own = chunk_of[:, span].astype(F32)
            low = jnp.min(jnp.where(valid[:, span], own, float(chunks)), axis=1, keepdims=True)
            high = jnp.max(jnp.where(valid[:, span], own, -1.0), axis=1, keepdims=True)
            longest = jnp.maximum(longest, high - low + 1.0)
            bounds = jnp.where(span_lane == m, low.astype(I32), bounds)
            bounds = jnp.where(span_lane == m + spans, high.astype(I32), bounds)
        ranges_ref[c : c + 1, :] = bounds
        start = start + count
    ranges_ref[groups : groups + 1, :] = jnp.broadcast_to(longest.astype(I32), (1, LANES))


def advect_kernel(
    directions, stretch, top_ref, bottom_ref, speed_ref, depth_ref, current_ref, slope_ref, out_ref, coef_ref, scratch
):
    turns, _, padded = top_ref.shape
    rows, lon = depth_ref.shape
    chunks = padded // LANES
    tail = lon - (chunks - 1) * LANES
    total_freqs, depths = speed_ref.shape
    parts = directions // turns
    freqs = SUBLANES // parts
    comp, band = lax.axis_index("comp"), lax.axis_index("band")
    speeds = speed_ref[...]
    freq_ids = iota(speeds.shape, 0)
    table = []
    for f in range(freqs):
        row = jnp.sum(jnp.where(freq_ids == comp * freqs + f, speeds, 0.0), axis=0, keepdims=True)
        table.append(jnp.broadcast_to(row, (parts, depths)))
    table = jnp.concatenate(table, axis=0)
    table = jnp.concatenate([table, jnp.zeros((SUBLANES, LANES - depths), F32)], axis=1) * (1.0 / 6.0)
    shape = (SUBLANES, LANES)
    for r in range(rows):
        place = slice(r * SUBLANES, (r + 1) * SUBLANES)
        widening = jnp.float32(0.0)
        for b in range(len(stretch) // rows):
            widening = jnp.where(band == b, jnp.float32(stretch[b * rows + r]), widening)
        for k in range(chunks):
            span = slice(k * LANES, (k + 1) * LANES)

            def field(row):
                if k == chunks - 1:
                    row = jnp.concatenate([row[:, :tail], jnp.zeros((1, LANES - tail), row.dtype)], axis=1)
                return jnp.broadcast_to(row, shape)

            own = slice(k * LANES, min((k + 1) * LANES, lon))
            classes = field(depth_ref[r : r + 1, own])
            sixth = jnp.take_along_axis(table, classes, axis=1, mode="promise_in_bounds")
            coef_ref[0, place, span] = sixth
            coef_ref[1, place, span] = field(current_ref[1, r : r + 1, own]) * (1.0 / 6.0)
            coef_ref[2, place, span] = sixth * TURNING_SCALE * field(slope_ref[0, r : r + 1, own])
            coef_ref[3, place, span] = sixth * TURNING_SCALE * field(slope_ref[1, r : r + 1, own])
            scratch[0, place, span] = sixth * widening
            scratch[1, place, span] = field(current_ref[0, r : r + 1, own]) * (1.0 / 6.0)

    width = LANES * (4 if chunks % 4 == 0 else 1)

    def window(ref, j, low, high):
        parts = []
        if low < LANES:
            parts.append(ref[j, :, padded - LANES :])
            parts.append(ref[j, :, : min(high + LANES, padded)])
        else:
            parts.append(ref[j, :, low - LANES : min(high + LANES, padded)])
        if high + LANES > padded:
            parts.append(ref[j, :, :LANES])
        return jnp.concatenate([part.astype(F32) for part in parts], axis=1)

    turn_sin, turn_cos = math.sin(2.0 * math.pi / directions), math.cos(2.0 * math.pi / directions)

    def one_turn(j, carry):
        sin, cos = carry
        for low in range(0, padded, width):
            high = low + width
            centres, shifted = [], []
            for ref in (top_ref, bottom_ref):
                wide = window(ref, j, low, high)
                moved = [
                    pltpu.roll(wide, shift % wide.shape[1], axis=1)[:, LANES : LANES + width] for shift in (2, 1, -1, -2)
                ]
                for half in (slice(0, SUBLANES), slice(SUBLANES, 2 * SUBLANES)):
                    centres.append(wide[half, LANES : LANES + width])
                    shifted.append([one[half] for one in moved])
            for r in range(rows):
                place = slice(r * SUBLANES, (r + 1) * SUBLANES)
                span = slice(low, high)
                speed_x = scratch[0, place, span] * cos + scratch[1, place, span]
                speed_y = coef_ref[0, place, span] * sin + coef_ref[1, place, span]
                near = [centres[n] if 0 <= n < rows else 0.0 for n in range(r - 2, r + 3)]
                far_behind, behind, ahead, far_ahead = shifted[r]
                along = upwind(speed_x, far_behind, behind, centres[r], ahead, far_ahead)
                across = upwind(speed_y, *near)
                out_ref[j, place, span] = centres[r] - along - across
        return sin * turn_cos + cos * turn_sin, cos * turn_cos - sin * turn_sin

    part = iota((SUBLANES, 1), 0) % parts
    lax.fori_loop(0, turns, one_turn, signs(part, parts, turns, directions, 0))


def pack_kernel(
    directions, adv_ref, above_ref, below_ref, coef_ref, cells_ref, ranges_ref, out_ref, packed, turned_values
):
    turns, height, padded = adv_ref.shape
    rows = height // SUBLANES
    chunks = padded // LANES
    parts = directions // turns
    units = turns // UNIT
    shape = (SUBLANES, LANES)
    part = iota(shape, 0) % parts
    scale = power_table(STEP_COUNT * 2.0**EXPONENT_ZERO, -1)
    together = turned_values.shape[0]

    def turned(value, by):
        if by == 0:
            return value
        if by > 0:
            return jnp.where(
                part == parts - 1, pltpu.roll(value, parts - 1, axis=0), pltpu.roll(value, SUBLANES - 1, axis=0)
            )
        return jnp.where(part == 0, pltpu.roll(value, SUBLANES - parts + 1, axis=0), pltpu.roll(value, 1, axis=0))

    def refract(r, k, into):
        place = slice(r * SUBLANES, (r + 1) * SUBLANES)
        span = pl.ds(pl.multiple_of(k * LANES, LANES), LANES)
        sixth, current_y, turn_x, turn_y = [coef_ref[n, place, span] for n in range(4)]
        advected = []
        for j in range(turns):
            sin, _ = signs(part, parts, turns, directions, j)
            speed = sixth * sin + current_y
            positive = speed > 0
            ref = above_ref if r < 2 else below_ref
            outer = ref[j, :, span].astype(F32)
            low, high = outer[:SUBLANES], outer[SUBLANES:]
            if r == 0:
                share = jnp.where(positive, low - 6.0 * high, 2.0 * high)
            elif r == 1:
                share = jnp.where(positive, high, 0.0)
            elif r == rows - 2:
                share = jnp.where(positive, 0.0, low)
            else:
                share = jnp.where(positive, 2.0 * low, high - 6.0 * low)
            advected.append(adv_ref[j, place, span] - jnp.abs(speed) * share)
        around = {j: turned(advected[j % turns], j // turns) for j in range(-2, turns + 2)}
        largest = [None] * units
        for j in range(turns):
            sin, cos = signs(part, parts, turns, directions, j)
            speed = sin * turn_x - cos * turn_y
            value = around[j] - upwind(speed, *[around[n] for n in range(j - 2, j + 3)])
            turned_values[into, j] = value
            size = jnp.abs(value)
            unit = j // UNIT
            largest[unit] = size if largest[unit] is None else jnp.maximum(largest[unit], size)
        return largest

    def code(chunk, come_from, unit, largest):
        level = jnp.ceil(jnp.log2(jnp.maximum(largest, 2.0**-98)))
        level = jnp.minimum(level, 28.0).astype(I32) + EXPONENT_ZERO
        level = jnp.maximum(level, 1)
        inverse = jnp.take_along_axis(scale, level, axis=1, mode="promise_in_bounds")
        codes = [
            (turned_values[come_from, unit * UNIT + n] * inverse + 65536.5).astype(I32) for n in range(UNIT)
        ]
        first = unit * WORDS
        rest = codes[8] | (level << 17)
        for n in range(4):
            even, odd = codes[2 * n], codes[2 * n + 1]
            packed[chunk, first + n] = even | (odd << 17)
            rest = rest | ((odd >> 15) << (24 + 2 * n))
        packed[chunk, first + 4] = rest

    for r in range(rows):

        def some_chunks(i, carry):
            found = [refract(r, i * together + n, n) for n in range(together)]
            for n in range(together):
                for unit in range(units):
                    code(r * chunks + i * together + n, n, unit, found[n][unit])
            return carry

        lax.fori_loop(0, chunks // together, some_chunks, 0)

    groups, words, slots = out_ref.shape
    words = words // SUBLANES
    spans = slots // LANES
    last = rows * chunks - 1

    def merged(cells, chunk, sums):
        lane = cells - chunk * LANES
        here = (lane >= 0) & (lane < LANES)
        lane = lane & (LANES - 1)
        return tuple(
            jnp.where(
                here, jnp.take_along_axis(packed[chunk, n], lane, axis=1, mode="promise_in_bounds"), sums[n]
            )
            for n in range(words)
        )

    def one_block(c, carry):
        for m in range(spans):
            span = slice(m * LANES, (m + 1) * LANES)
            cells = cells_ref[c, :, span]
            low = ranges_ref[c, m]
            sums = tuple(jnp.zeros(shape, I32) for _ in range(words))
            for t in range(WINDOW):
                sums = merged(cells, jnp.minimum(low + t, last), sums)
            for n in range(words):
                out_ref[c, n * SUBLANES : (n + 1) * SUBLANES, span] = sums[n]
        return carry

    lax.fori_loop(0, groups, one_block, 0)

    @pl.when(ranges_ref[groups, 0] > WINDOW)
    def _():
        def longer_block(c, carry):
            for m in range(spans):
                span = slice(m * LANES, (m + 1) * LANES)
                cells = cells_ref[c, :, span]
                low, high = ranges_ref[c, m], ranges_ref[c, m + spans]
                sums = tuple(out_ref[c, n * SUBLANES : (n + 1) * SUBLANES, span] for n in range(words))
                sums = lax.fori_loop(
                    low + WINDOW, high + 1, lambda chunk, sums: merged(cells, chunk, sums), sums
                )
                for n in range(words):
                    out_ref[c, n * SUBLANES : (n + 1) * SUBLANES, span] = sums[n]
            return carry

        lax.fori_loop(0, groups, longer_block, 0)


def grow_kernel(directions, wind_ref, cells_ref, ranges_ref, out_ref, flat, slot_wind):
    groups, turns, _, slots = out_ref.shape
    rows, lon = wind_ref.shape[1:]
    chunks = flat.shape[0] // rows
    tail = lon - (chunks - 1) * LANES
    spans = slots // LANES
    parts = directions // turns
    freqs = SUBLANES // parts
    shape = (SUBLANES, LANES)
    part = iota(shape, 0) % parts
    freq = iota(shape, 0) // parts
    comp = lax.axis_index("comp")
    for r in range(rows):
        for k in range(chunks):
            size = LANES if k < chunks - 1 else tail
            for n in range(2):
                flat[r * chunks + k, n : n + 1, :size] = wind_ref[n, r : r + 1, k * LANES : k * LANES + size]
    for m in range(spans):
        span = slice(m * LANES, (m + 1) * LANES)
        cells = cells_ref[comp, :, span]

        def merged(chunk, sums):
            lane = cells - chunk * LANES
            here = (lane >= 0) & (lane < LANES)
            lane = lane & (LANES - 1)
            return jnp.where(
                here, jnp.take_along_axis(flat[chunk], lane, axis=1, mode="promise_in_bounds"), sums
            )

        found = lax.fori_loop(
            ranges_ref[comp, m], ranges_ref[comp, m + spans] + 1, merged, jnp.zeros(shape, F32)
        )
        slot_wind[0, :, span] = jnp.broadcast_to(found[0:1], shape)
        slot_wind[1, :, span] = jnp.broadcast_to(found[1:2], shape)

    rates = []
    for source in range(groups):
        slope, threshold = jnp.zeros(shape, F32), jnp.zeros(shape, F32)
        for f in range(freqs):
            angular, ratio = frequency(source * freqs + f, groups * freqs)
            slope = jnp.where(freq == f, GROWTH_RATE * ratio * angular / 9.81, slope)
            threshold = jnp.where(freq == f, GROWTH_RATE * ratio, threshold)
        rates.append((slope, threshold))

    def one_span(m, carry):
        span = pl.ds(pl.multiple_of(m * LANES, LANES), LANES)
        east, north = slot_wind[0, :, span], slot_wind[1, :, span]
        for j in range(turns):
            sin, cos = signs(part, parts, turns, directions, j)
            along = east * cos + north * sin
            for source in range(groups):
                slope, threshold = rates[source]
                out_ref[source, j, :, span] = jnp.exp(jnp.maximum(along * slope - threshold, 0.0))
        return carry

    lax.fori_loop(0, spans, one_span, 0)


def finish_kernel(freqs, arrived, counts_ref, grown_ref, out_ref, values, ordered):
    groups = arrived.shape[0]
    turns = values.shape[1]
    units = turns // UNIT
    directions_per = turns * SUBLANES
    shape = (SUBLANES, LANES)
    scale = power_table(2.0**-EXPONENT_ZERO / STEP_COUNT, 1)
    comp = lax.axis_index("comp")
    sums = [jnp.zeros(shape, F32) for _ in range(2)]
    for source in range(groups):
        for unit in range(units):
            words = [
                arrived[source, n * SUBLANES : (n + 1) * SUBLANES, :]
                for n in range(unit * WORDS, (unit + 1) * WORDS)
            ]
            rest = words[4]
            level = lax.shift_right_logical(rest, 17) & 127
            size = jnp.take_along_axis(scale, level, axis=1, mode="promise_in_bounds")
            offset = size * 65536.0
            for n in range(UNIT):
                if n == 8:
                    coded = rest & 0x1FFFF
                elif n % 2 == 0:
                    coded = words[n // 2] & 0x1FFFF
                else:
                    coded = lax.shift_right_logical(words[n // 2], 17) | (
                        lax.shift_right_logical(rest, 9 + n - 1) & 0x18000
                    )
                value = coded.astype(F32) * size - offset
                j = unit * UNIT + n
                sums[n % 2] = sums[n % 2] + value * value
                values[source, j] = value * grown_ref[source, j]
    mean_sq = jnp.sum(sums[0] + sums[1], axis=0, keepdims=True) / float(groups * directions_per)
    strength = jnp.sqrt(mean_sq + 1e-06)
    strength = jnp.broadcast_to(strength, shape)
    occupied = (pl.program_id(0) * LANES + iota(shape, 1)) < counts_ref[0, comp]
    freq = iota(shape, 0) // (SUBLANES // freqs)
    for source in range(groups):
        rate = jnp.zeros(shape, F32)
        for f in range(freqs):
            rate = jnp.where(freq == f, DAMPING * frequency(source * freqs + f, groups * freqs)[1], rate)
        factor = jnp.exp(-(rate * strength))
        for j in range(turns):
            value = jnp.where(occupied, values[source, j] * factor, 0.0)
            ordered[pl.ds(source * directions_per + j, SUBLANES, stride=turns), :] = value
    square = (LANES, LANES)
    unit_matrix = (iota(square, 0) == iota(square, 1)).astype(jnp.bfloat16)
    turned = lax.dot_general(
        unit_matrix,
        ordered[...].astype(jnp.bfloat16),
        (((1,), (1,)), ((), ())),
        preferred_element_type=F32,
    )
    out_ref[...] = turned.astype(jnp.bfloat16)


def frequency(index, count):
    angular = 2.0 * math.pi * 0.0418 * 1.1**index
    return angular, 1.1 ** (index - (count - 1))


def body(spectra, depth_class, group_speed, current, depth_slope, wind, land_mask, block_counts):
    freqs, directions, rows, lon = spectra.shape
    total_freqs = group_speed.shape[1]
    groups = lax.axis_size("comp")
    bands = lax.axis_size("band")
    slot_count = rows * lon * 7 // (8 * groups)
    slots = -(-slot_count // LANES) * LANES
    parts = SUBLANES // freqs
    turns = directions // parts
    units = turns // UNIT
    chunks = -(-lon // LANES)
    padded = chunks * LANES
    height = rows * SUBLANES
    words = units * WORDS
    hbm = 2 * turns * height * padded
    latitude = (-60.0 + 120.0 * (np.arange(rows * bands) + 0.5) / (rows * bands)) * (math.pi / 180.0)
    stretch = [float(value) for value in 1.0 / np.cos(latitude)]
    smem = pl.BlockSpec(memory_space=pltpu.SMEM)
    vmem = pl.BlockSpec(memory_space=pltpu.VMEM)

    step = 3
    half = jax.ShapeDtypeStruct((turns, height // 2, padded), jnp.bfloat16)
    half_spec = pl.BlockSpec((step, height // 2, padded), lambda i: (i, 0, 0))
    top, bottom = call(
        arrange_kernel,
        [half, half],
        (4 * hbm, 2 * hbm),
        grid=(turns // step,),
        in_specs=[
            pl.BlockSpec((freqs, parts, step, rows, lon), lambda i: (0, 0, i, 0, 0)),
            pl.BlockSpec((rows, lon), lambda i: (0, 0)),
        ],
        out_specs=[half_spec, half_spec],
        scratch_shapes=[pltpu.VMEM((step, chunks, height, LANES), F32)],
    )(spectra.reshape(freqs, parts, turns, rows, lon), land_mask)
    down = [(i, i + 1) for i in range(bands - 1)]
    above = lax.ppermute(bottom, "band", down)
    below = lax.ppermute(top, "band", [(j, i) for i, j in down])

    range_rows = 2 * SUBLANES if groups < 2 * SUBLANES else 3 * SUBLANES
    cells, ranges = call(
        index_kernel,
        [
            jax.ShapeDtypeStruct((groups, SUBLANES, slots), I32),
            jax.ShapeDtypeStruct((range_rows, LANES), I32),
        ],
        (100 * groups * slots, 8 * groups * slots),
        in_specs=[vmem, smem],
        out_specs=[vmem, vmem],
        scratch_shapes=[pltpu.VMEM((rows * chunks, LANES), I32)],
    )(land_mask, block_counts)

    advected, coefs = call(
        functools.partial(advect_kernel, directions, stretch),
        [
            jax.ShapeDtypeStruct((turns, height, padded), F32),
            jax.ShapeDtypeStruct((4, height, padded), F32),
        ],
        (50 * hbm, 4 * hbm),
        in_specs=[vmem] * 6,
        out_specs=[vmem, vmem],
        scratch_shapes=[pltpu.VMEM((2, height, padded), F32)],
    )(top, bottom, group_speed.T, depth_class, current, depth_slope)

    sent = call(
        functools.partial(pack_kernel, directions),
        jax.ShapeDtypeStruct((groups, words * SUBLANES, slots), I32),
        (50 * hbm, 4 * hbm),
        in_specs=[vmem] * 5 + [smem],
        out_specs=vmem,
        scratch_shapes=[
            pltpu.VMEM((rows * chunks, words, SUBLANES, LANES), I32),
            pltpu.VMEM((4 if chunks % 4 == 0 else 1, turns, SUBLANES, LANES), F32),
        ],
    )(advected, above, below, coefs, cells, ranges)
    arrived = lax.all_to_all(sent, "comp", split_axis=0, concat_axis=0, tiled=True)

    total = total_freqs * directions
    grown = call(
        functools.partial(grow_kernel, directions),
        jax.ShapeDtypeStruct((groups, turns, SUBLANES, slots), F32),
        (20 * total * slots, 4 * total * slots),
        in_specs=[vmem, vmem, smem],
        out_specs=vmem,
        scratch_shapes=[
            pltpu.VMEM((rows * chunks, SUBLANES, LANES), F32),
            pltpu.VMEM((2, SUBLANES, slots), F32),
        ],
    )(wind, cells, ranges)

    result = call(
        functools.partial(finish_kernel, freqs),
        jax.ShapeDtypeStruct((slot_count, total), jnp.bfloat16),
        (50 * total * slots, 6 * total * slots),
        grid=(slots // LANES,),
        in_specs=[
            pl.BlockSpec((groups, words * SUBLANES, LANES), lambda i: (0, 0, i)),
            smem,
            pl.BlockSpec((groups, turns, SUBLANES, LANES), lambda i: (0, 0, 0, i)),
        ],
        out_specs=pl.BlockSpec((LANES, total), lambda i: (i, 0)),
        scratch_shapes=[
            pltpu.VMEM((groups, turns, SUBLANES, LANES), F32),
            pltpu.VMEM((total, LANES), F32),
        ],
    )(arrived, block_counts, grown)
    return result.T


def solution(mesh):
    return jax.shard_map(
        body,
        mesh=mesh,
        in_specs=(
            P("comp", None, "band", None),
            P("band", None),
            P(),
            P(None, "band", None),
            P(None, "band", None),
            P(None, "band", None),
            P("band", None),
            P("band", None),
        ),
        out_specs=P(None, ("comp", "band")),
        check_vma=False,
    )
```

time: 104 us -> 76.4 us (0.73); the launches traced: 101 us -> 75.9 us
  waiting for transfers between devices: 14.2 us -> 35.9 us
  Pallas kernels: 46.6 us -> 25.5 us
  local copies, waits for them, and re-layouts: 23.2 us -> 2.25 us
  starting transfers between devices: 15.5 us -> 12.1 us
  other arithmetic: 1.62 us -> 0 us
    pallas_call x4, Pallas kernels: 41.8 us -> 22.4 us  [the longest x1 9.16 us: body(): call(functools.partial(pack_kernel, directions), jax.ShapeDtypeStruct((gr...]
    all_to_all x2 -> x1, waiting for transfers between devices: 14.2 us -> 30.7 us  [body(): lax.all_to_all(sent, 'comp', split_axis=0, concat_axis=0, tiled=True)]
    unnamed x56 -> x16, local copies, waits for them, and re-layouts: 12.8 us -> 2.25 us
    gather x2 -> x0, local copies, waits for them, and re-layouts: 7.72 us -> none  [body(): winds = jnp.stack([jnp.take(winds[0], own), jnp.take(winds[1], own)])]
    ppermute x1, waiting for transfers between devices: 0.01 us -> 4.4 us  [body(): below = lax.ppermute(top, 'band', [(j, i) for i, j in down])]
    all_to_all x2 -> x1, starting transfers between devices: 9.1 us -> 5.69 us  [body(): lax.all_to_all(sent, 'comp', split_axis=0, concat_axis=0, tiled=True)]
    pallas_call x1, Pallas kernels: 3.16 us -> 1.51 us  [body(): call(arrange_kernel, [half, half], (4 * hbm, 2 * hbm), grid=(turns // ste...]
    pad x3 -> x0, local copies, waits for them, and re-layouts: 1.2 us -> none  [the longest x1 0.61 us: body(): depth = jnp.pad(depth_class, spare)]
  transfers between devices with their start and end apart: 4 -> 3, of which waited for: 2 -> 3; matrix products, arithmetic and copies ran while one was open for 11% -> 0% of each run, Pallas kernels for 22% -> 12%
where the time goes in v2:
time: 76.4 us; the launch traced here: 75.9 us
  waiting for transfers between devices  35.9 us (47%)
  Pallas kernels  25.5 us (33%)
  starting transfers between devices  12.1 us (16%)
  local copies, waits for them, and re-layouts  2.25 us (3%)
    all_to_all x1, waiting for transfers between devices, body(): lax.all_to_all(sent, 'comp', split_axis=0, concat_axis=0, tiled=True)  30.7 us
    pallas_call x1, Pallas kernels, body(): call(functools.partial(pack_kernel, directions), jax.ShapeDtypeStruct((gr...  9.16 us
    all_to_all x1, starting transfers between devices, body(): lax.all_to_all(sent, 'comp', split_axis=0, concat_axis=0, tiled=True)  5.69 us
    pallas_call x1, Pallas kernels, body(): call(functools.partial(advect_kernel, directions, stretch), [jax.ShapeDty...  5.47 us
    pallas_call x1, Pallas kernels, body(): call(functools.partial(finish_kernel, freqs), jax.ShapeDtypeStruct((slot_...  5.46 us
    ppermute x1, starting transfers between devices, body(): above = lax.ppermute(bottom, 'band', down)  4.51 us
    ppermute x1, waiting for transfers between devices, body(): below = lax.ppermute(top, 'band', [(j, i) for i, j in down])  4.4 us
    pallas_call x1, Pallas kernels, body(): call(functools.partial(grow_kernel, directions), jax.ShapeDtypeStruct((gr...  2.29 us
  transfers between devices with their start and end apart: 3, of which 3 were waited for; matrix products, arithmetic and copies ran while one was open for 0% of the time, Pallas kernels for 12%

profile of v2, /device:TPU:1, one launch (start us, length us, event | category | flops | bytes accessed | tf_op | source)
XLA Modules:
  0.0 75.9 jit_solution(10424179459455726268)
XLA Ops:
  0.0 0.0 copy-start.7
  0.0 0.0 copy-start
  0.0 1.5 %copy-done = bf16[4,36,4,1440]{3,2,1,0:T(4,128)(2,1)S(1)} copy-done((bf16[4,36,4,1440]{3,2,1,0:T(4,128)(2,1)S(1)}, bf16[4,36,4,1440]{3,2,1,0:T(4,128)(2,1)}, u32[]{:S(2)}) %copy-start) | copy-done | bytes 1658904
  1.5 0.0 copy-start.1
  1.5 0.7 copy-done.1
  2.2 0.0 copy-start.3
  2.2 1.5 %shard_map.82 = (bf16[18,16,1536]{2,1,0:T(8,128)(2,1)S(1)}, bf16[18,16,1536]{2,1,0:T(8,128)(2,1)S(1)}) custom-call(bf16[4,2,18,4,1440]{4,3,2,1,0:T(4,128)(2,1)S(1)} %bitcast.3, s32[4,1440]{1,0:T(4,128)S(1)} %copy-done.1), custom_call_target="tpu_custom_call" | custom-call | flops 7077888 | bytes 3538944 | tf_op jit(solution)/shard_map/pallas_call | solution.py:530
  3.8 4.5 %collective-permute-start = (bf16[18,16,1536]{2,1,0:T(8,128)(2,1)S(1)}, bf16[18,16,1536]{2,1,0:T(8,128)(2,1)S(1)}, u32[]{:S(2)}, u32[]{:S(2)}) collective-permute-start(bf16[18,16,1536]{2,1,0:T(8,128)(2,1)S(1)} %get-tuple-element.12.bottom_ref), channel_id=1, source_target_pairs={{0,1},{1,2},{2,3},{4,5},{5,6},{6,7},{8,9},{9,10},{10,11},{12,13},{... | collective-permute-start | bytes 2654216 | tf_op jit(solution)/shard_map/ppermute | solution.py:543
  8.3 1.9 %collective-permute-start.1 = (bf16[18,16,1536]{2,1,0:T(8,128)(2,1)S(1)}, bf16[18,16,1536]{2,1,0:T(8,128)(2,1)S(1)}, u32[]{:S(2)}, u32[]{:S(2)}) collective-permute-start(bf16[18,16,1536]{2,1,0:T(8,128)(2,1)S(1)} %get-tuple-element.11.top_ref), channel_id=1, source_target_pairs={{1,0},{2,1},{3,2},{5,4},{6,5},{7,6},{9,8},{10,9},{11,10},{13,12},{... | collective-permute-start | bytes 2654216 | tf_op jit(solution)/shard_map/ppermute | solution.py:544
  10.2 0.0 copy-done.7
  10.2 1.6 %shard_map.84 = (s32[8,8,640]{2,1,0:T(8,128)S(1)}, s32[16,128]{1,0:T(8,128)S(1)}) custom-call(s32[4,1440]{1,0:T(4,128)S(1)} %copy-done.1, s32[1,8]{1,0:T(1,128)S(1)} %copy-done.7), custom_call_target="tpu_custom_call" | custom-call | flops 512000 | bytes 40960 | tf_op jit(solution)/shard_map/pallas_call | solution.py:547
  11.9 0.0 copy-done.3
  11.9 0.0 copy-done.4
  11.9 0.0 copy-done.5
  11.9 0.0 copy-done.6
  11.9 5.5 %shard_map.83 = (f32[18,32,1536]{2,1,0:T(8,128)S(1)}, f32[4,32,1536]{2,1,0:T(8,128)S(1)}) custom-call(bf16[18,16,1536]{2,1,0:T(8,128)(2,1)S(1)} %get-tuple-element.11.top_ref, bf16[18,16,1536]{2,1,0:T(8,128)(2,1)S(1)} %get-tuple-element.12.bottom_ref, f32[32,64]{1,0:T(8,128)S(1)} %bitcast.4, s32[4,1440]{1,0:T(4,128)S(1)} %copy-done.5, ...), custom_call_target="tpu_custom_call" | custom-call | flops 88473600 | bytes 7077888 | tf_op jit(solution)/shard_map/pallas_call | solution.py:559
  17.4 0.9 %collective-permute-done.above_ref = bf16[18,16,1536]{2,1,0:T(8,128)(2,1)S(1)} collective-permute-done((bf16[18,16,1536]{2,1,0:T(8,128)(2,1)S(1)}, bf16[18,16,1536]{2,1,0:T(8,128)(2,1)S(1)}, u32[]{:S(2)}, u32[]{:S(2)}) %collective-permute-start) | collective-permute-done | bytes 884768 | tf_op jit(solution)/shard_map/ppermute | solution.py:543
  18.2 4.4 %collective-permute-done.1.below_ref = bf16[18,16,1536]{2,1,0:T(8,128)(2,1)S(1)} collective-permute-done((bf16[18,16,1536]{2,1,0:T(8,128)(2,1)S(1)}, bf16[18,16,1536]{2,1,0:T(8,128)(2,1)S(1)}, u32[]{:S(2)}, u32[]{:S(2)}) %collective-permute-start.1) | collective-permute-done | bytes 884768 | tf_op jit(solution)/shard_map/ppermute | solution.py:544
  22.6 9.2 %shard_map.85 = s32[8,80,640]{2,1,0:T(8,128)} custom-call(f32[18,32,1536]{2,1,0:T(8,128)S(1)} %get-tuple-element.13.adv_ref, bf16[18,16,1536]{2,1,0:T(8,128)(2,1)S(1)} %collective-permute-done.above_ref, bf16[18,16,1536]{2,1,0:T(8,128)(2,1)S(1)} %collective-permute-done.1.below_ref, f32[4,32,1536]{2,1,0:T(8,128)S(1)} %get-tuple-element.14.coef_ref, ...), custom_call_target="tpu_custom_call" | custom-call | flops 88473600 | bytes 7077888 | tf_op jit(solution)/shard_map/pallas_call | solution.py:571
  31.8 5.7 %all-to-all-start = ((s32[8,80,640]{2,1,0:T(8,128)}), s32[8,80,640]{2,1,0:T(8,128)}, u32[]{:S(2)}, u32[]{:S(2)}) async-start(s32[8,80,640]{2,1,0:T(8,128)} %shard_map.85), calls=%async_computation | async-start | bytes 3276800 | tf_op jit(solution)/shard_map/all_to_all | solution.py:582
  37.5 0.0 copy-done.2
  37.5 2.3 %shard_map.86.grown_ref = f32[8,18,8,640]{3,2,1,0:T(8,128)S(1)} custom-call(f32[2,4,1440]{2,1,0:T(4,128)S(1)} %copy-done.2, s32[8,8,640]{2,1,0:T(8,128)S(1)} %get-tuple-element.15.cells_ref, s32[16,128]{1,0:T(8,128)S(1)} %get-tuple-element.16.ranges_ref), custom_call_target="tpu_custom_call" | custom-call | flops 14745600 | bytes 2949120 | tf_op jit(solution)/shard_map/pallas_call | solution.py:585
  39.8 30.7 %all-to-all-done.arrived = s32[8,80,640]{2,1,0:T(8,128)} async-done(((s32[8,80,640]{2,1,0:T(8,128)}), s32[8,80,640]{2,1,0:T(8,128)}, u32[]{:S(2)}, u32[]{:S(2)}) %all-to-all-start) | async-done | bytes 1638432 | tf_op jit(solution)/shard_map/all_to_all | solution.py:582
  70.5 5.5 %shard_map.87 = bf16[630,1152]{1,0:T(8,128)(2,1)} custom-call(s32[8,80,640]{2,1,0:T(8,128)} %all-to-all-done.arrived, s32[1,8]{1,0:T(1,128)S(1)} %copy-done.7, f32[8,18,8,640]{3,2,1,0:T(8,128)S(1)} %shard_map.86.grown_ref), custom_call_target="tpu_custom_call" | custom-call | flops 36864000 | bytes 4423680 | tf_op jit(solution)/shard_map/pallas_call | solution.py:597
  (4 shorter events, 0.0 us)
Async XLA Ops:
  0.0 10.2 %copy-start.7 = (s32[1,8]{1,0:T(1,128)S(1)}, s32[1,8]{1,0:T(1,128)}, u32[]{:S(2)}) copy-start(s32[1,8]{1,0:T(1,128)} %counts_ref.3) | copy-start | bytes 100
  0.0 1.5 %copy-start = (bf16[4,36,4,1440]{3,2,1,0:T(4,128)(2,1)S(1)}, bf16[4,36,4,1440]{3,2,1,0:T(4,128)(2,1)}, u32[]{:S(2)}) copy-start(bf16[4,36,4,1440]{3,2,1,0:T(4,128)(2,1)} %param.8) | copy-start | bytes 4976644
  1.5 0.7 copy-start.1
  2.2 9.6 %copy-start.3 = (f32[2,4,1440]{2,1,0:T(4,128)S(1)}, f32[2,4,1440]{2,1,0:T(4,128)}, u32[]{:S(2)}) copy-start(f32[2,4,1440]{2,1,0:T(4,128)} %current_ref.1) | copy-start | bytes 138244
  2.2 9.6 %copy-start.4 = (f32[2,4,1440]{2,1,0:T(4,128)S(1)}, f32[2,4,1440]{2,1,0:T(4,128)}, u32[]{:S(2)}) copy-start(f32[2,4,1440]{2,1,0:T(4,128)} %slope_ref.1) | copy-start | bytes 138244
  2.2 9.7 %copy-start.5 = (s32[4,1440]{1,0:T(4,128)S(1)}, s32[4,1440]{1,0:T(4,128)}, u32[]{:S(2)}) copy-start(s32[4,1440]{1,0:T(4,128)} %depth_ref.1) | copy-start | bytes 69124
  2.2 9.7 %copy-start.6 = (f32[64,32]{0,1:T(8,128)S(1)}, f32[64,32]{0,1:T(8,128)}, u32[]{:S(2)}) copy-start(f32[64,32]{0,1:T(8,128)} %param.10) | copy-start | bytes 24580
  3.8 14.5 %collective-permute-start = (bf16[18,16,1536]{2,1,0:T(8,128)(2,1)S(1)}, bf16[18,16,1536]{2,1,0:T(8,128)(2,1)S(1)}, u32[]{:S(2)}, u32[]{:S(2)}) collective-permute-start(bf16[18,16,1536]{2,1,0:T(8,128)(2,1)S(1)} %get-tuple-element.12.bottom_ref), channel_id=1, source_target_pairs={{0,1},{1,2},{2,3},{4,5},{5,6},{6,7},{8,9},{9,10},{10,11},{12,13},{... | collective-permute-start | bytes 2654216 | tf_op jit(solution)/shard_map/ppermute | solution.py:543
  8.3 14.4 %collective-permute-start.1 = (bf16[18,16,1536]{2,1,0:T(8,128)(2,1)S(1)}, bf16[18,16,1536]{2,1,0:T(8,128)(2,1)S(1)}, u32[]{:S(2)}, u32[]{:S(2)}) collective-permute-start(bf16[18,16,1536]{2,1,0:T(8,128)(2,1)S(1)} %get-tuple-element.11.top_ref), channel_id=1, source_target_pairs={{1,0},{2,1},{3,2},{5,4},{6,5},{7,6},{9,8},{10,9},{11,10},{13,12},{... | collective-permute-start | bytes 2654216 | tf_op jit(solution)/shard_map/ppermute | solution.py:544
  31.8 5.7 %copy-start.2 = (f32[2,4,1440]{2,1,0:T(4,128)S(1)}, f32[2,4,1440]{2,1,0:T(4,128)}, u32[]{:S(2)}) copy-start(f32[2,4,1440]{2,1,0:T(4,128)} %wind_ref.1) | copy-start | bytes 138244
  31.8 38.7 %all-to-all-start = ((s32[8,80,640]{2,1,0:T(8,128)}), s32[8,80,640]{2,1,0:T(8,128)}, u32[]{:S(2)}, u32[]{:S(2)}) async-start(s32[8,80,640]{2,1,0:T(8,128)} %shard_map.85), calls=%async_computation | async-start | bytes 3276800 | tf_op jit(solution)/shard_map/all_to_all | solution.py:582

commit v3 on v2

--- a/solution.py
+++ b/solution.py
@@ -21,18 +21,19 @@
 EXPONENT_ZERO = 99
 WINDOW = 4
 VMEM_BYTES = 16 * 1024 * 1024
+WHOLE_VMEM = 62_000_000
 
 F32 = jnp.float32
 I32 = jnp.int32
 
 
-def call(kernel, out_shape, cost, **options):
+def call(kernel, out_shape, cost, vmem=VMEM_BYTES, **options):
     flops, moved = cost
     return pl.pallas_call(
         kernel,
         out_shape=out_shape,
         cost_estimate=pl.CostEstimate(flops=flops, bytes_accessed=moved, transcendentals=0),
-        compiler_params=pltpu.CompilerParams(vmem_limit_bytes=VMEM_BYTES),
+        compiler_params=pltpu.CompilerParams(vmem_limit_bytes=vmem),
         **options,
     )
 
@@ -155,14 +156,17 @@
         found = jnp.where(valid, chunk_of * LANES + lane.astype(I32), -1)
         cells_ref[c] = jnp.broadcast_to(found, (SUBLANES, slots))
         bounds = jnp.zeros((1, LANES), I32)
+        final = jnp.zeros((1, 1), F32)
         for m in range(spans):
             span = slice(m * LANES, (m + 1) * LANES)
             own = chunk_of[:, span].astype(F32)
             low = jnp.min(jnp.where(valid[:, span], own, float(chunks)), axis=1, keepdims=True)
             high = jnp.max(jnp.where(valid[:, span], own, -1.0), axis=1, keepdims=True)
             longest = jnp.maximum(longest, high - low + 1.0)
+            final = jnp.maximum(final, high)
             bounds = jnp.where(span_lane == m, low.astype(I32), bounds)
             bounds = jnp.where(span_lane == m + spans, high.astype(I32), bounds)
+        bounds = jnp.where(span_lane == 2 * spans, final.astype(I32), bounds)
         ranges_ref[c : c + 1, :] = bounds
         start = start + count
     ranges_ref[groups : groups + 1, :] = jnp.broadcast_to(longest.astype(I32), (1, LANES))
@@ -255,9 +259,8 @@
     lax.fori_loop(0, turns, one_turn, signs(part, parts, turns, directions, 0))
 
 
-def pack_kernel(
-    directions, adv_ref, above_ref, below_ref, coef_ref, cells_ref, ranges_ref, out_ref, packed, turned_values
-):
+def pack_kernel(directions, offsets, adv_ref, above_ref, below_ref, coef_ref, cells_ref, ranges_ref, after_ref, *refs):
+    out_refs, (packed, turned_values, trig) = refs[:-3], refs[-3:]
     turns, height, padded = adv_ref.shape
     rows = height // SUBLANES
     chunks = padded // LANES
@@ -267,6 +270,8 @@
     part = iota(shape, 0) % parts
     scale = power_table(STEP_COUNT * 2.0**EXPONENT_ZERO, -1)
     together = turned_values.shape[0]
+    for j in range(turns):
+        trig[0, j], trig[1, j] = signs(part, parts, turns, directions, j)
 
     def turned(value, by):
         if by == 0:
@@ -283,8 +288,7 @@
         sixth, current_y, turn_x, turn_y = [coef_ref[n, place, span] for n in range(4)]
         advected = []
         for j in range(turns):
-            sin, _ = signs(part, parts, turns, directions, j)
-            speed = sixth * sin + current_y
+            speed = sixth * trig[0, j] + current_y
             positive = speed > 0
             ref = above_ref if r < 2 else below_ref
             outer = ref[j, :, span].astype(F32)
@@ -301,8 +305,7 @@
         around = {j: turned(advected[j % turns], j // turns) for j in range(-2, turns + 2)}
         largest = [None] * units
         for j in range(turns):
-            sin, cos = signs(part, parts, turns, directions, j)
-            speed = sin * turn_x - cos * turn_y
+            speed = trig[0, j] * turn_x - trig[1, j] * turn_y
             value = around[j] - upwind(speed, *[around[n] for n in range(j - 2, j + 3)])
             turned_values[into, j] = value
             size = jnp.abs(value)
@@ -326,6 +329,15 @@
             rest = rest | ((odd >> 15) << (24 + 2 * n))
         packed[chunk, first + 4] = rest
 
+    half = len(offsets)
+    _, words, slots = out_refs[0].shape
+    words = words // SUBLANES
+    spans = slots // LANES
+    comp = lax.axis_index("comp")
+    base = ((comp ^ offsets[0]) // half) * half
+    first_set = ranges_ref[base, 0] // together
+    last_set = ranges_ref[base + half - 1, 2 * spans] // together
+    sets = chunks // together
     for r in range(rows):
 
         def some_chunks(i, carry):
@@ -335,11 +347,10 @@
                     code(r * chunks + i * together + n, n, unit, found[n][unit])
             return carry
 
-        lax.fori_loop(0, chunks // together, some_chunks, 0)
-
-    groups, words, slots = out_ref.shape
-    words = words // SUBLANES
-    spans = slots // LANES
+        low = jnp.clip(first_set - r * sets, 0, sets)
+        high = jnp.clip(last_set + 1 - r * sets, 0, sets)
+        lax.fori_loop(low, high, some_chunks, 0)
+
     last = rows * chunks - 1
 
     def merged(cells, chunk, sums):
@@ -353,36 +364,34 @@
             for n in range(words)
         )
 
-    def one_block(c, carry):
+    if len(out_refs) == half:
+        places = [(comp ^ offset, out_ref, 0) for offset, out_ref in zip(offsets, out_refs)]
+    else:
+        places = [(base + n, out_refs[0], n) for n in range(half)]
+    for block, out_ref, at in places:
         for m in range(spans):
             span = slice(m * LANES, (m + 1) * LANES)
-            cells = cells_ref[c, :, span]
-            low = ranges_ref[c, m]
+            cells = cells_ref[block, :, span]
+            low = ranges_ref[block, m]
             sums = tuple(jnp.zeros(shape, I32) for _ in range(words))
             for t in range(WINDOW):
                 sums = merged(cells, jnp.minimum(low + t, last), sums)
             for n in range(words):
-                out_ref[c, n * SUBLANES : (n + 1) * SUBLANES, span] = sums[n]
-        return carry
-
-    lax.fori_loop(0, groups, one_block, 0)
-
-    @pl.when(ranges_ref[groups, 0] > WINDOW)
+                out_ref[at, n * SUBLANES : (n + 1) * SUBLANES, span] = sums[n]
+
+    @pl.when(ranges_ref[cells_ref.shape[0], 0] > WINDOW)
     def _():
-        def longer_block(c, carry):
+        for block, out_ref, at in places:
             for m in range(spans):
                 span = slice(m * LANES, (m + 1) * LANES)
-                cells = cells_ref[c, :, span]
-                low, high = ranges_ref[c, m], ranges_ref[c, m + spans]
-                sums = tuple(out_ref[c, n * SUBLANES : (n + 1) * SUBLANES, span] for n in range(words))
+                cells = cells_ref[block, :, span]
+                low, high = ranges_ref[block, m], ranges_ref[block, m + spans]
+                sums = tuple(out_ref[at, n * SUBLANES : (n + 1) * SUBLANES, span] for n in range(words))
                 sums = lax.fori_loop(
                     low + WINDOW, high + 1, lambda chunk, sums: merged(cells, chunk, sums), sums
                 )
                 for n in range(words):
-                    out_ref[c, n * SUBLANES : (n + 1) * SUBLANES, span] = sums[n]
-            return carry
-
-        lax.fori_loop(0, groups, longer_block, 0)
+                    out_ref[at, n * SUBLANES : (n + 1) * SUBLANES, span] = sums[n]
 
 
 def grow_kernel(directions, wind_ref, cells_ref, ranges_ref, out_ref, flat, slot_wind):
@@ -420,8 +429,11 @@
         slot_wind[0, :, span] = jnp.broadcast_to(found[0:1], shape)
         slot_wind[1, :, span] = jnp.broadcast_to(found[1:2], shape)
 
-    rates = []
+    rates, places = [], []
+    half = groups // 2
     for source in range(groups):
+        index = source % half
+        places.append(jnp.where(comp // half == source // half, index, half + ((comp % half) ^ index)))
         slope, threshold = jnp.zeros(shape, F32), jnp.zeros(shape, F32)
         for f in range(freqs):
             angular, ratio = frequency(source * freqs + f, groups * freqs)
@@ -437,25 +449,19 @@
             along = east * cos + north * sin
             for source in range(groups):
                 slope, threshold = rates[source]
-                out_ref[source, j, :, span] = jnp.exp(jnp.maximum(along * slope - threshold, 0.0))
+                out_ref[places[source], j, :, span] = jnp.exp(jnp.maximum(along * slope - threshold, 0.0))
         return carry
 
     lax.fori_loop(0, spans, one_span, 0)
 
 
-def finish_kernel(freqs, arrived, counts_ref, grown_ref, out_ref, values, ordered):
-    groups = arrived.shape[0]
-    turns = values.shape[1]
-    units = turns // UNIT
-    directions_per = turns * SUBLANES
-    shape = (SUBLANES, LANES)
-    scale = power_table(2.0**-EXPONENT_ZERO / STEP_COUNT, 1)
-    comp = lax.axis_index("comp")
-    sums = [jnp.zeros(shape, F32) for _ in range(2)]
-    for source in range(groups):
-        for unit in range(units):
+def decode(arrived_refs, grown_ref, scale, store):
+    sums = [jnp.zeros((SUBLANES, LANES), F32) for _ in range(2)]
+    turns = grown_ref.shape[1]
+    for source, (arrived, at) in enumerate(arrived_refs):
+        for unit in range(turns // UNIT):
             words = [
-                arrived[source, n * SUBLANES : (n + 1) * SUBLANES, :]
+                arrived[at, n * SUBLANES : (n + 1) * SUBLANES, :]
                 for n in range(unit * WORDS, (unit + 1) * WORDS)
             ]
             rest = words[4]
@@ -472,31 +478,62 @@
                         lax.shift_right_logical(rest, 9 + n - 1) & 0x18000
                     )
                 value = coded.astype(F32) * size - offset
+                sums[n % 2] = sums[n % 2] + value * value
                 j = unit * UNIT + n
-                sums[n % 2] = sums[n % 2] + value * value
-                values[source, j] = value * grown_ref[source, j]
-    mean_sq = jnp.sum(sums[0] + sums[1], axis=0, keepdims=True) / float(groups * directions_per)
-    strength = jnp.sqrt(mean_sq + 1e-06)
-    strength = jnp.broadcast_to(strength, shape)
+                store(source, j, value * grown_ref[source, j])
+    return sums[0] + sums[1]
+
+
+def early_kernel(half, *refs):
+    arrived_refs, (grown_ref, out_ref, sums_ref) = [(ref, 0) for ref in refs[:half]], refs[half:]
+    own = lax.axis_index("comp") % half
+
+    def store(source, j, value):
+        out_ref[own ^ source, j] = value
+
+    sums_ref[...] = decode(arrived_refs, grown_ref, power_table(2.0**-EXPONENT_ZERO / STEP_COUNT, 1), store)
+
+
+def finish_kernel(freqs, half, *refs):
+    arrived_ref, grown_ref, early_ref, sums_ref, counts_ref, out_ref, values, ordered = refs
+    arrived_refs = [(arrived_ref, n) for n in range(half)]
+    groups = 2 * half
+    turns = values.shape[1]
+    each = turns * SUBLANES
+    shape = (SUBLANES, LANES)
+    comp = lax.axis_index("comp")
+    side = comp // half
+
+    def store(source, j, value):
+        values[source, j] = value
+
+    sums = decode(arrived_refs, grown_ref, power_table(2.0**-EXPONENT_ZERO / STEP_COUNT, 1), store)
+    mean_sq = jnp.sum(sums + sums_ref[...], axis=0, keepdims=True) / float(groups * each)
+    strength = jnp.broadcast_to(jnp.sqrt(mean_sq + 1e-06), shape)
     occupied = (pl.program_id(0) * LANES + iota(shape, 1)) < counts_ref[0, comp]
     freq = iota(shape, 0) // (SUBLANES // freqs)
-    for source in range(groups):
-        rate = jnp.zeros(shape, F32)
-        for f in range(freqs):
-            rate = jnp.where(freq == f, DAMPING * frequency(source * freqs + f, groups * freqs)[1], rate)
-        factor = jnp.exp(-(rate * strength))
-        for j in range(turns):
-            value = jnp.where(occupied, values[source, j] * factor, 0.0)
-            ordered[pl.ds(source * directions_per + j, SUBLANES, stride=turns), :] = value
+    for far in range(2):
+        place = side ^ far
+        step = jnp.where(place == 0, jnp.float32(1.0), jnp.float32(1.1 ** (half * freqs)))
+        for source in range(half):
+            rate = jnp.zeros(shape, F32)
+            for f in range(freqs):
+                rate = jnp.where(freq == f, DAMPING * frequency(source * freqs + f, groups * freqs)[1], rate)
+            factor = jnp.exp(-(rate * step * strength))
+            for j in range(turns):
+                value = early_ref[source, j] if far else values[source, j]
+                value = jnp.where(occupied, value * factor, 0.0)
+                ordered[place, pl.ds(source * each + j, SUBLANES, stride=turns), :] = value
     square = (LANES, LANES)
     unit_matrix = (iota(square, 0) == iota(square, 1)).astype(jnp.bfloat16)
-    turned = lax.dot_general(
-        unit_matrix,
-        ordered[...].astype(jnp.bfloat16),
-        (((1,), (1,)), ((), ())),
-        preferred_element_type=F32,
-    )
-    out_ref[...] = turned.astype(jnp.bfloat16)
+    for place in range(2):
+        turned = lax.dot_general(
+            unit_matrix,
+            ordered[place].astype(jnp.bfloat16),
+            (((1,), (1,)), ((), ())),
+            preferred_element_type=F32,
+        )
+        out_ref[:, place * half * each : (place + 1) * half * each] = turned.astype(jnp.bfloat16)
 
 
 def frequency(index, count):
@@ -531,6 +568,7 @@
         arrange_kernel,
         [half, half],
         (4 * hbm, 2 * hbm),
+        vmem=WHOLE_VMEM,
         grid=(turns // step,),
         in_specs=[
             pl.BlockSpec((freqs, parts, step, rows, lon), lambda i: (0, 0, i, 0, 0)),
@@ -568,18 +606,30 @@
         scratch_shapes=[pltpu.VMEM((2, height, padded), F32)],
     )(top, bottom, group_speed.T, depth_class, current, depth_slope)
 
-    sent = call(
-        functools.partial(pack_kernel, directions),
-        jax.ShapeDtypeStruct((groups, words * SUBLANES, slots), I32),
-        (50 * hbm, 4 * hbm),
-        in_specs=[vmem] * 5 + [smem],
-        out_specs=vmem,
-        scratch_shapes=[
-            pltpu.VMEM((rows * chunks, words, SUBLANES, LANES), I32),
-            pltpu.VMEM((4 if chunks % 4 == 0 else 1, turns, SUBLANES, LANES), F32),
-        ],
-    )(advected, above, below, coefs, cells, ranges)
-    arrived = lax.all_to_all(sent, "comp", split_axis=0, concat_axis=0, tiled=True)
+    half = groups // 2
+    block = (words * SUBLANES, slots)
+    after, shipped = ranges, []
+    for offsets, outputs in ((range(half, groups), [(1,) + block] * half), (range(half), [(half,) + block])):
+        shipped.append(
+            call(
+                functools.partial(pack_kernel, directions, tuple(offsets)),
+                [jax.ShapeDtypeStruct(shape, I32) for shape in outputs],
+                (25 * hbm, 3 * hbm),
+                in_specs=[vmem] * 5 + [smem, pl.BlockSpec(memory_space=pl.ANY)],
+                out_specs=[vmem] * len(outputs),
+                scratch_shapes=[
+                    pltpu.VMEM((rows * chunks, words, SUBLANES, LANES), I32),
+                    pltpu.VMEM((4 if chunks % 4 == 0 else 1, turns, SUBLANES, LANES), F32),
+                    pltpu.VMEM((2, turns, SUBLANES, LANES), F32),
+                ],
+            )(advected, above, below, coefs, cells, ranges, after)
+        )
+        after = shipped[0][0]
+    far = [
+        lax.ppermute(part, "comp", [(i, i ^ (half + n)) for i in range(groups)]) for n, part in enumerate(shipped[0])
+    ]
+    halves = [list(range(half)), list(range(half, groups))]
+    near = lax.all_to_all(shipped[1][0], "comp", split_axis=0, concat_axis=0, axis_index_groups=halves, tiled=True)
 
     total = total_freqs * directions
     grown = call(
@@ -594,22 +644,39 @@
         ],
     )(wind, cells, ranges)
 
+    arrived_spec = pl.BlockSpec((1, words * SUBLANES, LANES), lambda i: (0, 0, i))
+    half_block = (half, turns, SUBLANES, LANES)
+    sums_spec = pl.BlockSpec((SUBLANES, LANES), lambda i: (0, i))
+    early, sums = call(
+        functools.partial(early_kernel, half),
+        [
+            jax.ShapeDtypeStruct((half, turns, SUBLANES, slots), F32),
+            jax.ShapeDtypeStruct((SUBLANES, slots), F32),
+        ],
+        (10 * total * slots, 4 * total * slots),
+        grid=(slots // LANES,),
+        in_specs=[arrived_spec] * half + [pl.BlockSpec(half_block, lambda i: (1, 0, 0, i))],
+        out_specs=[pl.BlockSpec(half_block, lambda i: (0, 0, 0, i)), sums_spec],
+    )(*far, grown)
+
     result = call(
-        functools.partial(finish_kernel, freqs),
+        functools.partial(finish_kernel, freqs, half),
         jax.ShapeDtypeStruct((slot_count, total), jnp.bfloat16),
         (50 * total * slots, 6 * total * slots),
         grid=(slots // LANES,),
         in_specs=[
-            pl.BlockSpec((groups, words * SUBLANES, LANES), lambda i: (0, 0, i)),
+            pl.BlockSpec((half, words * SUBLANES, LANES), lambda i: (0, 0, i)),
+            pl.BlockSpec(half_block, lambda i: (0, 0, 0, i)),
+            pl.BlockSpec(half_block, lambda i: (0, 0, 0, i)),
+            sums_spec,
             smem,
-            pl.BlockSpec((groups, turns, SUBLANES, LANES), lambda i: (0, 0, 0, i)),
         ],
         out_specs=pl.BlockSpec((LANES, total), lambda i: (i, 0)),
         scratch_shapes=[
-            pltpu.VMEM((groups, turns, SUBLANES, LANES), F32),
-            pltpu.VMEM((total, LANES), F32),
+            pltpu.VMEM(half_block, F32),
+            pltpu.VMEM((2, total // 2, LANES), F32),
         ],
-    )(arrived, block_counts, grown)
+    )(near, grown, early, sums, block_counts)
     return result.T
 
 

time: 76.4 us -> 83.7 us (1.096)
  the two profiles are of different devices: /device:TPU:1 before, /device:TPU:18 now
where the time goes in v3:
time: 83.7 us; the launch traced here: 83.2 us
  Pallas kernels  31.6 us (38%)
  waiting for transfers between devices  30.9 us (37%)
  starting transfers between devices  15.7 us (19%)
  local copies, waits for them, and re-layouts  4.86 us (6%)
    ppermute x4, waiting for transfers between devices, body(): lax.ppermute(part, 'comp', [(i, i ^ half + n) for i in range(groups)])  29.6 us
    pallas_call x2, Pallas kernels, body(): call(functools.partial(pack_kernel, directions, tuple(offsets)), [jax.Sha...  10.7 us
    ppermute x4, starting transfers between devices, body(): lax.ppermute(part, 'comp', [(i, i ^ half + n) for i in range(groups)])  5.91 us
    pallas_call x1, Pallas kernels, body(): call(functools.partial(finish_kernel, freqs, half), jax.ShapeDtypeStruct(...  5.49 us
    pallas_call x1, Pallas kernels, body(): call(functools.partial(advect_kernel, directions, stretch), [jax.ShapeDty...  5.45 us
    pallas_call x1, Pallas kernels, body(): call(arrange_kernel, [half, half], (4 * hbm, 2 * hbm), vmem=WHOLE_VMEM, g...  5.39 us
    unnamed x22, local copies, waits for them, and re-layouts  4.86 us
    all_to_all x1, starting transfers between devices, body(): lax.all_to_all(shipped[1][0], 'comp', split_axis=0, concat_axis=0, axis_i...  4.2 us
  transfers between devices with their start and end apart: 7, of which 5 were waited for; matrix products, arithmetic and copies ran while one was open for 0% of the time, Pallas kernels for 12%

profile of v3, /device:TPU:18, one launch (start us, length us, event | category | flops | bytes accessed | tf_op | source)
XLA Modules:
  0.0 83.2 jit_solution(3163329460543192817)
XLA Ops:
  0.0 5.4 %shard_map.82 = (bf16[18,16,1536]{2,1,0:T(8,128)(2,1)}, bf16[18,16,1536]{2,1,0:T(8,128)(2,1)}) custom-call(bf16[4,2,18,4,1440]{4,3,2,1,0:T(4,128)(2,1)} %bitcast.4, s32[4,1440]{1,0:T(4,128)} %land_ref.3), custom_call_target="tpu_custom_call" | custom-call | flops 7077888 | bytes 3538944 | tf_op jit(solution)/shard_map/pallas_call | solution.py:567
  5.4 1.9 %collective-permute-start = (bf16[18,16,1536]{2,1,0:T(8,128)(2,1)}, bf16[18,16,1536]{2,1,0:T(8,128)(2,1)S(1)}, u32[]{:S(2)}, u32[]{:S(2)}) collective-permute-start(bf16[18,16,1536]{2,1,0:T(8,128)(2,1)} %get-tuple-element.18.bottom_ref), channel_id=1, source_target_pairs={{0,1},{1,2},{2,3},{4,5},{5,6},{6,7},{8,9},{9,10},{10,11},{12,13},{... | collective-permute-start | bytes 2654216 | tf_op jit(solution)/shard_map/ppermute | solution.py:581
  7.3 3.6 %collective-permute-start.1 = (bf16[18,16,1536]{2,1,0:T(8,128)(2,1)}, bf16[18,16,1536]{2,1,0:T(8,128)(2,1)S(1)}, u32[]{:S(2)}, u32[]{:S(2)}) collective-permute-start(bf16[18,16,1536]{2,1,0:T(8,128)(2,1)} %get-tuple-element.17.top_ref), channel_id=1, source_target_pairs={{1,0},{2,1},{3,2},{5,4},{6,5},{7,6},{9,8},{10,9},{11,10},{13,12},{... | collective-permute-start | bytes 2654216 | tf_op jit(solution)/shard_map/ppermute | solution.py:582
  11.0 1.7 %shard_map.84 = (s32[8,8,640]{2,1,0:T(8,128)S(1)}, s32[16,128]{1,0:T(8,128)S(1)}) custom-call(s32[4,1440]{1,0:T(4,128)S(1)} %copy-done.4, s32[1,8]{1,0:T(1,128)S(1)} %copy-done.10), custom_call_target="tpu_custom_call" | custom-call | flops 512000 | bytes 40960 | tf_op jit(solution)/shard_map/pallas_call | solution.py:585
  12.7 1.2 %copy-done.2 = bf16[18,16,1536]{2,1,0:T(8,128)(2,1)S(1)} copy-done((bf16[18,16,1536]{2,1,0:T(8,128)(2,1)S(1)}, bf16[18,16,1536]{2,1,0:T(8,128)(2,1)}, u32[]{:S(2)}) %copy-start.2) | copy-done | bytes 884760
  13.9 1.2 %copy-done.3 = bf16[18,16,1536]{2,1,0:T(8,128)(2,1)S(1)} copy-done((bf16[18,16,1536]{2,1,0:T(8,128)(2,1)S(1)}, bf16[18,16,1536]{2,1,0:T(8,128)(2,1)}, u32[]{:S(2)}) %copy-start.3) | copy-done | bytes 884760
  15.1 5.4 %shard_map.83 = (f32[18,32,1536]{2,1,0:T(8,128)S(1)}, f32[4,32,1536]{2,1,0:T(8,128)S(1)}) custom-call(bf16[18,16,1536]{2,1,0:T(8,128)(2,1)S(1)} %copy-done.2, bf16[18,16,1536]{2,1,0:T(8,128)(2,1)S(1)} %copy-done.3, f32[32,64]{1,0:T(8,128)S(1)} %bitcast.3, s32[4,1440]{1,0:T(4,128)S(1)} %copy-done.8, f32[2,4,1440]{2,1,0:T(4,128)S(1)} %copy-done.6, ...), custom_call_target="tpu_custom_call" | custom-call | flops 88473600 | bytes 7077888 | tf_op jit(solution)/shard_map/pallas_call | solution.py:597
  20.5 1.3 %collective-permute-done.1.below_ref = bf16[18,16,1536]{2,1,0:T(8,128)(2,1)S(1)} collective-permute-done((bf16[18,16,1536]{2,1,0:T(8,128)(2,1)}, bf16[18,16,1536]{2,1,0:T(8,128)(2,1)S(1)}, u32[]{:S(2)}, u32[]{:S(2)}) %collective-permute-start.1) | collective-permute-done | bytes 884768 | tf_op jit(solution)/shard_map/ppermute | solution.py:582
  21.9 5.2 %shard_map.85 = (s32[1,80,640]{2,1,0:T(8,128)S(1)}, s32[1,80,640]{2,1,0:T(8,128)}, s32[1,80,640]{2,1,0:T(8,128)}, s32[1,80,640]{2,1,0:T(8,128)}) custom-call(f32[18,32,1536]{2,1,0:T(8,128)S(1)} %get-tuple-element.19.adv_ref, bf16[18,16,1536]{2,1,0:T(8,128)(2,1)S(1)} %collective-permute-done.above_ref, ...), custom_call_target="tpu_custom_call" | custom-call | flops 44236800 | bytes 5308416 | tf_op jit(solution)/shard_map/pallas_call | solution.py:614
  27.0 5.6 %shard_map.86 = s32[4,80,640]{2,1,0:T(8,128)} custom-call(f32[18,32,1536]{2,1,0:T(8,128)S(1)} %get-tuple-element.19.adv_ref, bf16[18,16,1536]{2,1,0:T(8,128)(2,1)S(1)} %collective-permute-done.above_ref, bf16[18,16,1536]{2,1,0:T(8,128)(2,1)S(1)} %collective-permute-done.1.below_ref, f32[4,32,1536]{2,1,0:T(8,128)S(1)} %get-tuple-element.20.coef_ref, ...), custom_call_target="tpu_custom_call" | custom-call | flops 44236800 | bytes 5308416 | tf_op jit(solution)/shard_map/pallas_call | solution.py:614
  32.6 4.2 %all-to-all-start = ((s32[4,80,640]{2,1,0:T(8,128)}), s32[4,80,640]{2,1,0:T(8,128)}, u32[]{:S(2)}, u32[]{:S(2)}) async-start(s32[4,80,640]{2,1,0:T(8,128)} %shard_map.86), calls=%async_computation | async-start | bytes 1638400 | tf_op jit(solution)/shard_map/all_to_all | solution.py:632
  36.8 0.4 collective-permute-start.2
  37.2 3.9 %collective-permute-start.3 = (s32[1,80,640]{2,1,0:T(8,128)}, s32[1,80,640]{2,1,0:T(8,128)S(1)}, u32[]{:S(2)}, u32[]{:S(2)}) collective-permute-start(s32[1,80,640]{2,1,0:T(8,128)} %get-tuple-element.24), channel_id=1, source_target_pairs={{0,20},{4,16},{8,28},{12,24},{16,4},{20,0},{24,12},{28,8},{1,21},{... | collective-permute-start | bytes 614408 | tf_op jit(solution)/shard_map/ppermute | solution.py:629
  41.1 0.3 collective-permute-start.4
  41.5 1.2 %collective-permute-start.5 = (s32[1,80,640]{2,1,0:T(8,128)}, s32[1,80,640]{2,1,0:T(8,128)S(1)}, u32[]{:S(2)}, u32[]{:S(2)}) collective-permute-start(s32[1,80,640]{2,1,0:T(8,128)} %get-tuple-element.26), channel_id=1, source_target_pairs={{0,28},{4,24},{8,20},{12,16},{16,12},{20,8},{24,4},{28,0},{1,29},{... | collective-permute-start | bytes 614408 | tf_op jit(solution)/shard_map/ppermute | solution.py:629
  42.7 1.8 %shard_map.87.refs_4_.refs_1_ = f32[8,18,8,640]{3,2,1,0:T(8,128)S(1)} custom-call(f32[2,4,1440]{2,1,0:T(4,128)S(1)} %copy-done.5, s32[8,8,640]{2,1,0:T(8,128)S(1)} %get-tuple-element.21.cells_ref, s32[16,128]{1,0:T(8,128)S(1)} %get-tuple-element.22.ranges_ref.after_ref), custom_call_target="tpu_custom_call" | custom-call | flops 14745600 | bytes 2949120 | tf_op jit(solution)/shard_map/pallas_call | solution.py:635
  44.5 7.7 %collective-permute-done.2.refs_0_ = s32[1,80,640]{2,1,0:T(8,128)S(1)} collective-permute-done((s32[1,80,640]{2,1,0:T(8,128)S(1)}, s32[1,80,640]{2,1,0:T(8,128)S(1)}, u32[]{:S(2)}, u32[]{:S(2)}) %collective-permute-start.2) | collective-permute-done | bytes 204832 | tf_op jit(solution)/shard_map/ppermute | solution.py:629
  52.2 12.4 %collective-permute-done.3.refs_1_ = s32[1,80,640]{2,1,0:T(8,128)S(1)} collective-permute-done((s32[1,80,640]{2,1,0:T(8,128)}, s32[1,80,640]{2,1,0:T(8,128)S(1)}, u32[]{:S(2)}, u32[]{:S(2)}) %collective-permute-start.3) | collective-permute-done | bytes 204832 | tf_op jit(solution)/shard_map/ppermute | solution.py:629
  64.6 6.4 %collective-permute-done.4.refs_2_ = s32[1,80,640]{2,1,0:T(8,128)S(1)} collective-permute-done((s32[1,80,640]{2,1,0:T(8,128)}, s32[1,80,640]{2,1,0:T(8,128)S(1)}, u32[]{:S(2)}, u32[]{:S(2)}) %collective-permute-start.4) | collective-permute-done | bytes 204832 | tf_op jit(solution)/shard_map/ppermute | solution.py:629
  71.0 3.1 %collective-permute-done.5.refs_3_ = s32[1,80,640]{2,1,0:T(8,128)S(1)} collective-permute-done((s32[1,80,640]{2,1,0:T(8,128)}, s32[1,80,640]{2,1,0:T(8,128)S(1)}, u32[]{:S(2)}, u32[]{:S(2)}) %collective-permute-start.5) | collective-permute-done | bytes 204832 | tf_op jit(solution)/shard_map/ppermute | solution.py:629
  74.1 1.1 %shard_map.88 = (f32[4,18,8,640]{3,2,1,0:T(8,128)S(1)}, f32[8,640]{1,0:T(8,128)S(1)}) custom-call(s32[1,80,640]{2,1,0:T(8,128)S(1)} %collective-permute-done.2.refs_0_, s32[1,80,640]{2,1,0:T(8,128)S(1)} %collective-permute-done.3.refs_1_, s32[1,80,640]{2,1,0:T(8,128)S(1)} %collective-permute-done.4.refs_2_, ...), custom_call_target="tpu_custom_call" | custom-call | flops 7372800 | bytes 2949120 | tf_op jit(solution)/shard_map/pallas_call | solution.py:650
  75.2 1.1 %copy-done = f32[4,18,8,640]{3,2,1,0:T(8,128)} copy-done((f32[4,18,8,640]{3,2,1,0:T(8,128)}, f32[4,18,8,640]{3,2,1,0:T(8,128)S(1)}, u32[]{:S(2)}) %copy-start) | copy-done | bytes 1474584
  76.3 1.4 %copy-done.1 = f32[4,18,8,640]{3,2,1,0:T(8,128)S(1)} copy-done((f32[4,18,8,640]{3,2,1,0:T(8,128)S(1)}, f32[4,18,8,640]{3,2,1,0:T(8,128)}, u32[]{:S(2)}) %copy-start.1) | copy-done | bytes 1474584
  77.7 5.5 %shard_map.89 = bf16[630,1152]{1,0:T(8,128)(2,1)} custom-call(s32[4,80,640]{2,1,0:T(8,128)} %all-to-all-done.refs_0_, f32[8,18,8,640]{3,2,1,0:T(8,128)S(1)} %shard_map.87.refs_4_.refs_1_, f32[4,18,8,640]{3,2,1,0:T(8,128)S(1)} %copy-done.1, f32[8,640]{1,0:T(8,128)S(1)} %get-tuple-element.28.refs_3_, s32[1,8]{1,0:T(1,128)S(1)} %copy-done.10), custom_call_target="tpu_custom_call" | custom-call | flops 36864000 | bytes 4423680 | tf_op jit(solution)/shard_map/pallas_call | solution.py:662
  (20 shorter events, 0.0 us)
Async XLA Ops:
  0.0 11.0 %copy-start.4 = (s32[4,1440]{1,0:T(4,128)S(1)}, s32[4,1440]{1,0:T(4,128)}, u32[]{:S(2)}) copy-start(s32[4,1440]{1,0:T(4,128)} %land_ref.3) | copy-start | bytes 69124
  0.0 11.0 %copy-start.10 = (s32[1,8]{1,0:T(1,128)S(1)}, s32[1,8]{1,0:T(1,128)}, u32[]{:S(2)}) copy-start(s32[1,8]{1,0:T(1,128)} %refs_4_.1) | copy-start | bytes 100
  0.0 12.7 %copy-start.9 = (f32[64,32]{0,1:T(8,128)S(1)}, f32[64,32]{0,1:T(8,128)}, u32[]{:S(2)}) copy-start(f32[64,32]{0,1:T(8,128)} %param.10) | copy-start | bytes 24580
  0.0 12.7 %copy-start.8 = (s32[4,1440]{1,0:T(4,128)S(1)}, s32[4,1440]{1,0:T(4,128)}, u32[]{:S(2)}) copy-start(s32[4,1440]{1,0:T(4,128)} %depth_ref.1) | copy-start | bytes 69124
  0.0 12.7 %copy-start.6 = (f32[2,4,1440]{2,1,0:T(4,128)S(1)}, f32[2,4,1440]{2,1,0:T(4,128)}, u32[]{:S(2)}) copy-start(f32[2,4,1440]{2,1,0:T(4,128)} %current_ref.1) | copy-start | bytes 138244
  0.0 12.7 %copy-start.7 = (f32[2,4,1440]{2,1,0:T(4,128)S(1)}, f32[2,4,1440]{2,1,0:T(4,128)}, u32[]{:S(2)}) copy-start(f32[2,4,1440]{2,1,0:T(4,128)} %slope_ref.1) | copy-start | bytes 138244
  5.4 15.1 %collective-permute-start = (bf16[18,16,1536]{2,1,0:T(8,128)(2,1)}, bf16[18,16,1536]{2,1,0:T(8,128)(2,1)S(1)}, u32[]{:S(2)}, u32[]{:S(2)}) collective-permute-start(bf16[18,16,1536]{2,1,0:T(8,128)(2,1)} %get-tuple-element.18.bottom_ref), channel_id=1, source_target_pairs={{0,1},{1,2},{2,3},{4,5},{5,6},{6,7},{8,9},{9,10},{10,11},{12,13},{... | collective-permute-start | bytes 2654216 | tf_op jit(solution)/shard_map/ppermute | solution.py:581
  7.3 14.5 %collective-permute-start.1 = (bf16[18,16,1536]{2,1,0:T(8,128)(2,1)}, bf16[18,16,1536]{2,1,0:T(8,128)(2,1)S(1)}, u32[]{:S(2)}, u32[]{:S(2)}) collective-permute-start(bf16[18,16,1536]{2,1,0:T(8,128)(2,1)} %get-tuple-element.17.top_ref), channel_id=1, source_target_pairs={{1,0},{2,1},{3,2},{5,4},{6,5},{7,6},{9,8},{10,9},{11,10},{13,12},{... | collective-permute-start | bytes 2654216 | tf_op jit(solution)/shard_map/ppermute | solution.py:582
  12.7 1.2 %copy-start.2 = (bf16[18,16,1536]{2,1,0:T(8,128)(2,1)S(1)}, bf16[18,16,1536]{2,1,0:T(8,128)(2,1)}, u32[]{:S(2)}) copy-start(bf16[18,16,1536]{2,1,0:T(8,128)(2,1)} %get-tuple-element.17.top_ref) | copy-start | bytes 2654212
  13.9 1.2 %copy-start.3 = (bf16[18,16,1536]{2,1,0:T(8,128)(2,1)S(1)}, bf16[18,16,1536]{2,1,0:T(8,128)(2,1)}, u32[]{:S(2)}) copy-start(bf16[18,16,1536]{2,1,0:T(8,128)(2,1)} %get-tuple-element.18.bottom_ref) | copy-start | bytes 2654212
  27.0 15.7 %copy-start.5 = (f32[2,4,1440]{2,1,0:T(4,128)S(1)}, f32[2,4,1440]{2,1,0:T(4,128)}, u32[]{:S(2)}) copy-start(f32[2,4,1440]{2,1,0:T(4,128)} %wind_ref.1) | copy-start | bytes 138244
  32.6 43.7 %all-to-all-start = ((s32[4,80,640]{2,1,0:T(8,128)}), s32[4,80,640]{2,1,0:T(8,128)}, u32[]{:S(2)}, u32[]{:S(2)}) async-start(s32[4,80,640]{2,1,0:T(8,128)} %shard_map.86), calls=%async_computation | async-start | bytes 1638400 | tf_op jit(solution)/shard_map/all_to_all | solution.py:632
  36.8 15.4 %collective-permute-start.2 = (s32[1,80,640]{2,1,0:T(8,128)S(1)}, s32[1,80,640]{2,1,0:T(8,128)S(1)}, u32[]{:S(2)}, u32[]{:S(2)}) collective-permute-start(s32[1,80,640]{2,1,0:T(8,128)S(1)} %get-tuple-element.23.after_ref), channel_id=1, source_target_pairs={{0,16},{4,20},{8,24},{12,28},{16,0},{20,4},{24,8},{28,12},{1,17},{... | collective-permute-start | bytes 614408 | tf_op jit(solution)/shard_map/ppermute | solution.py:629
  37.2 27.4 %collective-permute-start.3 = (s32[1,80,640]{2,1,0:T(8,128)}, s32[1,80,640]{2,1,0:T(8,128)S(1)}, u32[]{:S(2)}, u32[]{:S(2)}) collective-permute-start(s32[1,80,640]{2,1,0:T(8,128)} %get-tuple-element.24), channel_id=1, source_target_pairs={{0,20},{4,16},{8,28},{12,24},{16,4},{20,0},{24,12},{28,8},{1,21},{... | collective-permute-start | bytes 614408 | tf_op jit(solution)/shard_map/ppermute | solution.py:629
  41.1 29.9 %collective-permute-start.4 = (s32[1,80,640]{2,1,0:T(8,128)}, s32[1,80,640]{2,1,0:T(8,128)S(1)}, u32[]{:S(2)}, u32[]{:S(2)}) collective-permute-start(s32[1,80,640]{2,1,0:T(8,128)} %get-tuple-element.25), channel_id=1, source_target_pairs={{0,24},{4,28},{8,16},{12,20},{16,8},{20,12},{24,0},{28,4},{1,25},{... | collective-permute-start | bytes 614408 | tf_op jit(solution)/shard_map/ppermute | solution.py:629
  41.5 32.6 %collective-permute-start.5 = (s32[1,80,640]{2,1,0:T(8,128)}, s32[1,80,640]{2,1,0:T(8,128)S(1)}, u32[]{:S(2)}, u32[]{:S(2)}) collective-permute-start(s32[1,80,640]{2,1,0:T(8,128)} %get-tuple-element.26), channel_id=1, source_target_pairs={{0,28},{4,24},{8,20},{12,16},{16,12},{20,8},{24,4},{28,0},{1,29},{... | collective-permute-start | bytes 614408 | tf_op jit(solution)/shard_map/ppermute | solution.py:629
  75.2 1.1 %copy-start = (f32[4,18,8,640]{3,2,1,0:T(8,128)}, f32[4,18,8,640]{3,2,1,0:T(8,128)S(1)}, u32[]{:S(2)}) copy-start(f32[4,18,8,640]{3,2,1,0:T(8,128)S(1)} %get-tuple-element.27.refs_2_) | copy-start | bytes 4423684
  76.3 1.4 %copy-start.1 = (f32[4,18,8,640]{3,2,1,0:T(8,128)S(1)}, f32[4,18,8,640]{3,2,1,0:T(8,128)}, u32[]{:S(2)}) copy-start(f32[4,18,8,640]{3,2,1,0:T(8,128)} %copy-done) | copy-start | bytes 4423684

commit v4 on v3

--- a/solution.py
+++ b/solution.py
@@ -21,7 +21,9 @@
 EXPONENT_ZERO = 99
 WINDOW = 4
 VMEM_BYTES = 16 * 1024 * 1024
-WHOLE_VMEM = 62_000_000
+LITTLE = (1_000, 1_000)
+MUCH = (200_000_000_000, 1_000_000)
+FINISH_VMEM = 28 * 1024 * 1024
 
 F32 = jnp.float32
 I32 = jnp.int32
@@ -394,8 +396,9 @@
                     out_ref[at, n * SUBLANES : (n + 1) * SUBLANES, span] = sums[n]
 
 
-def grow_kernel(directions, wind_ref, cells_ref, ranges_ref, out_ref, flat, slot_wind):
-    groups, turns, _, slots = out_ref.shape
+def grow_kernel(directions, wind_ref, cells_ref, ranges_ref, near_ref, far_ref, flat, slot_wind):
+    half, turns, _, slots = near_ref.shape
+    groups = 2 * half
     rows, lon = wind_ref.shape[1:]
     chunks = flat.shape[0] // rows
     tail = lon - (chunks - 1) * LANES
@@ -429,17 +432,16 @@
         slot_wind[0, :, span] = jnp.broadcast_to(found[0:1], shape)
         slot_wind[1, :, span] = jnp.broadcast_to(found[1:2], shape)
 
-    rates, places = [], []
-    half = groups // 2
-    for source in range(groups):
-        index = source % half
-        places.append(jnp.where(comp // half == source // half, index, half + ((comp % half) ^ index)))
-        slope, threshold = jnp.zeros(shape, F32), jnp.zeros(shape, F32)
-        for f in range(freqs):
-            angular, ratio = frequency(source * freqs + f, groups * freqs)
-            slope = jnp.where(freq == f, GROWTH_RATE * ratio * angular / 9.81, slope)
-            threshold = jnp.where(freq == f, GROWTH_RATE * ratio, threshold)
-        rates.append((slope, threshold))
+    rates = []
+    for far in range(2):
+        step = jnp.where((comp // half) ^ far == 0, jnp.float32(1.0), jnp.float32(1.1 ** (half * freqs)))
+        for source in range(half):
+            slope, threshold = jnp.zeros(shape, F32), jnp.zeros(shape, F32)
+            for f in range(freqs):
+                angular, ratio = frequency(source * freqs + f, groups * freqs)
+                slope = jnp.where(freq == f, GROWTH_RATE * ratio * angular / 9.81, slope)
+                threshold = jnp.where(freq == f, GROWTH_RATE * ratio, threshold)
+            rates.append((slope * (step * step), threshold * step))
 
     def one_span(m, carry):
         span = pl.ds(pl.multiple_of(m * LANES, LANES), LANES)
@@ -447,21 +449,23 @@
         for j in range(turns):
             sin, cos = signs(part, parts, turns, directions, j)
             along = east * cos + north * sin
-            for source in range(groups):
+            for source in range(half):
                 slope, threshold = rates[source]
-                out_ref[places[source], j, :, span] = jnp.exp(jnp.maximum(along * slope - threshold, 0.0))
+                near_ref[source, j, :, span] = jnp.exp(jnp.maximum(along * slope - threshold, 0.0))
+                slope, threshold = rates[half + source]
+                far_ref[(comp % half) ^ source, j, :, span] = jnp.exp(jnp.maximum(along * slope - threshold, 0.0))
         return carry
 
     lax.fori_loop(0, spans, one_span, 0)
 
 
-def decode(arrived_refs, grown_ref, scale, store):
+def decode(arrived_refs, grown_ref, scale, span, store):
     sums = [jnp.zeros((SUBLANES, LANES), F32) for _ in range(2)]
     turns = grown_ref.shape[1]
     for source, (arrived, at) in enumerate(arrived_refs):
         for unit in range(turns // UNIT):
             words = [
-                arrived[at, n * SUBLANES : (n + 1) * SUBLANES, :]
+                arrived[at, n * SUBLANES : (n + 1) * SUBLANES, span]
                 for n in range(unit * WORDS, (unit + 1) * WORDS)
             ]
             rest = words[4]
@@ -480,60 +484,68 @@
                 value = coded.astype(F32) * size - offset
                 sums[n % 2] = sums[n % 2] + value * value
                 j = unit * UNIT + n
-                store(source, j, value * grown_ref[source, j])
+                store(source, j, value * grown_ref[source, j, :, span])
     return sums[0] + sums[1]
 
 
 def early_kernel(half, *refs):
     arrived_refs, (grown_ref, out_ref, sums_ref) = [(ref, 0) for ref in refs[:half]], refs[half:]
     own = lax.axis_index("comp") % half
-
-    def store(source, j, value):
-        out_ref[own ^ source, j] = value
-
-    sums_ref[...] = decode(arrived_refs, grown_ref, power_table(2.0**-EXPONENT_ZERO / STEP_COUNT, 1), store)
-
-
-def finish_kernel(freqs, half, *refs):
-    arrived_ref, grown_ref, early_ref, sums_ref, counts_ref, out_ref, values, ordered = refs
+    scale = power_table(2.0**-EXPONENT_ZERO / STEP_COUNT, 1)
+    for low in range(0, out_ref.shape[-1], LANES):
+        span = slice(low, low + LANES)
+
+        def store(source, j, value):
+            out_ref[own ^ source, j, :, span] = value
+
+        sums_ref[:, span] = decode(arrived_refs, grown_ref, scale, span, store)
+
+
+def finish_kernel(freqs, half, arrived_ref, grown_ref, early_ref, sums_ref, counts_ref, out_ref, values, ordered):
     arrived_refs = [(arrived_ref, n) for n in range(half)]
     groups = 2 * half
-    turns = values.shape[1]
+    turns = values.shape[2]
     each = turns * SUBLANES
     shape = (SUBLANES, LANES)
     comp = lax.axis_index("comp")
     side = comp // half
-
-    def store(source, j, value):
-        values[source, j] = value
-
-    sums = decode(arrived_refs, grown_ref, power_table(2.0**-EXPONENT_ZERO / STEP_COUNT, 1), store)
-    mean_sq = jnp.sum(sums + sums_ref[...], axis=0, keepdims=True) / float(groups * each)
-    strength = jnp.broadcast_to(jnp.sqrt(mean_sq + 1e-06), shape)
-    occupied = (pl.program_id(0) * LANES + iota(shape, 1)) < counts_ref[0, comp]
+    count = counts_ref[0, comp]
+    scale = power_table(2.0**-EXPONENT_ZERO / STEP_COUNT, 1)
     freq = iota(shape, 0) // (SUBLANES // freqs)
-    for far in range(2):
-        place = side ^ far
-        step = jnp.where(place == 0, jnp.float32(1.0), jnp.float32(1.1 ** (half * freqs)))
-        for source in range(half):
-            rate = jnp.zeros(shape, F32)
-            for f in range(freqs):
-                rate = jnp.where(freq == f, DAMPING * frequency(source * freqs + f, groups * freqs)[1], rate)
-            factor = jnp.exp(-(rate * step * strength))
-            for j in range(turns):
-                value = early_ref[source, j] if far else values[source, j]
-                value = jnp.where(occupied, value * factor, 0.0)
-                ordered[place, pl.ds(source * each + j, SUBLANES, stride=turns), :] = value
     square = (LANES, LANES)
     unit_matrix = (iota(square, 0) == iota(square, 1)).astype(jnp.bfloat16)
-    for place in range(2):
-        turned = lax.dot_general(
-            unit_matrix,
-            ordered[place].astype(jnp.bfloat16),
-            (((1,), (1,)), ((), ())),
-            preferred_element_type=F32,
-        )
-        out_ref[:, place * half * each : (place + 1) * half * each] = turned.astype(jnp.bfloat16)
+    steps = [jnp.where(side ^ far == 0, jnp.float32(1.0), jnp.float32(1.1 ** (half * freqs))) for far in range(2)]
+    for m in range(values.shape[0]):
+        span = slice(m * LANES, (m + 1) * LANES)
+
+        def store(source, j, value):
+            values[m, source, j] = value
+
+        sums = decode(arrived_refs, grown_ref, scale, span, store)
+        mean_sq = jnp.sum(sums + sums_ref[:, span], axis=0, keepdims=True) / float(groups * each)
+        strength = jnp.broadcast_to(jnp.sqrt(mean_sq + 1e-06), shape)
+        occupied = (m * LANES + iota(shape, 1)) < count
+        for far in range(2):
+            for source in range(half):
+                rate = jnp.zeros(shape, F32)
+                for f in range(freqs):
+                    rate = jnp.where(freq == f, DAMPING * frequency(source * freqs + f, groups * freqs)[1], rate)
+                factor = jnp.exp(-(rate * steps[far] * strength))
+                for j in range(turns):
+                    value = early_ref[source, j, :, span] if far else values[m, source, j]
+                    value = jnp.where(occupied, value * factor, 0.0)
+                    ordered[m, side ^ far, pl.ds(source * each + j, SUBLANES, stride=turns), :] = value
+        slots = slice(m * LANES, min((m + 1) * LANES, out_ref.shape[0]))
+        for place in range(2):
+            turned = lax.dot_general(
+                unit_matrix,
+                ordered[m, place].astype(jnp.bfloat16),
+                (((1,), (1,)), ((), ())),
+                preferred_element_type=F32,
+            )
+            out_ref[slots, place * half * each : (place + 1) * half * each] = turned[
+                : slots.stop - slots.start
+            ].astype(jnp.bfloat16)
 
 
 def frequency(index, count):
@@ -568,7 +580,6 @@
         arrange_kernel,
         [half, half],
         (4 * hbm, 2 * hbm),
-        vmem=WHOLE_VMEM,
         grid=(turns // step,),
         in_specs=[
             pl.BlockSpec((freqs, parts, step, rows, lon), lambda i: (0, 0, i, 0, 0)),
@@ -614,12 +625,12 @@
             call(
                 functools.partial(pack_kernel, directions, tuple(offsets)),
                 [jax.ShapeDtypeStruct(shape, I32) for shape in outputs],
-                (25 * hbm, 3 * hbm),
+                (25 * hbm, 3 * hbm) if len(outputs) > 1 else LITTLE,
                 in_specs=[vmem] * 5 + [smem, pl.BlockSpec(memory_space=pl.ANY)],
                 out_specs=[vmem] * len(outputs),
                 scratch_shapes=[
                     pltpu.VMEM((rows * chunks, words, SUBLANES, LANES), I32),
-                    pltpu.VMEM((4 if chunks % 4 == 0 else 1, turns, SUBLANES, LANES), F32),
+                    pltpu.VMEM((6 if chunks % 6 == 0 else 1, turns, SUBLANES, LANES), F32),
                     pltpu.VMEM((2, turns, SUBLANES, LANES), F32),
                 ],
             )(advected, above, below, coefs, cells, ranges, after)
@@ -632,51 +643,39 @@
     near = lax.all_to_all(shipped[1][0], "comp", split_axis=0, concat_axis=0, axis_index_groups=halves, tiled=True)
 
     total = total_freqs * directions
-    grown = call(
+    values = jax.ShapeDtypeStruct((half, turns, SUBLANES, slots), F32)
+    grown_near, grown_far = call(
         functools.partial(grow_kernel, directions),
-        jax.ShapeDtypeStruct((groups, turns, SUBLANES, slots), F32),
-        (20 * total * slots, 4 * total * slots),
+        [values, values],
+        LITTLE,
         in_specs=[vmem, vmem, smem],
-        out_specs=vmem,
+        out_specs=[vmem, vmem],
         scratch_shapes=[
             pltpu.VMEM((rows * chunks, SUBLANES, LANES), F32),
             pltpu.VMEM((2, SUBLANES, slots), F32),
         ],
     )(wind, cells, ranges)
 
-    arrived_spec = pl.BlockSpec((1, words * SUBLANES, LANES), lambda i: (0, 0, i))
-    half_block = (half, turns, SUBLANES, LANES)
-    sums_spec = pl.BlockSpec((SUBLANES, LANES), lambda i: (0, i))
     early, sums = call(
         functools.partial(early_kernel, half),
-        [
-            jax.ShapeDtypeStruct((half, turns, SUBLANES, slots), F32),
-            jax.ShapeDtypeStruct((SUBLANES, slots), F32),
-        ],
-        (10 * total * slots, 4 * total * slots),
-        grid=(slots // LANES,),
-        in_specs=[arrived_spec] * half + [pl.BlockSpec(half_block, lambda i: (1, 0, 0, i))],
-        out_specs=[pl.BlockSpec(half_block, lambda i: (0, 0, 0, i)), sums_spec],
-    )(*far, grown)
+        [values, jax.ShapeDtypeStruct((SUBLANES, slots), F32)],
+        MUCH,
+        in_specs=[vmem] * (half + 1),
+        out_specs=[vmem, vmem],
+    )(*far, grown_far)
 
     result = call(
         functools.partial(finish_kernel, freqs, half),
         jax.ShapeDtypeStruct((slot_count, total), jnp.bfloat16),
         (50 * total * slots, 6 * total * slots),
-        grid=(slots // LANES,),
-        in_specs=[
-            pl.BlockSpec((half, words * SUBLANES, LANES), lambda i: (0, 0, i)),
-            pl.BlockSpec(half_block, lambda i: (0, 0, 0, i)),
-            pl.BlockSpec(half_block, lambda i: (0, 0, 0, i)),
-            sums_spec,
-            smem,
+        vmem=FINISH_VMEM,
+        in_specs=[vmem] * 4 + [smem],
+        out_specs=vmem,
+        scratch_shapes=[
+            pltpu.VMEM((slots // LANES, half, turns, SUBLANES, LANES), F32),
+            pltpu.VMEM((slots // LANES, 2, total // 2, LANES), F32),
         ],
-        out_specs=pl.BlockSpec((LANES, total), lambda i: (i, 0)),
-        scratch_shapes=[
-            pltpu.VMEM(half_block, F32),
-            pltpu.VMEM((2, total // 2, LANES), F32),
-        ],
-    )(near, grown, early, sums, block_counts)
+    )(near, grown_near, early, sums, block_counts)
     return result.T
 
 

time: 83.7 us -> 68.9 us (0.82)
  the two profiles are of different devices: /device:TPU:18 before, /device:TPU:19 now
where the time goes in v4:
time: 68.9 us; the launch traced here: 68.5 us
  Pallas kernels  24.8 us (36%)
  waiting for transfers between devices  20.9 us (30%)
  starting transfers between devices  14.4 us (21%)
  local copies, waits for them, and re-layouts  8.12 us (12%)
    ppermute x4, waiting for transfers between devices, body(): lax.ppermute(part, 'comp', [(i, i ^ half + n) for i in range(groups)])  20.9 us
    pallas_call x2, Pallas kernels, body(): call(functools.partial(pack_kernel, directions, tuple(offsets)), [jax.Sha...  9.61 us
    unnamed x32, local copies, waits for them, and re-layouts  8.12 us
    pallas_call x1, Pallas kernels, body(): call(functools.partial(advect_kernel, directions, stretch), [jax.ShapeDty...  5.47 us
    all_to_all x1, starting transfers between devices, body(): lax.all_to_all(shipped[1][0], 'comp', split_axis=0, concat_axis=0, axis_i...  5.09 us
    ppermute x4, starting transfers between devices, body(): lax.ppermute(part, 'comp', [(i, i ^ half + n) for i in range(groups)])  4.79 us
    pallas_call x1, Pallas kernels, body(): call(functools.partial(finish_kernel, freqs, half), jax.ShapeDtypeStruct(...  3.99 us
    ppermute x1, starting transfers between devices, body(): below = lax.ppermute(top, 'band', [(j, i) for i, j in down])  3.26 us
  transfers between devices with their start and end apart: 7, of which 3 were waited for; matrix products, arithmetic and copies ran while one was open for 0% of the time, Pallas kernels for 21%

profile of v4, /device:TPU:19, one launch (start us, length us, event | category | flops | bytes accessed | tf_op | source)
XLA Modules:
  0.0 68.5 jit_solution(3384683353786211126)
XLA Ops:
  0.0 1.5 %copy-done = bf16[4,36,4,1440]{3,2,1,0:T(4,128)(2,1)S(1)} copy-done((bf16[4,36,4,1440]{3,2,1,0:T(4,128)(2,1)S(1)}, bf16[4,36,4,1440]{3,2,1,0:T(4,128)(2,1)}, u32[]{:S(2)}) %copy-start) | copy-done | bytes 1658904
  1.5 0.7 %copy-done.1 = s32[4,1440]{1,0:T(4,128)S(1)} copy-done((s32[4,1440]{1,0:T(4,128)S(1)}, s32[4,1440]{1,0:T(4,128)}, u32[]{:S(2)}) %copy-start.1) | copy-done | bytes 23064
  2.3 1.5 %shard_map.82 = (bf16[18,16,1536]{2,1,0:T(8,128)(2,1)S(1)}, bf16[18,16,1536]{2,1,0:T(8,128)(2,1)S(1)}) custom-call(bf16[4,2,18,4,1440]{4,3,2,1,0:T(4,128)(2,1)S(1)} %bitcast.3, s32[4,1440]{1,0:T(4,128)S(1)} %copy-done.1), custom_call_target="tpu_custom_call" | custom-call | flops 7077888 | bytes 3538944 | tf_op jit(solution)/shard_map/pallas_call | solution.py:579
  3.8 1.3 %collective-permute-start = (bf16[18,16,1536]{2,1,0:T(8,128)(2,1)S(1)}, bf16[18,16,1536]{2,1,0:T(8,128)(2,1)S(1)}, u32[]{:S(2)}, u32[]{:S(2)}) collective-permute-start(bf16[18,16,1536]{2,1,0:T(8,128)(2,1)S(1)} %get-tuple-element.20.bottom_ref), channel_id=1, source_target_pairs={{0,1},{1,2},{2,3},{4,5},{5,6},{6,7},{8,9},{9,10},{10,11},{12,13},{... | collective-permute-start | bytes 2654216 | tf_op jit(solution)/shard_map/ppermute | solution.py:592
  5.1 3.3 %collective-permute-start.1 = (bf16[18,16,1536]{2,1,0:T(8,128)(2,1)S(1)}, bf16[18,16,1536]{2,1,0:T(8,128)(2,1)S(1)}, u32[]{:S(2)}, u32[]{:S(2)}) collective-permute-start(bf16[18,16,1536]{2,1,0:T(8,128)(2,1)S(1)} %get-tuple-element.19.top_ref), channel_id=1, source_target_pairs={{1,0},{2,1},{3,2},{5,4},{6,5},{7,6},{9,8},{10,9},{11,10},{13,12},{... | collective-permute-start | bytes 2654216 | tf_op jit(solution)/shard_map/ppermute | solution.py:593
  8.4 1.7 %shard_map.84 = (s32[8,8,640]{2,1,0:T(8,128)S(1)}, s32[16,128]{1,0:T(8,128)S(1)}) custom-call(s32[4,1440]{1,0:T(4,128)S(1)} %copy-done.2, s32[1,8]{1,0:T(1,128)S(1)} %copy-done.8), custom_call_target="tpu_custom_call" | custom-call | flops 512000 | bytes 40960 | tf_op jit(solution)/shard_map/pallas_call | solution.py:596
  10.1 5.5 %shard_map.83 = (f32[18,32,1536]{2,1,0:T(8,128)S(1)}, f32[4,32,1536]{2,1,0:T(8,128)S(1)}) custom-call(bf16[18,16,1536]{2,1,0:T(8,128)(2,1)S(1)} %get-tuple-element.19.top_ref, bf16[18,16,1536]{2,1,0:T(8,128)(2,1)S(1)} %get-tuple-element.20.bottom_ref, f32[32,64]{1,0:T(8,128)S(1)} %bitcast.4, s32[4,1440]{1,0:T(4,128)S(1)} %copy-done.6, ...), custom_call_target="tpu_custom_call" | custom-call | flops 88473600 | bytes 7077888 | tf_op jit(solution)/shard_map/pallas_call | solution.py:608
  15.6 4.6 %shard_map.85 = (s32[1,80,640]{2,1,0:T(8,128)S(1)}, s32[1,80,640]{2,1,0:T(8,128)S(1)}, s32[1,80,640]{2,1,0:T(8,128)S(1)}, s32[1,80,640]{2,1,0:T(8,128)S(1)}) custom-call(f32[18,32,1536]{2,1,0:T(8,128)S(1)} %get-tuple-element.21.adv_ref, bf16[18,16,1536]{2,1,0:T(8,128)(2,1)S(1)} %collective-permute-done.above_ref, ...), custom_call_target="tpu_custom_call" | custom-call | flops 44236800 | bytes 5308416 | tf_op jit(solution)/shard_map/pallas_call | solution.py:625
  20.3 3.3 %collective-permute-start.3 = (s32[1,80,640]{2,1,0:T(8,128)S(1)}, s32[1,80,640]{2,1,0:T(8,128)S(1)}, u32[]{:S(2)}, u32[]{:S(2)}) collective-permute-start(s32[1,80,640]{2,1,0:T(8,128)S(1)} %get-tuple-element.27), channel_id=1, source_target_pairs={{0,20},{4,16},{8,28},{12,24},{16,4},{20,0},{24,12},{28,8},{1,21},{... | collective-permute-start | bytes 614408 | tf_op jit(solution)/shard_map/ppermute | solution.py:640
  23.8 1.2 %collective-permute-start.5 = (s32[1,80,640]{2,1,0:T(8,128)S(1)}, s32[1,80,640]{2,1,0:T(8,128)S(1)}, u32[]{:S(2)}, u32[]{:S(2)}) collective-permute-start(s32[1,80,640]{2,1,0:T(8,128)S(1)} %get-tuple-element.29), channel_id=1, source_target_pairs={{0,28},{4,24},{8,20},{12,16},{16,12},{20,8},{24,4},{28,0},{1,29},{... | collective-permute-start | bytes 614408 | tf_op jit(solution)/shard_map/ppermute | solution.py:640
  25.0 2.1 %shard_map.87 = (f32[4,18,8,640]{3,2,1,0:T(8,128)S(1)}, f32[4,18,8,640]{3,2,1,0:T(8,128)S(1)}) custom-call(f32[2,4,1440]{2,1,0:T(4,128)S(1)} %copy-done.3, s32[8,8,640]{2,1,0:T(8,128)S(1)} %get-tuple-element.23.cells_ref, s32[16,128]{1,0:T(8,128)S(1)} %get-tuple-element.24.ranges_ref.after_ref), custom_call_target="tpu_custom_call" | custom-call | flops 1000 | bytes 1000 | tf_op jit(solution)/shard_map/pallas_call | solution.py:647
  27.1 1.1 %copy-done.10 = f32[4,18,8,640]{3,2,1,0:T(8,128)} copy-done((f32[4,18,8,640]{3,2,1,0:T(8,128)}, f32[4,18,8,640]{3,2,1,0:T(8,128)S(1)}, u32[]{:S(2)}) %copy-start.10) | copy-done | bytes 1474584
  28.2 5.0 %shard_map.86 = s32[4,80,640]{2,1,0:T(8,128)} custom-call(f32[18,32,1536]{2,1,0:T(8,128)S(1)} %get-tuple-element.21.adv_ref, bf16[18,16,1536]{2,1,0:T(8,128)(2,1)S(1)} %collective-permute-done.above_ref, bf16[18,16,1536]{2,1,0:T(8,128)(2,1)S(1)} %collective-permute-done.1.below_ref, f32[4,32,1536]{2,1,0:T(8,128)S(1)} %get-tuple-element.22.coef_ref, ...), custom_call_target="tpu_custom_call" | custom-call | flops 1000 | bytes 1000 | tf_op jit(solution)/shard_map/pallas_call | solution.py:625
  33.2 5.1 %all-to-all-start = ((s32[4,80,640]{2,1,0:T(8,128)}), s32[4,80,640]{2,1,0:T(8,128)}, u32[]{:S(2)}, u32[]{:S(2)}) async-start(s32[4,80,640]{2,1,0:T(8,128)} %shard_map.86), calls=%async_computation | async-start | bytes 1638400 | tf_op jit(solution)/shard_map/all_to_all | solution.py:643
  38.3 6.6 %collective-permute-done.3.refs_1_ = s32[1,80,640]{2,1,0:T(8,128)S(1)} collective-permute-done((s32[1,80,640]{2,1,0:T(8,128)S(1)}, s32[1,80,640]{2,1,0:T(8,128)S(1)}, u32[]{:S(2)}, u32[]{:S(2)}) %collective-permute-start.3) | collective-permute-done | bytes 204832 | tf_op jit(solution)/shard_map/ppermute | solution.py:640
  44.9 9.7 %collective-permute-done.4.refs_2_ = s32[1,80,640]{2,1,0:T(8,128)S(1)} collective-permute-done((s32[1,80,640]{2,1,0:T(8,128)S(1)}, s32[1,80,640]{2,1,0:T(8,128)S(1)}, u32[]{:S(2)}, u32[]{:S(2)}) %collective-permute-start.4) | collective-permute-done | bytes 204832 | tf_op jit(solution)/shard_map/ppermute | solution.py:640
  54.6 0.7 copy-done.12
  55.2 4.7 %collective-permute-done.5.refs_3_ = s32[1,80,640]{2,1,0:T(8,128)S(1)} collective-permute-done((s32[1,80,640]{2,1,0:T(8,128)S(1)}, s32[1,80,640]{2,1,0:T(8,128)S(1)}, u32[]{:S(2)}, u32[]{:S(2)}) %collective-permute-start.5) | collective-permute-done | bytes 204832 | tf_op jit(solution)/shard_map/ppermute | solution.py:640
  59.9 0.7 %copy-done.14 = s32[1,80,640]{2,1,0:T(8,128)} copy-done((s32[1,80,640]{2,1,0:T(8,128)}, s32[1,80,640]{2,1,0:T(8,128)S(1)}, u32[]{:S(2)}) %copy-start.14) | copy-done | bytes 204824
  60.6 1.4 %copy-done.11 = f32[4,18,8,640]{3,2,1,0:T(8,128)S(1)} copy-done((f32[4,18,8,640]{3,2,1,0:T(8,128)S(1)}, f32[4,18,8,640]{3,2,1,0:T(8,128)}, u32[]{:S(2)}) %copy-start.11) | copy-done | bytes 1474584
  62.0 0.9 %copy-done.13 = s32[1,80,640]{2,1,0:T(8,128)S(1)} copy-done((s32[1,80,640]{2,1,0:T(8,128)S(1)}, s32[1,80,640]{2,1,0:T(8,128)}, u32[]{:S(2)}) %copy-start.13) | copy-done | bytes 204824
  62.9 0.9 %copy-done.15 = s32[1,80,640]{2,1,0:T(8,128)S(1)} copy-done((s32[1,80,640]{2,1,0:T(8,128)S(1)}, s32[1,80,640]{2,1,0:T(8,128)}, u32[]{:S(2)}) %copy-start.15) | copy-done | bytes 204824
  63.8 0.5 shard_map.88
  64.5 4.0 %shard_map.89 = bf16[630,1152]{1,0:T(8,128)(2,1)} custom-call(s32[4,80,640]{2,1,0:T(8,128)} %all-to-all-done.arrived_ref, f32[4,18,8,640]{3,2,1,0:T(8,128)S(1)} %get-tuple-element.26.grown_ref, f32[4,18,8,640]{3,2,1,0:T(8,128)S(1)} %get-tuple-element.31.early_ref, f32[8,640]{1,0:T(8,128)S(1)} %get-tuple-element.32.sums_ref, s32[1,8]{1,0:T(1,128)S(1)} %copy-done.9), custom_call_target="tpu_custom_call" | custom-call | flops 36864000 | bytes 4423680 | tf_op jit(solution)/shard_map/pallas_call | solution.py:667
  (30 shorter events, 0.5 us)
Async XLA Ops:
  0.0 8.3 %copy-start.8 = (s32[1,8]{1,0:T(1,128)S(1)}, s32[1,8]{1,0:T(1,128)}, u32[]{:S(2)}) copy-start(s32[1,8]{1,0:T(1,128)} %counts_ref.3) | copy-start | bytes 100
  0.0 1.5 %copy-start = (bf16[4,36,4,1440]{3,2,1,0:T(4,128)(2,1)S(1)}, bf16[4,36,4,1440]{3,2,1,0:T(4,128)(2,1)}, u32[]{:S(2)}) copy-start(bf16[4,36,4,1440]{3,2,1,0:T(4,128)(2,1)} %param.8) | copy-start | bytes 4976644
  1.5 0.7 %copy-start.1 = (s32[4,1440]{1,0:T(4,128)S(1)}, s32[4,1440]{1,0:T(4,128)}, u32[]{:S(2)}) copy-start(s32[4,1440]{1,0:T(4,128)} %land_ref.3) | copy-start | bytes 69124
  2.2 6.1 %copy-start.2 = (s32[4,1440]{1,0:T(4,128)S(1)}, s32[4,1440]{1,0:T(4,128)}, u32[]{:S(2)}) copy-start(s32[4,1440]{1,0:T(4,128)} %land_ref.3) | copy-start | bytes 69124
  2.2 7.8 %copy-start.4 = (f32[2,4,1440]{2,1,0:T(4,128)S(1)}, f32[2,4,1440]{2,1,0:T(4,128)}, u32[]{:S(2)}) copy-start(f32[2,4,1440]{2,1,0:T(4,128)} %current_ref.1) | copy-start | bytes 138244
  2.2 7.8 %copy-start.5 = (f32[2,4,1440]{2,1,0:T(4,128)S(1)}, f32[2,4,1440]{2,1,0:T(4,128)}, u32[]{:S(2)}) copy-start(f32[2,4,1440]{2,1,0:T(4,128)} %slope_ref.1) | copy-start | bytes 138244
  2.2 7.8 %copy-start.6 = (s32[4,1440]{1,0:T(4,128)S(1)}, s32[4,1440]{1,0:T(4,128)}, u32[]{:S(2)}) copy-start(s32[4,1440]{1,0:T(4,128)} %depth_ref.1) | copy-start | bytes 69124
  2.2 7.8 %copy-start.7 = (f32[64,32]{0,1:T(8,128)S(1)}, f32[64,32]{0,1:T(8,128)}, u32[]{:S(2)}) copy-start(f32[64,32]{0,1:T(8,128)} %param.10) | copy-start | bytes 24580
  3.8 11.8 %collective-permute-start = (bf16[18,16,1536]{2,1,0:T(8,128)(2,1)S(1)}, bf16[18,16,1536]{2,1,0:T(8,128)(2,1)S(1)}, u32[]{:S(2)}, u32[]{:S(2)}) collective-permute-start(bf16[18,16,1536]{2,1,0:T(8,128)(2,1)S(1)} %get-tuple-element.20.bottom_ref), channel_id=1, source_target_pairs={{0,1},{1,2},{2,3},{4,5},{5,6},{6,7},{8,9},{9,10},{10,11},{12,13},{... | collective-permute-start | bytes 2654216 | tf_op jit(solution)/shard_map/ppermute | solution.py:592
  5.1 10.5 %collective-permute-start.1 = (bf16[18,16,1536]{2,1,0:T(8,128)(2,1)S(1)}, bf16[18,16,1536]{2,1,0:T(8,128)(2,1)S(1)}, u32[]{:S(2)}, u32[]{:S(2)}) collective-permute-start(bf16[18,16,1536]{2,1,0:T(8,128)(2,1)S(1)} %get-tuple-element.19.top_ref), channel_id=1, source_target_pairs={{1,0},{2,1},{3,2},{5,4},{6,5},{7,6},{9,8},{10,9},{11,10},{13,12},{... | collective-permute-start | bytes 2654216 | tf_op jit(solution)/shard_map/ppermute | solution.py:593
  15.6 9.4 %copy-start.3 = (f32[2,4,1440]{2,1,0:T(4,128)S(1)}, f32[2,4,1440]{2,1,0:T(4,128)}, u32[]{:S(2)}) copy-start(f32[2,4,1440]{2,1,0:T(4,128)} %wind_ref.1) | copy-start | bytes 138244
  20.2 18.1 %collective-permute-start.2 = (s32[1,80,640]{2,1,0:T(8,128)S(1)}, s32[1,80,640]{2,1,0:T(8,128)S(1)}, u32[]{:S(2)}, u32[]{:S(2)}) collective-permute-start(s32[1,80,640]{2,1,0:T(8,128)S(1)} %get-tuple-element.25.after_ref), channel_id=1, source_target_pairs={{0,16},{4,20},{8,24},{12,28},{16,0},{20,4},{24,8},{28,12},{1,17},{... | collective-permute-start | bytes 614408 | tf_op jit(solution)/shard_map/ppermute | solution.py:640
  20.3 24.6 %collective-permute-start.3 = (s32[1,80,640]{2,1,0:T(8,128)S(1)}, s32[1,80,640]{2,1,0:T(8,128)S(1)}, u32[]{:S(2)}, u32[]{:S(2)}) collective-permute-start(s32[1,80,640]{2,1,0:T(8,128)S(1)} %get-tuple-element.27), channel_id=1, source_target_pairs={{0,20},{4,16},{8,28},{12,24},{16,4},{20,0},{24,12},{28,8},{1,21},{... | collective-permute-start | bytes 614408 | tf_op jit(solution)/shard_map/ppermute | solution.py:640
  23.6 31.0 %collective-permute-start.4 = (s32[1,80,640]{2,1,0:T(8,128)S(1)}, s32[1,80,640]{2,1,0:T(8,128)S(1)}, u32[]{:S(2)}, u32[]{:S(2)}) collective-permute-start(s32[1,80,640]{2,1,0:T(8,128)S(1)} %get-tuple-element.28), channel_id=1, source_target_pairs={{0,24},{4,28},{8,16},{12,20},{16,8},{20,12},{24,0},{28,4},{1,25},{... | collective-permute-start | bytes 614408 | tf_op jit(solution)/shard_map/ppermute | solution.py:640
  23.8 36.1 %collective-permute-start.5 = (s32[1,80,640]{2,1,0:T(8,128)S(1)}, s32[1,80,640]{2,1,0:T(8,128)S(1)}, u32[]{:S(2)}, u32[]{:S(2)}) collective-permute-start(s32[1,80,640]{2,1,0:T(8,128)S(1)} %get-tuple-element.29), channel_id=1, source_target_pairs={{0,28},{4,24},{8,20},{12,16},{16,12},{20,8},{24,4},{28,0},{1,29},{... | collective-permute-start | bytes 614408 | tf_op jit(solution)/shard_map/ppermute | solution.py:640
  27.1 1.1 %copy-start.10 = (f32[4,18,8,640]{3,2,1,0:T(8,128)}, f32[4,18,8,640]{3,2,1,0:T(8,128)S(1)}, u32[]{:S(2)}) copy-start(f32[4,18,8,640]{3,2,1,0:T(8,128)S(1)} %get-tuple-element.30.refs_4_) | copy-start | bytes 4423684
  33.2 31.1 %all-to-all-start = ((s32[4,80,640]{2,1,0:T(8,128)}), s32[4,80,640]{2,1,0:T(8,128)}, u32[]{:S(2)}, u32[]{:S(2)}) async-start(s32[4,80,640]{2,1,0:T(8,128)} %shard_map.86), calls=%async_computation | async-start | bytes 1638400 | tf_op jit(solution)/shard_map/all_to_all | solution.py:643
  54.6 0.7 copy-start.12
  59.9 0.7 %copy-start.14 = (s32[1,80,640]{2,1,0:T(8,128)}, s32[1,80,640]{2,1,0:T(8,128)S(1)}, u32[]{:S(2)}) copy-start(s32[1,80,640]{2,1,0:T(8,128)S(1)} %collective-permute-done.5.refs_3_) | copy-start | bytes 614404
  60.6 1.4 %copy-start.11 = (f32[4,18,8,640]{3,2,1,0:T(8,128)S(1)}, f32[4,18,8,640]{3,2,1,0:T(8,128)}, u32[]{:S(2)}) copy-start(f32[4,18,8,640]{3,2,1,0:T(8,128)} %copy-done.10) | copy-start | bytes 4423684
  62.0 0.9 %copy-start.13 = (s32[1,80,640]{2,1,0:T(8,128)S(1)}, s32[1,80,640]{2,1,0:T(8,128)}, u32[]{:S(2)}) copy-start(s32[1,80,640]{2,1,0:T(8,128)} %copy-done.12) | copy-start | bytes 614404
  62.9 0.9 %copy-start.15 = (s32[1,80,640]{2,1,0:T(8,128)S(1)}, s32[1,80,640]{2,1,0:T(8,128)}, u32[]{:S(2)}) copy-start(s32[1,80,640]{2,1,0:T(8,128)} %copy-done.14) | copy-start | bytes 614404
  63.8 0.7 copy-start.9

commit v5 on v4

--- a/solution.py
+++ b/solution.py
@@ -74,7 +74,7 @@
     return table
 
 
-def arrange_kernel(x_ref, land_ref, top_ref, bottom_ref, scratch):
+def arrange_kernel(x_ref, land_ref, after_ref, top_ref, bottom_ref, scratch):
     freqs, parts, step, rows, lon = x_ref.shape
     chunks = scratch.shape[1]
     tail = lon - (chunks - 1) * LANES
@@ -396,9 +396,23 @@
                     out_ref[at, n * SUBLANES : (n + 1) * SUBLANES, span] = sums[n]
 
 
-def grow_kernel(directions, wind_ref, cells_ref, ranges_ref, near_ref, far_ref, flat, slot_wind):
+def growth_rates(half, freqs, side):
+    shape = (SUBLANES, LANES)
+    freq = iota(shape, 0) // (SUBLANES // freqs)
+    step = jnp.where(side == 0, jnp.float32(1.0), jnp.float32(1.1 ** (half * freqs)))
+    rates = []
+    for source in range(half):
+        slope, threshold = jnp.zeros(shape, F32), jnp.zeros(shape, F32)
+        for f in range(freqs):
+            angular, ratio = frequency(source * freqs + f, 2 * half * freqs)
+            slope = jnp.where(freq == f, GROWTH_RATE * ratio * angular / 9.81, slope)
+            threshold = jnp.where(freq == f, GROWTH_RATE * ratio, threshold)
+        rates.append((slope * (step * step), threshold * step))
+    return rates
+
+
+def grow_kernel(directions, wind_ref, cells_ref, ranges_ref, near_ref, slot_wind, flat):
     half, turns, _, slots = near_ref.shape
-    groups = 2 * half
     rows, lon = wind_ref.shape[1:]
     chunks = flat.shape[0] // rows
     tail = lon - (chunks - 1) * LANES
@@ -407,7 +421,6 @@
     freqs = SUBLANES // parts
     shape = (SUBLANES, LANES)
     part = iota(shape, 0) % parts
-    freq = iota(shape, 0) // parts
     comp = lax.axis_index("comp")
     for r in range(rows):
         for k in range(chunks):
@@ -432,16 +445,7 @@
         slot_wind[0, :, span] = jnp.broadcast_to(found[0:1], shape)
         slot_wind[1, :, span] = jnp.broadcast_to(found[1:2], shape)
 
-    rates = []
-    for far in range(2):
-        step = jnp.where((comp // half) ^ far == 0, jnp.float32(1.0), jnp.float32(1.1 ** (half * freqs)))
-        for source in range(half):
-            slope, threshold = jnp.zeros(shape, F32), jnp.zeros(shape, F32)
-            for f in range(freqs):
-                angular, ratio = frequency(source * freqs + f, groups * freqs)
-                slope = jnp.where(freq == f, GROWTH_RATE * ratio * angular / 9.81, slope)
-                threshold = jnp.where(freq == f, GROWTH_RATE * ratio, threshold)
-            rates.append((slope * (step * step), threshold * step))
+    rates = growth_rates(half, freqs, comp // half)
 
     def one_span(m, carry):
         span = pl.ds(pl.multiple_of(m * LANES, LANES), LANES)
@@ -452,20 +456,17 @@
             for source in range(half):
                 slope, threshold = rates[source]
                 near_ref[source, j, :, span] = jnp.exp(jnp.maximum(along * slope - threshold, 0.0))
-                slope, threshold = rates[half + source]
-                far_ref[(comp % half) ^ source, j, :, span] = jnp.exp(jnp.maximum(along * slope - threshold, 0.0))
         return carry
 
     lax.fori_loop(0, spans, one_span, 0)
 
 
-def decode(arrived_refs, grown_ref, scale, span, store):
+def decode(arrived_refs, turns, scale, span, store):
     sums = [jnp.zeros((SUBLANES, LANES), F32) for _ in range(2)]
-    turns = grown_ref.shape[1]
     for source, (arrived, at) in enumerate(arrived_refs):
         for unit in range(turns // UNIT):
             words = [
-                arrived[at, n * SUBLANES : (n + 1) * SUBLANES, span]
+                arrived[(*at, slice(n * SUBLANES, (n + 1) * SUBLANES), span)]
                 for n in range(unit * WORDS, (unit + 1) * WORDS)
             ]
             rest = words[4]
@@ -484,25 +485,43 @@
                 value = coded.astype(F32) * size - offset
                 sums[n % 2] = sums[n % 2] + value * value
                 j = unit * UNIT + n
-                store(source, j, value * grown_ref[source, j, :, span])
+                store(source, j, value)
     return sums[0] + sums[1]
 
 
-def early_kernel(half, *refs):
-    arrived_refs, (grown_ref, out_ref, sums_ref) = [(ref, 0) for ref in refs[:half]], refs[half:]
-    own = lax.axis_index("comp") % half
+def early_kernel(directions, half, *refs):
+    far_refs, (wind_ref, out_ref, sums_ref, buffer, arrivals) = refs[:half], refs[half:]
+    copies = [pltpu.make_async_copy(ref, buffer.at[n], arrivals.at[n]) for n, ref in enumerate(far_refs)]
+    for copy in copies:
+        copy.start()
+    _, turns, _, slots = out_ref.shape
+    parts = directions // turns
+    part = iota((SUBLANES, LANES), 0) % parts
+    comp = lax.axis_index("comp")
+    own = comp % half
+    rates = growth_rates(half, SUBLANES // parts, (comp // half) ^ 1)
     scale = power_table(2.0**-EXPONENT_ZERO / STEP_COUNT, 1)
-    for low in range(0, out_ref.shape[-1], LANES):
-        span = slice(low, low + LANES)
+    spans = [slice(low, low + LANES) for low in range(0, slots, LANES)]
+    for span in spans:
+        east, north = wind_ref[0, :, span], wind_ref[1, :, span]
+        for j in range(turns):
+            sin, cos = signs(part, parts, turns, directions, j)
+            along = east * cos + north * sin
+            for source in range(half):
+                slope, threshold = rates[source]
+                out_ref[source, j, :, span] = jnp.exp(jnp.maximum(along * slope - threshold, 0.0))
+    for copy in copies:
+        copy.wait()
+    for span in spans:
 
         def store(source, j, value):
-            out_ref[own ^ source, j, :, span] = value
-
-        sums_ref[:, span] = decode(arrived_refs, grown_ref, scale, span, store)
+            out_ref[own ^ source, j, :, span] = value * out_ref[own ^ source, j, :, span]
+
+        sums_ref[:, span] = decode([(buffer, (n, 0)) for n in range(half)], turns, scale, span, store)
 
 
 def finish_kernel(freqs, half, arrived_ref, grown_ref, early_ref, sums_ref, counts_ref, out_ref, values, ordered):
-    arrived_refs = [(arrived_ref, n) for n in range(half)]
+    arrived_refs = [(arrived_ref, (n,)) for n in range(half)]
     groups = 2 * half
     turns = values.shape[2]
     each = turns * SUBLANES
@@ -519,9 +538,9 @@
         span = slice(m * LANES, (m + 1) * LANES)
 
         def store(source, j, value):
-            values[m, source, j] = value
-
-        sums = decode(arrived_refs, grown_ref, scale, span, store)
+            values[m, source, j] = value * grown_ref[source, j, :, span]
+
+        sums = decode(arrived_refs, turns, scale, span, store)
         mean_sq = jnp.sum(sums + sums_ref[:, span], axis=0, keepdims=True) / float(groups * each)
         strength = jnp.broadcast_to(jnp.sqrt(mean_sq + 1e-06), shape)
         occupied = (m * LANES + iota(shape, 1)) < count
@@ -537,12 +556,15 @@
                     ordered[m, side ^ far, pl.ds(source * each + j, SUBLANES, stride=turns), :] = value
         slots = slice(m * LANES, min((m + 1) * LANES, out_ref.shape[0]))
         for place in range(2):
-            turned = lax.dot_general(
-                unit_matrix,
-                ordered[m, place].astype(jnp.bfloat16),
-                (((1,), (1,)), ((), ())),
-                preferred_element_type=F32,
-            )
+            if place == 0:
+                turned = lax.dot_general(
+                    unit_matrix,
+                    ordered[m, place].astype(jnp.bfloat16),
+                    (((1,), (1,)), ((), ())),
+                    preferred_element_type=F32,
+                )
+            else:
+                turned = ordered[m, place].T
             out_ref[slots, place * half * each : (place + 1) * half * each] = turned[
                 : slots.stop - slots.start
             ].astype(jnp.bfloat16)
@@ -573,25 +595,6 @@
     smem = pl.BlockSpec(memory_space=pltpu.SMEM)
     vmem = pl.BlockSpec(memory_space=pltpu.VMEM)
 
-    step = 3
-    half = jax.ShapeDtypeStruct((turns, height // 2, padded), jnp.bfloat16)
-    half_spec = pl.BlockSpec((step, height // 2, padded), lambda i: (i, 0, 0))
-    top, bottom = call(
-        arrange_kernel,
-        [half, half],
-        (4 * hbm, 2 * hbm),
-        grid=(turns // step,),
-        in_specs=[
-            pl.BlockSpec((freqs, parts, step, rows, lon), lambda i: (0, 0, i, 0, 0)),
-            pl.BlockSpec((rows, lon), lambda i: (0, 0)),
-        ],
-        out_specs=[half_spec, half_spec],
-        scratch_shapes=[pltpu.VMEM((step, chunks, height, LANES), F32)],
-    )(spectra.reshape(freqs, parts, turns, rows, lon), land_mask)
-    down = [(i, i + 1) for i in range(bands - 1)]
-    above = lax.ppermute(bottom, "band", down)
-    below = lax.ppermute(top, "band", [(j, i) for i, j in down])
-
     range_rows = 2 * SUBLANES if groups < 2 * SUBLANES else 3 * SUBLANES
     cells, ranges = call(
         index_kernel,
@@ -604,6 +607,26 @@
         out_specs=[vmem, vmem],
         scratch_shapes=[pltpu.VMEM((rows * chunks, LANES), I32)],
     )(land_mask, block_counts)
+
+    step = 3
+    half = jax.ShapeDtypeStruct((turns, height // 2, padded), jnp.bfloat16)
+    half_spec = pl.BlockSpec((step, height // 2, padded), lambda i: (i, 0, 0))
+    top, bottom = call(
+        arrange_kernel,
+        [half, half],
+        (4 * hbm, 2 * hbm),
+        grid=(turns // step,),
+        in_specs=[
+            pl.BlockSpec((freqs, parts, step, rows, lon), lambda i: (0, 0, i, 0, 0)),
+            pl.BlockSpec((rows, lon), lambda i: (0, 0)),
+            pl.BlockSpec(memory_space=pl.ANY),
+        ],
+        out_specs=[half_spec, half_spec],
+        scratch_shapes=[pltpu.VMEM((step, chunks, height, LANES), F32)],
+    )(spectra.reshape(freqs, parts, turns, rows, lon), land_mask, ranges)
+    down = [(i, i + 1) for i in range(bands - 1)]
+    above = lax.ppermute(bottom, "band", down)
+    below = lax.ppermute(top, "band", [(j, i) for i, j in down])
 
     advected, coefs = call(
         functools.partial(advect_kernel, directions, stretch),
@@ -644,25 +667,23 @@
 
     total = total_freqs * directions
     values = jax.ShapeDtypeStruct((half, turns, SUBLANES, slots), F32)
-    grown_near, grown_far = call(
+    grown, slot_wind = call(
         functools.partial(grow_kernel, directions),
-        [values, values],
+        [values, jax.ShapeDtypeStruct((2, SUBLANES, slots), F32)],
         LITTLE,
         in_specs=[vmem, vmem, smem],
         out_specs=[vmem, vmem],
-        scratch_shapes=[
-            pltpu.VMEM((rows * chunks, SUBLANES, LANES), F32),
-            pltpu.VMEM((2, SUBLANES, slots), F32),
-        ],
+        scratch_shapes=[pltpu.VMEM((rows * chunks, SUBLANES, LANES), F32)],
     )(wind, cells, ranges)
 
     early, sums = call(
-        functools.partial(early_kernel, half),
+        functools.partial(early_kernel, directions, half),
         [values, jax.ShapeDtypeStruct((SUBLANES, slots), F32)],
         MUCH,
-        in_specs=[vmem] * (half + 1),
+        in_specs=[pl.BlockSpec(memory_space=pltpu.HBM)] * half + [vmem],
         out_specs=[vmem, vmem],
-    )(*far, grown_far)
+        scratch_shapes=[pltpu.VMEM((half, 1) + block, I32), pltpu.SemaphoreType.DMA((half,))],
+    )(*far, slot_wind)
 
     result = call(
         functools.partial(finish_kernel, freqs, half),
@@ -675,7 +696,7 @@
             pltpu.VMEM((slots // LANES, half, turns, SUBLANES, LANES), F32),
             pltpu.VMEM((slots // LANES, 2, total // 2, LANES), F32),
         ],
-    )(near, grown_near, early, sums, block_counts)
+    )(near, grown, early, sums, block_counts)
     return result.T
 
 

time: 68.9 us -> 68.8 us (level)
  the two profiles are of different devices: /device:TPU:19 before, /device:TPU:17 now
where the time goes in v5:
time: 68.8 us; the launch traced here: 68.4 us
  Pallas kernels  25.5 us (37%)
  waiting for transfers between devices  21 us (31%)
  starting transfers between devices  15.7 us (23%)
  local copies, waits for them, and re-layouts  6.09 us (9%)
    ppermute x4, waiting for transfers between devices, body(): lax.ppermute(part, 'comp', [(i, i ^ half + n) for i in range(groups)])  13.7 us
    pallas_call x2, Pallas kernels, body(): call(functools.partial(pack_kernel, directions, tuple(offsets)), [jax.Sha...  9.61 us
    unnamed x26, local copies, waits for them, and re-layouts  6.09 us
    pallas_call x1, Pallas kernels, body(): call(functools.partial(advect_kernel, directions, stretch), [jax.ShapeDty...  5.46 us
    all_to_all x1, starting transfers between devices, body(): lax.all_to_all(shipped[1][0], 'comp', split_axis=0, concat_axis=0, axis_i...  5.32 us
    ppermute x4, starting transfers between devices, body(): lax.ppermute(part, 'comp', [(i, i ^ half + n) for i in range(groups)])  4.79 us
    ppermute x1, waiting for transfers between devices, body(): below = lax.ppermute(top, 'band', [(j, i) for i, j in down])  4.69 us
    pallas_call x1, Pallas kernels, body(): call(functools.partial(finish_kernel, freqs, half), jax.ShapeDtypeStruct(...  3.9 us
  transfers between devices with their start and end apart: 7, of which 5 were waited for; matrix products, arithmetic and copies ran while one was open for 0% of the time, Pallas kernels for 20%

profile of v5, /device:TPU:17, one launch (start us, length us, event | category | flops | bytes accessed | tf_op | source)
XLA Modules:
  0.0 68.4 jit_solution(13208138588156480054)
XLA Ops:
  0.0 0.7 %copy-done.1 = s32[4,1440]{1,0:T(4,128)S(1)} copy-done((s32[4,1440]{1,0:T(4,128)S(1)}, s32[4,1440]{1,0:T(4,128)}, u32[]{:S(2)}) %copy-start.1) | copy-done | bytes 23064
  1.4 1.7 %shard_map.82 = (s32[8,8,640]{2,1,0:T(8,128)S(1)}, s32[16,128]{1,0:T(8,128)S(1)}) custom-call(s32[4,1440]{1,0:T(4,128)S(1)} %copy-done.1, s32[1,8]{1,0:T(1,128)S(1)} %copy-done.7), custom_call_target="tpu_custom_call" | custom-call | flops 512000 | bytes 40960 | tf_op jit(solution)/shard_map/pallas_call | solution.py:599
  3.1 1.5 %copy-done = bf16[4,36,4,1440]{3,2,1,0:T(4,128)(2,1)S(1)} copy-done((bf16[4,36,4,1440]{3,2,1,0:T(4,128)(2,1)S(1)}, bf16[4,36,4,1440]{3,2,1,0:T(4,128)(2,1)}, u32[]{:S(2)}) %copy-start) | copy-done | bytes 1658904
  4.5 1.5 %shard_map.83 = (bf16[18,16,1536]{2,1,0:T(8,128)(2,1)S(1)}, bf16[18,16,1536]{2,1,0:T(8,128)(2,1)S(1)}) custom-call(bf16[4,2,18,4,1440]{4,3,2,1,0:T(4,128)(2,1)S(1)} %bitcast.3, s32[4,1440]{1,0:T(4,128)S(1)} %copy-done.1, s32[16,128]{1,0:T(8,128)S(1)} %get-tuple-element.19.after_ref.ranges_ref), custom_call_target="tpu_custom_call" | custom-call | flops 7077888 | bytes 3538944 | tf_op jit(solution)/shard_map/pallas_call | solution.py:614
  6.0 3.7 %collective-permute-start = (bf16[18,16,1536]{2,1,0:T(8,128)(2,1)S(1)}, bf16[18,16,1536]{2,1,0:T(8,128)(2,1)S(1)}, u32[]{:S(2)}, u32[]{:S(2)}) collective-permute-start(bf16[18,16,1536]{2,1,0:T(8,128)(2,1)S(1)} %get-tuple-element.21.bottom_ref), channel_id=1, source_target_pairs={{0,1},{1,2},{2,3},{4,5},{5,6},{6,7},{8,9},{9,10},{10,11},{12,13},{... | collective-permute-start | bytes 2654216 | tf_op jit(solution)/shard_map/ppermute | solution.py:628
  9.7 1.9 %collective-permute-start.1 = (bf16[18,16,1536]{2,1,0:T(8,128)(2,1)S(1)}, bf16[18,16,1536]{2,1,0:T(8,128)(2,1)S(1)}, u32[]{:S(2)}, u32[]{:S(2)}) collective-permute-start(bf16[18,16,1536]{2,1,0:T(8,128)(2,1)S(1)} %get-tuple-element.20.top_ref), channel_id=1, source_target_pairs={{1,0},{2,1},{3,2},{5,4},{6,5},{7,6},{9,8},{10,9},{11,10},{13,12},{... | collective-permute-start | bytes 2654216 | tf_op jit(solution)/shard_map/ppermute | solution.py:629
  11.7 5.5 %shard_map.84 = (f32[18,32,1536]{2,1,0:T(8,128)S(1)}, f32[4,32,1536]{2,1,0:T(8,128)S(1)}) custom-call(bf16[18,16,1536]{2,1,0:T(8,128)(2,1)S(1)} %get-tuple-element.20.top_ref, bf16[18,16,1536]{2,1,0:T(8,128)(2,1)S(1)} %get-tuple-element.21.bottom_ref, f32[32,64]{1,0:T(8,128)S(1)} %bitcast.4, s32[4,1440]{1,0:T(4,128)S(1)} %copy-done.5, ...), custom_call_target="tpu_custom_call" | custom-call | flops 88473600 | bytes 7077888 | tf_op jit(solution)/shard_map/pallas_call | solution.py:631
  17.2 2.5 %collective-permute-done.above_ref = bf16[18,16,1536]{2,1,0:T(8,128)(2,1)S(1)} collective-permute-done((bf16[18,16,1536]{2,1,0:T(8,128)(2,1)S(1)}, bf16[18,16,1536]{2,1,0:T(8,128)(2,1)S(1)}, u32[]{:S(2)}, u32[]{:S(2)}) %collective-permute-start) | collective-permute-done | bytes 884768 | tf_op jit(solution)/shard_map/ppermute | solution.py:628
  19.7 4.7 %collective-permute-done.1.below_ref = bf16[18,16,1536]{2,1,0:T(8,128)(2,1)S(1)} collective-permute-done((bf16[18,16,1536]{2,1,0:T(8,128)(2,1)S(1)}, bf16[18,16,1536]{2,1,0:T(8,128)(2,1)S(1)}, u32[]{:S(2)}, u32[]{:S(2)}) %collective-permute-start.1) | collective-permute-done | bytes 884768 | tf_op jit(solution)/shard_map/ppermute | solution.py:629
  24.4 4.6 %shard_map.85 = (s32[1,80,640]{2,1,0:T(8,128)S(1)}, s32[1,80,640]{2,1,0:T(8,128)S(1)}, s32[1,80,640]{2,1,0:T(8,128)S(1)}, s32[1,80,640]{2,1,0:T(8,128)S(1)}) custom-call(f32[18,32,1536]{2,1,0:T(8,128)S(1)} %get-tuple-element.22.adv_ref, bf16[18,16,1536]{2,1,0:T(8,128)(2,1)S(1)} %collective-permute-done.above_ref, ...), custom_call_target="tpu_custom_call" | custom-call | flops 44236800 | bytes 5308416 | tf_op jit(solution)/shard_map/pallas_call | solution.py:648
  29.1 3.3 %collective-permute-start.3 = (s32[1,80,640]{2,1,0:T(8,128)S(1)}, s32[1,80,640]{2,1,0:T(8,128)S(1)}, u32[]{:S(2)}, u32[]{:S(2)}) collective-permute-start(s32[1,80,640]{2,1,0:T(8,128)S(1)} %get-tuple-element.27), channel_id=1, source_target_pairs={{0,20},{4,16},{8,28},{12,24},{16,4},{20,0},{24,12},{28,8},{1,21},{... | collective-permute-start | bytes 614408 | tf_op jit(solution)/shard_map/ppermute | solution.py:663
  32.6 1.2 %collective-permute-start.5 = (s32[1,80,640]{2,1,0:T(8,128)S(1)}, s32[1,80,640]{2,1,0:T(8,128)S(1)}, u32[]{:S(2)}, u32[]{:S(2)}) collective-permute-start(s32[1,80,640]{2,1,0:T(8,128)S(1)} %get-tuple-element.29), channel_id=1, source_target_pairs={{0,28},{4,24},{8,20},{12,16},{16,12},{20,8},{24,4},{28,0},{1,29},{... | collective-permute-start | bytes 614408 | tf_op jit(solution)/shard_map/ppermute | solution.py:663
  33.8 1.6 %shard_map.87 = (f32[4,18,8,640]{3,2,1,0:T(8,128)S(1)}, f32[2,8,640]{2,1,0:T(8,128)S(1)}) custom-call(f32[2,4,1440]{2,1,0:T(4,128)S(1)} %copy-done.2, s32[8,8,640]{2,1,0:T(8,128)S(1)} %get-tuple-element.24.cells_ref, s32[16,128]{1,0:T(8,128)S(1)} %get-tuple-element.19.after_ref.ranges_ref), custom_call_target="tpu_custom_call" | custom-call | flops 1000 | bytes 1000 | tf_op jit(solution)/shard_map/pallas_call | solution.py:670
  35.4 5.0 %shard_map.86 = s32[4,80,640]{2,1,0:T(8,128)} custom-call(f32[18,32,1536]{2,1,0:T(8,128)S(1)} %get-tuple-element.22.adv_ref, bf16[18,16,1536]{2,1,0:T(8,128)(2,1)S(1)} %collective-permute-done.above_ref, bf16[18,16,1536]{2,1,0:T(8,128)(2,1)S(1)} %collective-permute-done.1.below_ref, f32[4,32,1536]{2,1,0:T(8,128)S(1)} %get-tuple-element.23.coef_ref, ...), custom_call_target="tpu_custom_call" | custom-call | flops 1000 | bytes 1000 | tf_op jit(solution)/shard_map/pallas_call | solution.py:648
  40.4 5.3 %all-to-all-start = ((s32[4,80,640]{2,1,0:T(8,128)}), s32[4,80,640]{2,1,0:T(8,128)}, u32[]{:S(2)}, u32[]{:S(2)}) async-start(s32[4,80,640]{2,1,0:T(8,128)} %shard_map.86), calls=%async_computation | async-start | bytes 1638400 | tf_op jit(solution)/shard_map/all_to_all | solution.py:666
  45.7 4.3 %collective-permute-done.3.refs_1_ = s32[1,80,640]{2,1,0:T(8,128)S(1)} collective-permute-done((s32[1,80,640]{2,1,0:T(8,128)S(1)}, s32[1,80,640]{2,1,0:T(8,128)S(1)}, u32[]{:S(2)}, u32[]{:S(2)}) %collective-permute-start.3) | collective-permute-done | bytes 204832 | tf_op jit(solution)/shard_map/ppermute | solution.py:663
  50.0 5.1 %collective-permute-done.4.refs_2_ = s32[1,80,640]{2,1,0:T(8,128)S(1)} collective-permute-done((s32[1,80,640]{2,1,0:T(8,128)S(1)}, s32[1,80,640]{2,1,0:T(8,128)S(1)}, u32[]{:S(2)}, u32[]{:S(2)}) %collective-permute-start.4) | collective-permute-done | bytes 204832 | tf_op jit(solution)/shard_map/ppermute | solution.py:663
  55.2 0.7 copy-done.9
  55.8 4.3 %collective-permute-done.5.refs_3_ = s32[1,80,640]{2,1,0:T(8,128)S(1)} collective-permute-done((s32[1,80,640]{2,1,0:T(8,128)S(1)}, s32[1,80,640]{2,1,0:T(8,128)S(1)}, u32[]{:S(2)}, u32[]{:S(2)}) %collective-permute-start.5) | collective-permute-done | bytes 204832 | tf_op jit(solution)/shard_map/ppermute | solution.py:663
  60.1 0.7 copy-done.11
  60.8 0.9 %copy-done.10 = s32[1,80,640]{2,1,0:T(8,128)S(1)} copy-done((s32[1,80,640]{2,1,0:T(8,128)S(1)}, s32[1,80,640]{2,1,0:T(8,128)}, u32[]{:S(2)}) %copy-start.10) | copy-done | bytes 204824
  61.7 0.9 %copy-done.12 = s32[1,80,640]{2,1,0:T(8,128)S(1)} copy-done((s32[1,80,640]{2,1,0:T(8,128)S(1)}, s32[1,80,640]{2,1,0:T(8,128)}, u32[]{:S(2)}) %copy-start.12) | copy-done | bytes 204824
  62.7 1.8 %shard_map.88 = (f32[4,18,8,640]{3,2,1,0:T(8,128)S(1)}, f32[8,640]{1,0:T(8,128)S(1)}) custom-call(s32[1,80,640]{2,1,0:T(8,128)S(1)} %collective-permute-done.2.refs_0_, s32[1,80,640]{2,1,0:T(8,128)S(1)} %collective-permute-done.3.refs_1_, s32[1,80,640]{2,1,0:T(8,128)S(1)} %copy-done.10, s32[1,80,640]{2,1,0:T(8,128)S(1)} %copy-done.12, ...), custom_call_target="tpu_custom_call" | custom-call | flops 199999995904 | bytes 1000000 | tf_op jit(solution)/shard_map/pallas_call | solution.py:679
  64.5 3.9 %shard_map.89 = bf16[630,1152]{1,0:T(8,128)(2,1)} custom-call(s32[4,80,640]{2,1,0:T(8,128)} %all-to-all-done.arrived_ref, f32[4,18,8,640]{3,2,1,0:T(8,128)S(1)} %get-tuple-element.26.grown_ref, f32[4,18,8,640]{3,2,1,0:T(8,128)S(1)} %get-tuple-element.31.early_ref, f32[8,640]{1,0:T(8,128)S(1)} %get-tuple-element.32.sums_ref, s32[1,8]{1,0:T(1,128)S(1)} %copy-done.8), custom_call_target="tpu_custom_call" | custom-call | flops 36864000 | bytes 4423680 | tf_op jit(solution)/shard_map/pallas_call | solution.py:688
  (24 shorter events, 1.0 us)
Async XLA Ops:
  0.0 0.7 %copy-start.1 = (s32[4,1440]{1,0:T(4,128)S(1)}, s32[4,1440]{1,0:T(4,128)}, u32[]{:S(2)}) copy-start(s32[4,1440]{1,0:T(4,128)} %land_ref.3) | copy-start | bytes 69124
  0.7 0.7 copy-start.7
  1.4 10.3 %copy-start.5 = (s32[4,1440]{1,0:T(4,128)S(1)}, s32[4,1440]{1,0:T(4,128)}, u32[]{:S(2)}) copy-start(s32[4,1440]{1,0:T(4,128)} %depth_ref.1) | copy-start | bytes 69124
  3.1 1.5 %copy-start = (bf16[4,36,4,1440]{3,2,1,0:T(4,128)(2,1)S(1)}, bf16[4,36,4,1440]{3,2,1,0:T(4,128)(2,1)}, u32[]{:S(2)}) copy-start(bf16[4,36,4,1440]{3,2,1,0:T(4,128)(2,1)} %param.8) | copy-start | bytes 4976644
  4.5 7.1 %copy-start.3 = (f32[2,4,1440]{2,1,0:T(4,128)S(1)}, f32[2,4,1440]{2,1,0:T(4,128)}, u32[]{:S(2)}) copy-start(f32[2,4,1440]{2,1,0:T(4,128)} %current_ref.1) | copy-start | bytes 138244
  4.5 7.1 %copy-start.4 = (f32[2,4,1440]{2,1,0:T(4,128)S(1)}, f32[2,4,1440]{2,1,0:T(4,128)}, u32[]{:S(2)}) copy-start(f32[2,4,1440]{2,1,0:T(4,128)} %slope_ref.1) | copy-start | bytes 138244
  4.5 7.2 %copy-start.6 = (f32[64,32]{0,1:T(8,128)S(1)}, f32[64,32]{0,1:T(8,128)}, u32[]{:S(2)}) copy-start(f32[64,32]{0,1:T(8,128)} %param.10) | copy-start | bytes 24580
  6.0 13.7 %collective-permute-start = (bf16[18,16,1536]{2,1,0:T(8,128)(2,1)S(1)}, bf16[18,16,1536]{2,1,0:T(8,128)(2,1)S(1)}, u32[]{:S(2)}, u32[]{:S(2)}) collective-permute-start(bf16[18,16,1536]{2,1,0:T(8,128)(2,1)S(1)} %get-tuple-element.21.bottom_ref), channel_id=1, source_target_pairs={{0,1},{1,2},{2,3},{4,5},{5,6},{6,7},{8,9},{9,10},{10,11},{12,13},{... | collective-permute-start | bytes 2654216 | tf_op jit(solution)/shard_map/ppermute | solution.py:628
  9.7 14.7 %collective-permute-start.1 = (bf16[18,16,1536]{2,1,0:T(8,128)(2,1)S(1)}, bf16[18,16,1536]{2,1,0:T(8,128)(2,1)S(1)}, u32[]{:S(2)}, u32[]{:S(2)}) collective-permute-start(bf16[18,16,1536]{2,1,0:T(8,128)(2,1)S(1)} %get-tuple-element.20.top_ref), channel_id=1, source_target_pairs={{1,0},{2,1},{3,2},{5,4},{6,5},{7,6},{9,8},{10,9},{11,10},{13,12},{... | collective-permute-start | bytes 2654216 | tf_op jit(solution)/shard_map/ppermute | solution.py:629
  24.4 9.4 %copy-start.2 = (f32[2,4,1440]{2,1,0:T(4,128)S(1)}, f32[2,4,1440]{2,1,0:T(4,128)}, u32[]{:S(2)}) copy-start(f32[2,4,1440]{2,1,0:T(4,128)} %wind_ref.1) | copy-start | bytes 138244
  29.0 16.7 %collective-permute-start.2 = (s32[1,80,640]{2,1,0:T(8,128)S(1)}, s32[1,80,640]{2,1,0:T(8,128)S(1)}, u32[]{:S(2)}, u32[]{:S(2)}) collective-permute-start(s32[1,80,640]{2,1,0:T(8,128)S(1)} %get-tuple-element.25.after_ref), channel_id=1, source_target_pairs={{0,16},{4,20},{8,24},{12,28},{16,0},{20,4},{24,8},{28,12},{1,17},{... | collective-permute-start | bytes 614408 | tf_op jit(solution)/shard_map/ppermute | solution.py:663
  29.1 20.9 %collective-permute-start.3 = (s32[1,80,640]{2,1,0:T(8,128)S(1)}, s32[1,80,640]{2,1,0:T(8,128)S(1)}, u32[]{:S(2)}, u32[]{:S(2)}) collective-permute-start(s32[1,80,640]{2,1,0:T(8,128)S(1)} %get-tuple-element.27), channel_id=1, source_target_pairs={{0,20},{4,16},{8,28},{12,24},{16,4},{20,0},{24,12},{28,8},{1,21},{... | collective-permute-start | bytes 614408 | tf_op jit(solution)/shard_map/ppermute | solution.py:663
  32.4 22.8 %collective-permute-start.4 = (s32[1,80,640]{2,1,0:T(8,128)S(1)}, s32[1,80,640]{2,1,0:T(8,128)S(1)}, u32[]{:S(2)}, u32[]{:S(2)}) collective-permute-start(s32[1,80,640]{2,1,0:T(8,128)S(1)} %get-tuple-element.28), channel_id=1, source_target_pairs={{0,24},{4,28},{8,16},{12,20},{16,8},{20,12},{24,0},{28,4},{1,25},{... | collective-permute-start | bytes 614408 | tf_op jit(solution)/shard_map/ppermute | solution.py:663
  32.6 27.5 %collective-permute-start.5 = (s32[1,80,640]{2,1,0:T(8,128)S(1)}, s32[1,80,640]{2,1,0:T(8,128)S(1)}, u32[]{:S(2)}, u32[]{:S(2)}) collective-permute-start(s32[1,80,640]{2,1,0:T(8,128)S(1)} %get-tuple-element.29), channel_id=1, source_target_pairs={{0,28},{4,24},{8,20},{12,16},{16,12},{20,8},{24,4},{28,0},{1,29},{... | collective-permute-start | bytes 614408 | tf_op jit(solution)/shard_map/ppermute | solution.py:663
  40.4 24.1 %all-to-all-start = ((s32[4,80,640]{2,1,0:T(8,128)}), s32[4,80,640]{2,1,0:T(8,128)}, u32[]{:S(2)}, u32[]{:S(2)}) async-start(s32[4,80,640]{2,1,0:T(8,128)} %shard_map.86), calls=%async_computation | async-start | bytes 1638400 | tf_op jit(solution)/shard_map/all_to_all | solution.py:666
  55.2 0.7 copy-start.9
  60.1 0.7 copy-start.11
  60.8 0.9 %copy-start.10 = (s32[1,80,640]{2,1,0:T(8,128)S(1)}, s32[1,80,640]{2,1,0:T(8,128)}, u32[]{:S(2)}) copy-start(s32[1,80,640]{2,1,0:T(8,128)} %copy-done.9) | copy-start | bytes 614404
  61.7 0.9 %copy-start.12 = (s32[1,80,640]{2,1,0:T(8,128)S(1)}, s32[1,80,640]{2,1,0:T(8,128)}, u32[]{:S(2)}) copy-start(s32[1,80,640]{2,1,0:T(8,128)} %copy-done.11) | copy-start | bytes 614404
  62.7 1.8 %copy-start.8 = (s32[1,8]{1,0:T(1,128)S(1)}, s32[1,8]{1,0:T(1,128)}, u32[]{:S(2)}) copy-start(s32[1,8]{1,0:T(1,128)} %counts_ref.3) | copy-start | bytes 100

commit v6 on v5

--- a/solution.py
+++ b/solution.py
@@ -23,7 +23,7 @@
 VMEM_BYTES = 16 * 1024 * 1024
 LITTLE = (1_000, 1_000)
 MUCH = (200_000_000_000, 1_000_000)
-FINISH_VMEM = 28 * 1024 * 1024
+WHOLE_VMEM = 62_000_000
 
 F32 = jnp.float32
 I32 = jnp.int32
@@ -175,7 +175,19 @@
 
 
 def advect_kernel(
-    directions, stretch, top_ref, bottom_ref, speed_ref, depth_ref, current_ref, slope_ref, out_ref, coef_ref, scratch
+    directions,
+    stretch,
+    top_ref,
+    bottom_ref,
+    speed_ref,
+    depth_ref,
+    current_ref,
+    slope_ref,
+    out_ref,
+    coef_ref,
+    scratch,
+    along,
+    trig,
 ):
     turns, _, padded = top_ref.shape
     rows, lon = depth_ref.shape
@@ -217,48 +229,47 @@
             scratch[0, place, span] = sixth * widening
             scratch[1, place, span] = field(current_ref[0, r : r + 1, own]) * (1.0 / 6.0)
 
-    width = LANES * (4 if chunks % 4 == 0 else 1)
-
-    def window(ref, j, low, high):
-        parts = []
-        if low < LANES:
-            parts.append(ref[j, :, padded - LANES :])
-            parts.append(ref[j, :, : min(high + LANES, padded)])
-        else:
-            parts.append(ref[j, :, low - LANES : min(high + LANES, padded)])
-        if high + LANES > padded:
-            parts.append(ref[j, :, :LANES])
-        return jnp.concatenate([part.astype(F32) for part in parts], axis=1)
-
-    turn_sin, turn_cos = math.sin(2.0 * math.pi / directions), math.cos(2.0 * math.pi / directions)
-
-    def one_turn(j, carry):
-        sin, cos = carry
-        for low in range(0, padded, width):
-            high = low + width
-            centres, shifted = [], []
+    source, target = iota((3 * LANES, 2 * LANES), 0), iota((3 * LANES, 2 * LANES), 1)
+    distance = source - LANES - (target & (LANES - 1))
+    odd = target < LANES
+    weights = jnp.zeros(distance.shape, F32)
+    for at, first, second in ((-2, 0.5, 0.5), (-1, -4.0, -2.0), (0, 0.0, 3.0), (1, 4.0, -2.0), (2, -0.5, 0.5)):
+        weights = jnp.where(distance == at, jnp.where(odd, first, second), weights)
+    weights = weights.astype(jnp.bfloat16)
+    part = iota(shape, 0) % parts
+    for j in range(turns):
+        trig[0, j], trig[1, j] = signs(part, parts, turns, directions, j)
+
+    def one_chunk(k, carry):
+        span = pl.ds(pl.multiple_of(k * LANES, LANES), LANES)
+        before = pl.ds(pl.multiple_of(((k + chunks - 1) % chunks) * LANES, LANES), LANES)
+        after = pl.ds(pl.multiple_of(((k + 1) % chunks) * LANES, LANES), LANES)
+        for n, ref in enumerate((top_ref, bottom_ref)):
+            wide = jnp.concatenate([ref[:, :, before], ref[:, :, span], ref[:, :, after]], axis=2)
+            wide = wide.reshape(turns * 2 * SUBLANES, 3 * LANES)
+            product = jnp.dot(wide, weights, preferred_element_type=F32)
+            along[n] = product.reshape(turns, 2 * SUBLANES, 2 * LANES)
+        places = [slice(r * SUBLANES, (r + 1) * SUBLANES) for r in range(rows)]
+        sixths = [coef_ref[0, place, span] for place in places]
+        currents_y = [coef_ref[1, place, span] for place in places]
+        widened = [scratch[0, place, span] for place in places]
+        currents_x = [scratch[1, place, span] for place in places]
+        for j in range(turns):
+            sin, cos = trig[0, j], trig[1, j]
+            centres = []
             for ref in (top_ref, bottom_ref):
-                wide = window(ref, j, low, high)
-                moved = [
-                    pltpu.roll(wide, shift % wide.shape[1], axis=1)[:, LANES : LANES + width] for shift in (2, 1, -1, -2)
-                ]
-                for half in (slice(0, SUBLANES), slice(SUBLANES, 2 * SUBLANES)):
-                    centres.append(wide[half, LANES : LANES + width])
-                    shifted.append([one[half] for one in moved])
+                pair = ref[j, :, span].astype(F32)
+                centres += [pair[:SUBLANES], pair[SUBLANES:]]
             for r in range(rows):
-                place = slice(r * SUBLANES, (r + 1) * SUBLANES)
-                span = slice(low, high)
-                speed_x = scratch[0, place, span] * cos + scratch[1, place, span]
-                speed_y = coef_ref[0, place, span] * sin + coef_ref[1, place, span]
+                at = slice((r % 2) * SUBLANES, (r % 2 + 1) * SUBLANES)
+                speed_x = widened[r] * cos + currents_x[r]
+                moved = speed_x * along[r // 2, j, at, :LANES] + jnp.abs(speed_x) * along[r // 2, j, at, LANES:]
+                speed_y = sixths[r] * sin + currents_y[r]
                 near = [centres[n] if 0 <= n < rows else 0.0 for n in range(r - 2, r + 3)]
-                far_behind, behind, ahead, far_ahead = shifted[r]
-                along = upwind(speed_x, far_behind, behind, centres[r], ahead, far_ahead)
-                across = upwind(speed_y, *near)
-                out_ref[j, place, span] = centres[r] - along - across
-        return sin * turn_cos + cos * turn_sin, cos * turn_cos - sin * turn_sin
-
-    part = iota((SUBLANES, 1), 0) % parts
-    lax.fori_loop(0, turns, one_turn, signs(part, parts, turns, directions, 0))
+                out_ref[j, places[r], span] = centres[r] - moved - upwind(speed_y, *near)
+        return carry
+
+    lax.fori_loop(0, chunks, one_chunk, 0)
 
 
 def pack_kernel(directions, offsets, adv_ref, above_ref, below_ref, coef_ref, cells_ref, ranges_ref, after_ref, *refs):
@@ -411,7 +422,7 @@
     return rates
 
 
-def grow_kernel(directions, wind_ref, cells_ref, ranges_ref, near_ref, slot_wind, flat):
+def grow_kernel(directions, wind_ref, cells_ref, ranges_ref, after_ref, near_ref, far_ref, flat, slot_wind):
     half, turns, _, slots = near_ref.shape
     rows, lon = wind_ref.shape[1:]
     chunks = flat.shape[0] // rows
@@ -445,7 +456,7 @@
         slot_wind[0, :, span] = jnp.broadcast_to(found[0:1], shape)
         slot_wind[1, :, span] = jnp.broadcast_to(found[1:2], shape)
 
-    rates = growth_rates(half, freqs, comp // half)
+    rates = growth_rates(half, freqs, comp // half) + growth_rates(half, freqs, (comp // half) ^ 1)
 
     def one_span(m, carry):
         span = pl.ds(pl.multiple_of(m * LANES, LANES), LANES)
@@ -456,17 +467,19 @@
             for source in range(half):
                 slope, threshold = rates[source]
                 near_ref[source, j, :, span] = jnp.exp(jnp.maximum(along * slope - threshold, 0.0))
+                slope, threshold = rates[half + source]
+                far_ref[(comp % half) ^ source, j, :, span] = jnp.exp(jnp.maximum(along * slope - threshold, 0.0))
         return carry
 
     lax.fori_loop(0, spans, one_span, 0)
 
 
-def decode(arrived_refs, turns, scale, span, store):
+def decode(arrived, half, turns, scale, span, store):
     sums = [jnp.zeros((SUBLANES, LANES), F32) for _ in range(2)]
-    for source, (arrived, at) in enumerate(arrived_refs):
+    for source in range(half):
         for unit in range(turns // UNIT):
             words = [
-                arrived[(*at, slice(n * SUBLANES, (n + 1) * SUBLANES), span)]
+                arrived[source, n * SUBLANES : (n + 1) * SUBLANES, span]
                 for n in range(unit * WORDS, (unit + 1) * WORDS)
             ]
             rest = words[4]
@@ -489,59 +502,49 @@
     return sums[0] + sums[1]
 
 
-def early_kernel(directions, half, *refs):
-    far_refs, (wind_ref, out_ref, sums_ref, buffer, arrivals) = refs[:half], refs[half:]
-    copies = [pltpu.make_async_copy(ref, buffer.at[n], arrivals.at[n]) for n, ref in enumerate(far_refs)]
-    for copy in copies:
-        copy.start()
-    _, turns, _, slots = out_ref.shape
-    parts = directions // turns
-    part = iota((SUBLANES, LANES), 0) % parts
-    comp = lax.axis_index("comp")
-    own = comp % half
-    rates = growth_rates(half, SUBLANES // parts, (comp // half) ^ 1)
-    scale = power_table(2.0**-EXPONENT_ZERO / STEP_COUNT, 1)
-    spans = [slice(low, low + LANES) for low in range(0, slots, LANES)]
-    for span in spans:
-        east, north = wind_ref[0, :, span], wind_ref[1, :, span]
-        for j in range(turns):
-            sin, cos = signs(part, parts, turns, directions, j)
-            along = east * cos + north * sin
-            for source in range(half):
-                slope, threshold = rates[source]
-                out_ref[source, j, :, span] = jnp.exp(jnp.maximum(along * slope - threshold, 0.0))
-    for copy in copies:
-        copy.wait()
-    for span in spans:
-
-        def store(source, j, value):
-            out_ref[own ^ source, j, :, span] = value * out_ref[own ^ source, j, :, span]
-
-        sums_ref[:, span] = decode([(buffer, (n, 0)) for n in range(half)], turns, scale, span, store)
-
-
-def finish_kernel(freqs, half, arrived_ref, grown_ref, early_ref, sums_ref, counts_ref, out_ref, values, ordered):
-    arrived_refs = [(arrived_ref, (n,)) for n in range(half)]
+def gate_kernel(*refs):
+    refs[-1][...] = jnp.zeros(refs[-1].shape, F32)
+
+
+def finish_kernel(freqs, half, *refs):
+    far_refs, refs = refs[:half], refs[half:]
+    near_ref, grown_near_ref, grown_far_ref, _, counts_ref, out_ref = refs[:6]
+    far_words, near_words, near_values, far_values, ordered, arrivals = refs[6:]
     groups = 2 * half
-    turns = values.shape[2]
+    turns = near_values.shape[1]
     each = turns * SUBLANES
     shape = (SUBLANES, LANES)
     comp = lax.axis_index("comp")
-    side = comp // half
+    side, own = comp // half, comp % half
     count = counts_ref[0, comp]
+    spans = [slice(low, low + LANES) for low in range(0, near_values.shape[-1], LANES)]
+    copies = []
+    for m, span in enumerate(spans):
+        pairs = [(ref.at[0, :, span], far_words.at[n, :, span]) for n, ref in enumerate(far_refs)]
+        pairs.append((near_ref.at[:, :, span], near_words.at[:, :, span]))
+        pairs.append((grown_far_ref.at[:, :, :, span], far_values.at[:, :, :, span]))
+        pairs.append((grown_near_ref.at[:, :, :, span], near_values.at[:, :, :, span]))
+        copies.append([pltpu.make_async_copy(*pair, arrivals.at[m, n]) for n, pair in enumerate(pairs)])
+        for copy in copies[-1]:
+            copy.start()
     scale = power_table(2.0**-EXPONENT_ZERO / STEP_COUNT, 1)
     freq = iota(shape, 0) // (SUBLANES // freqs)
     square = (LANES, LANES)
     unit_matrix = (iota(square, 0) == iota(square, 1)).astype(jnp.bfloat16)
     steps = [jnp.where(side ^ far == 0, jnp.float32(1.0), jnp.float32(1.1 ** (half * freqs))) for far in range(2)]
-    for m in range(values.shape[0]):
-        span = slice(m * LANES, (m + 1) * LANES)
-
-        def store(source, j, value):
-            values[m, source, j] = value * grown_ref[source, j, :, span]
-
-        sums = decode(arrived_refs, turns, scale, span, store)
-        mean_sq = jnp.sum(sums + sums_ref[:, span], axis=0, keepdims=True) / float(groups * each)
+    for m, span in enumerate(spans):
+        for copy in copies[m]:
+            copy.wait()
+
+        def store_far(source, j, value):
+            far_values[source, j, :, span] = value * far_values[source, j, :, span]
+
+        def store_near(source, j, value):
+            near_values[source, j, :, span] = value * near_values[source, j, :, span]
+
+        sums = decode(far_words, half, turns, scale, span, store_far)
+        sums = sums + decode(near_words, half, turns, scale, span, store_near)
+        mean_sq = jnp.sum(sums, axis=0, keepdims=True) / float(groups * each)
         strength = jnp.broadcast_to(jnp.sqrt(mean_sq + 1e-06), shape)
         occupied = (m * LANES + iota(shape, 1)) < count
         for far in range(2):
@@ -551,7 +554,7 @@
                     rate = jnp.where(freq == f, DAMPING * frequency(source * freqs + f, groups * freqs)[1], rate)
                 factor = jnp.exp(-(rate * steps[far] * strength))
                 for j in range(turns):
-                    value = early_ref[source, j, :, span] if far else values[m, source, j]
+                    value = far_values[own ^ source, j, :, span] if far else near_values[source, j, :, span]
                     value = jnp.where(occupied, value * factor, 0.0)
                     ordered[m, side ^ far, pl.ds(source * each + j, SUBLANES, stride=turns), :] = value
         slots = slice(m * LANES, min((m + 1) * LANES, out_ref.shape[0]))
@@ -594,6 +597,7 @@
     stretch = [float(value) for value in 1.0 / np.cos(latitude)]
     smem = pl.BlockSpec(memory_space=pltpu.SMEM)
     vmem = pl.BlockSpec(memory_space=pltpu.VMEM)
+    anywhere = pl.BlockSpec(memory_space=pl.ANY)
 
     range_rows = 2 * SUBLANES if groups < 2 * SUBLANES else 3 * SUBLANES
     cells, ranges = call(
@@ -602,7 +606,7 @@
             jax.ShapeDtypeStruct((groups, SUBLANES, slots), I32),
             jax.ShapeDtypeStruct((range_rows, LANES), I32),
         ],
-        (100 * groups * slots, 8 * groups * slots),
+        (400_000 * groups * slots, 8 * groups * slots),
         in_specs=[vmem, smem],
         out_specs=[vmem, vmem],
         scratch_shapes=[pltpu.VMEM((rows * chunks, LANES), I32)],
@@ -619,7 +623,7 @@
         in_specs=[
             pl.BlockSpec((freqs, parts, step, rows, lon), lambda i: (0, 0, i, 0, 0)),
             pl.BlockSpec((rows, lon), lambda i: (0, 0)),
-            pl.BlockSpec(memory_space=pl.ANY),
+            anywhere,
         ],
         out_specs=[half_spec, half_spec],
         scratch_shapes=[pltpu.VMEM((step, chunks, height, LANES), F32)],
@@ -637,7 +641,11 @@
         (50 * hbm, 4 * hbm),
         in_specs=[vmem] * 6,
         out_specs=[vmem, vmem],
-        scratch_shapes=[pltpu.VMEM((2, height, padded), F32)],
+        scratch_shapes=[
+            pltpu.VMEM((2, height, padded), F32),
+            pltpu.VMEM((rows // 2, turns, 2 * SUBLANES, 2 * LANES), F32),
+            pltpu.VMEM((2, turns, SUBLANES, LANES), F32),
+        ],
     )(top, bottom, group_speed.T, depth_class, current, depth_slope)
 
     half = groups // 2
@@ -649,7 +657,7 @@
                 functools.partial(pack_kernel, directions, tuple(offsets)),
                 [jax.ShapeDtypeStruct(shape, I32) for shape in outputs],
                 (25 * hbm, 3 * hbm) if len(outputs) > 1 else LITTLE,
-                in_specs=[vmem] * 5 + [smem, pl.BlockSpec(memory_space=pl.ANY)],
+                in_specs=[vmem] * 5 + [smem, anywhere],
                 out_specs=[vmem] * len(outputs),
                 scratch_shapes=[
                     pltpu.VMEM((rows * chunks, words, SUBLANES, LANES), I32),
@@ -667,36 +675,44 @@
 
     total = total_freqs * directions
     values = jax.ShapeDtypeStruct((half, turns, SUBLANES, slots), F32)
-    grown, slot_wind = call(
+    grown_near, grown_far = call(
         functools.partial(grow_kernel, directions),
-        [values, jax.ShapeDtypeStruct((2, SUBLANES, slots), F32)],
+        [values, values],
         LITTLE,
-        in_specs=[vmem, vmem, smem],
+        vmem=WHOLE_VMEM,
+        in_specs=[vmem, vmem, smem, anywhere],
         out_specs=[vmem, vmem],
-        scratch_shapes=[pltpu.VMEM((rows * chunks, SUBLANES, LANES), F32)],
-    )(wind, cells, ranges)
-
-    early, sums = call(
-        functools.partial(early_kernel, directions, half),
-        [values, jax.ShapeDtypeStruct((SUBLANES, slots), F32)],
+        scratch_shapes=[
+            pltpu.VMEM((rows * chunks, SUBLANES, LANES), F32),
+            pltpu.VMEM((2, SUBLANES, slots), F32),
+        ],
+    )(wind, cells, ranges, shipped[1][0])
+
+    gate = call(
+        gate_kernel,
+        jax.ShapeDtypeStruct((SUBLANES, LANES), F32),
         MUCH,
-        in_specs=[pl.BlockSpec(memory_space=pltpu.HBM)] * half + [vmem],
-        out_specs=[vmem, vmem],
-        scratch_shapes=[pltpu.VMEM((half, 1) + block, I32), pltpu.SemaphoreType.DMA((half,))],
-    )(*far, slot_wind)
+        vmem=WHOLE_VMEM,
+        in_specs=[anywhere] * half,
+        out_specs=vmem,
+    )(*far)
 
     result = call(
         functools.partial(finish_kernel, freqs, half),
         jax.ShapeDtypeStruct((slot_count, total), jnp.bfloat16),
         (50 * total * slots, 6 * total * slots),
-        vmem=FINISH_VMEM,
-        in_specs=[vmem] * 4 + [smem],
+        vmem=WHOLE_VMEM,
+        in_specs=[anywhere] * (half + 4) + [smem],
         out_specs=vmem,
         scratch_shapes=[
-            pltpu.VMEM((slots // LANES, half, turns, SUBLANES, LANES), F32),
+            pltpu.VMEM((half,) + block, I32),
+            pltpu.VMEM((half,) + block, I32),
+            pltpu.VMEM((half, turns, SUBLANES, slots), F32),
+            pltpu.VMEM((half, turns, SUBLANES, slots), F32),
             pltpu.VMEM((slots // LANES, 2, total // 2, LANES), F32),
+            pltpu.SemaphoreType.DMA((slots // LANES, half + 3)),
         ],
-    )(near, grown, early, sums, block_counts)
+    )(*far, near, grown_near, grown_far, gate, block_counts)
     return result.T
 
 

time: 68.8 us -> 67.6 us (0.983)
  the two profiles are of different devices: /device:TPU:17 before, /device:TPU:1 now
where the time goes in v6:
time: 67.6 us; the launch traced here: 67.4 us
  Pallas kernels  28.5 us (42%)
  waiting for transfers between devices  19.7 us (29%)
  starting transfers between devices  16.7 us (25%)
  local copies, waits for them, and re-layouts  2.23 us (3%)
    ppermute x4, waiting for transfers between devices, body(): lax.ppermute(part, 'comp', [(i, i ^ half + n) for i in range(groups)])  14.9 us
    pallas_call x2, Pallas kernels, body(): call(functools.partial(pack_kernel, directions, tuple(offsets)), [jax.Sha...  9.61 us
    ppermute x4, starting transfers between devices, body(): lax.ppermute(part, 'comp', [(i, i ^ half + n) for i in range(groups)])  6.02 us
    pallas_call x1, Pallas kernels, body(): call(functools.partial(finish_kernel, freqs, half), jax.ShapeDtypeStruct(...  6.01 us
    pallas_call x1, Pallas kernels, body(): call(functools.partial(advect_kernel, directions, stretch), [jax.ShapeDty...  5.13 us
    ppermute x1, starting transfers between devices, body(): above = lax.ppermute(bottom, 'band', down)  4.47 us
    all_to_all x1, starting transfers between devices, body(): lax.all_to_all(shipped[1][0], 'comp', split_axis=0, concat_axis=0, axis_i...  4.2 us
    pallas_call x1, Pallas kernels, body(): call(functools.partial(grow_kernel, directions), [values, values], LITTLE...  3.96 us
  transfers between devices with their start and end apart: 7, of which 4 were waited for; matrix products, arithmetic and copies ran while one was open for 0% of the time, Pallas kernels for 22%

profile of v6, /device:TPU:1, one launch (start us, length us, event | category | flops | bytes accessed | tf_op | source)
XLA Modules:
  0.0 67.4 jit_solution(15008773716041161562)
XLA Ops:
  0.0 0.9 %copy-done.5 = s32[4,1440]{1,0:T(4,128)S(1)} copy-done((s32[4,1440]{1,0:T(4,128)S(1)}, s32[4,1440]{1,0:T(4,128)}, u32[]{:S(2)}) %copy-start.5) | copy-done | bytes 23064
  0.9 0.7 copy-done.8
  1.5 1.7 %shard_map.82 = (s32[8,8,640]{2,1,0:T(8,128)S(1)}, s32[16,128]{1,0:T(8,128)S(1)}) custom-call(s32[4,1440]{1,0:T(4,128)S(1)} %copy-done.5, s32[1,8]{1,0:T(1,128)S(1)} %copy-done.8), custom_call_target="tpu_custom_call" | custom-call | flops 2048000000 | bytes 40960 | tf_op jit(solution)/shard_map/pallas_call | solution.py:603
  3.2 0.0 copy-start.3
  3.2 0.0 copy-start.4
  3.2 0.0 copy-start.6
  3.3 1.5 %shard_map.83 = (bf16[18,16,1536]{2,1,0:T(8,128)(2,1)S(1)}, bf16[18,16,1536]{2,1,0:T(8,128)(2,1)S(1)}) custom-call(bf16[4,2,18,4,1440]{4,3,2,1,0:T(4,128)(2,1)S(1)} %bitcast.3, s32[4,1440]{1,0:T(4,128)S(1)} %copy-done.5, s32[16,128]{1,0:T(8,128)S(1)} %get-tuple-element.17.after_ref.ranges_ref), custom_call_target="tpu_custom_call" | custom-call | flops 7077888 | bytes 3538944 | tf_op jit(solution)/shard_map/pallas_call | solution.py:618
  4.8 2.0 %collective-permute-start.1 = (bf16[18,16,1536]{2,1,0:T(8,128)(2,1)S(1)}, bf16[18,16,1536]{2,1,0:T(8,128)(2,1)S(1)}, u32[]{:S(2)}, u32[]{:S(2)}) collective-permute-start(bf16[18,16,1536]{2,1,0:T(8,128)(2,1)S(1)} %get-tuple-element.18.top_ref), channel_id=1, source_target_pairs={{1,0},{2,1},{3,2},{5,4},{6,5},{7,6},{9,8},{10,9},{11,10},{13,12},{... | collective-permute-start | bytes 2654216 | tf_op jit(solution)/shard_map/ppermute | solution.py:633
  6.8 4.5 %collective-permute-start = (bf16[18,16,1536]{2,1,0:T(8,128)(2,1)S(1)}, bf16[18,16,1536]{2,1,0:T(8,128)(2,1)S(1)}, u32[]{:S(2)}, u32[]{:S(2)}) collective-permute-start(bf16[18,16,1536]{2,1,0:T(8,128)(2,1)S(1)} %get-tuple-element.19.bottom_ref), channel_id=1, source_target_pairs={{0,1},{1,2},{2,3},{4,5},{5,6},{6,7},{8,9},{9,10},{10,11},{12,13},{... | collective-permute-start | bytes 2654216 | tf_op jit(solution)/shard_map/ppermute | solution.py:632
  11.3 5.1 %shard_map.84 = (f32[18,32,1536]{2,1,0:T(8,128)S(1)}, f32[4,32,1536]{2,1,0:T(8,128)S(1)}) custom-call(bf16[18,16,1536]{2,1,0:T(8,128)(2,1)S(1)} %get-tuple-element.18.top_ref, bf16[18,16,1536]{2,1,0:T(8,128)(2,1)S(1)} %get-tuple-element.19.bottom_ref, f32[32,64]{1,0:T(8,128)S(1)} %bitcast.4, s32[4,1440]{1,0:T(4,128)S(1)} %copy-done.6, ...), custom_call_target="tpu_custom_call" | custom-call | flops 88473600 | bytes 7077888 | tf_op jit(solution)/shard_map/pallas_call | solution.py:635
  16.4 3.6 %collective-permute-done.1.below_ref = bf16[18,16,1536]{2,1,0:T(8,128)(2,1)S(1)} collective-permute-done((bf16[18,16,1536]{2,1,0:T(8,128)(2,1)S(1)}, bf16[18,16,1536]{2,1,0:T(8,128)(2,1)S(1)}, u32[]{:S(2)}, u32[]{:S(2)}) %collective-permute-start.1) | collective-permute-done | bytes 884768 | tf_op jit(solution)/shard_map/ppermute | solution.py:633
  20.0 1.2 %collective-permute-done.above_ref = bf16[18,16,1536]{2,1,0:T(8,128)(2,1)S(1)} collective-permute-done((bf16[18,16,1536]{2,1,0:T(8,128)(2,1)S(1)}, bf16[18,16,1536]{2,1,0:T(8,128)(2,1)S(1)}, u32[]{:S(2)}, u32[]{:S(2)}) %collective-permute-start) | collective-permute-done | bytes 884768 | tf_op jit(solution)/shard_map/ppermute | solution.py:632
  21.2 4.6 %shard_map.85 = (s32[1,80,640]{2,1,0:T(8,128)S(1)}, s32[1,80,640]{2,1,0:T(8,128)S(1)}, s32[1,80,640]{2,1,0:T(8,128)S(1)}, s32[1,80,640]{2,1,0:T(8,128)S(1)}) custom-call(f32[18,32,1536]{2,1,0:T(8,128)S(1)} %get-tuple-element.20.adv_ref, bf16[18,16,1536]{2,1,0:T(8,128)(2,1)S(1)} %collective-permute-done.above_ref, ...), custom_call_target="tpu_custom_call" | custom-call | flops 44236800 | bytes 5308416 | tf_op jit(solution)/shard_map/pallas_call | solution.py:656
  25.8 2.8 %collective-permute-start.3 = (s32[1,80,640]{2,1,0:T(8,128)S(1)}, s32[1,80,640]{2,1,0:T(8,128)S(1)}, u32[]{:S(2)}, u32[]{:S(2)}) collective-permute-start(s32[1,80,640]{2,1,0:T(8,128)S(1)} %get-tuple-element.24), channel_id=1, source_target_pairs={{0,20},{4,16},{8,28},{12,24},{16,4},{20,0},{24,12},{28,8},{1,21},{... | collective-permute-start | bytes 614408 | tf_op jit(solution)/shard_map/ppermute | solution.py:671
  28.6 1.6 %collective-permute-start.4 = (s32[1,80,640]{2,1,0:T(8,128)S(1)}, s32[1,80,640]{2,1,0:T(8,128)S(1)}, u32[]{:S(2)}, u32[]{:S(2)}) collective-permute-start(s32[1,80,640]{2,1,0:T(8,128)S(1)} %get-tuple-element.25), channel_id=1, source_target_pairs={{0,24},{4,28},{8,16},{12,20},{16,8},{20,12},{24,0},{28,4},{1,25},{... | collective-permute-start | bytes 614408 | tf_op jit(solution)/shard_map/ppermute | solution.py:671
  30.2 1.6 %collective-permute-start.5 = (s32[1,80,640]{2,1,0:T(8,128)S(1)}, s32[1,80,640]{2,1,0:T(8,128)S(1)}, u32[]{:S(2)}, u32[]{:S(2)}) collective-permute-start(s32[1,80,640]{2,1,0:T(8,128)S(1)} %get-tuple-element.26), channel_id=1, source_target_pairs={{0,28},{4,24},{8,20},{12,16},{16,12},{20,8},{24,4},{28,0},{1,29},{... | collective-permute-start | bytes 614408 | tf_op jit(solution)/shard_map/ppermute | solution.py:671
  31.9 5.0 %shard_map.86.after_ref = s32[4,80,640]{2,1,0:T(8,128)} custom-call(f32[18,32,1536]{2,1,0:T(8,128)S(1)} %get-tuple-element.20.adv_ref, bf16[18,16,1536]{2,1,0:T(8,128)(2,1)S(1)} %collective-permute-done.above_ref, bf16[18,16,1536]{2,1,0:T(8,128)(2,1)S(1)} %collective-permute-done.1.below_ref, f32[4,32,1536]{2,1,0:T(8,128)S(1)} %get-tuple-element.21.coef_ref, ...), custom_call_target="tpu_custom_call" | custom-call | flops 1000 | bytes 1000 | tf_op jit(solution)/shard_map/pallas_call | solution.py:656
  36.8 4.2 %all-to-all-start = ((s32[4,80,640]{2,1,0:T(8,128)}), s32[4,80,640]{2,1,0:T(8,128)}, u32[]{:S(2)}, u32[]{:S(2)}) async-start(s32[4,80,640]{2,1,0:T(8,128)} %shard_map.86.after_ref), calls=%async_computation | async-start | bytes 1638400 | tf_op jit(solution)/shard_map/all_to_all | solution.py:674
  41.1 4.0 %shard_map.87 = (f32[4,18,8,640]{3,2,1,0:T(8,128)}, f32[4,18,8,640]{3,2,1,0:T(8,128)}) custom-call(f32[2,4,1440]{2,1,0:T(4,128)} %wind_ref.1, s32[8,8,640]{2,1,0:T(8,128)} %copy-done.1, s32[16,128]{1,0:T(8,128)} %copy-done.2, s32[4,80,640]{2,1,0:T(8,128)} %shard_map.86.after_ref), custom_call_target="tpu_custom_call" | custom-call | flops 1000 | bytes 1000 | tf_op jit(solution)/shard_map/pallas_call | solution.py:678
  45.0 3.6 %collective-permute-done.3.refs_1_ = s32[1,80,640]{2,1,0:T(8,128)S(1)} collective-permute-done((s32[1,80,640]{2,1,0:T(8,128)S(1)}, s32[1,80,640]{2,1,0:T(8,128)S(1)}, u32[]{:S(2)}, u32[]{:S(2)}) %collective-permute-start.3) | collective-permute-done | bytes 204832 | tf_op jit(solution)/shard_map/ppermute | solution.py:671
  48.7 11.3 %collective-permute-done.2.refs_0_ = s32[1,80,640]{2,1,0:T(8,128)S(1)} collective-permute-done((s32[1,80,640]{2,1,0:T(8,128)S(1)}, s32[1,80,640]{2,1,0:T(8,128)S(1)}, u32[]{:S(2)}, u32[]{:S(2)}) %collective-permute-start.2) | collective-permute-done | bytes 204832 | tf_op jit(solution)/shard_map/ppermute | solution.py:671
  59.9 0.7 copy-done.12
  60.6 0.6 shard_map.88.refs_7_
  61.2 6.0 %shard_map.89 = bf16[630,1152]{1,0:T(8,128)(2,1)} custom-call(s32[1,80,640]{2,1,0:T(8,128)} %copy-done.12, s32[1,80,640]{2,1,0:T(8,128)} %copy-done.9, s32[1,80,640]{2,1,0:T(8,128)} %copy-done.10, s32[1,80,640]{2,1,0:T(8,128)} %copy-done.11, s32[4,80,640]{2,1,0:T(8,128)} %all-to-all-done.refs_4_, f32[4,18,8,640]{3,2,1,0:T(8,128)} %get-tuple-element.27.refs_5_, ...), custom_call_target="tpu_custom_call" | custom-call | flops 36864000 | bytes 4423680 | tf_op jit(solution)/shard_map/pallas_call | solution.py:700
  (24 shorter events, 0.1 us)
Async XLA Ops:
  0.0 3.3 %copy-start = (bf16[4,36,4,1440]{3,2,1,0:T(4,128)(2,1)S(1)}, bf16[4,36,4,1440]{3,2,1,0:T(4,128)(2,1)}, u32[]{:S(2)}) copy-start(bf16[4,36,4,1440]{3,2,1,0:T(4,128)(2,1)} %param.8) | copy-start | bytes 4976644
  0.0 0.9 %copy-start.5 = (s32[4,1440]{1,0:T(4,128)S(1)}, s32[4,1440]{1,0:T(4,128)}, u32[]{:S(2)}) copy-start(s32[4,1440]{1,0:T(4,128)} %land_ref.3) | copy-start | bytes 69124
  0.9 0.7 copy-start.8
  3.2 28.6 %copy-start.1 = (s32[8,8,640]{2,1,0:T(8,128)}, s32[8,8,640]{2,1,0:T(8,128)S(1)}, u32[]{:S(2)}) copy-start(s32[8,8,640]{2,1,0:T(8,128)S(1)} %get-tuple-element.22.cells_ref) | copy-start | bytes 491524
  3.2 28.6 %copy-start.2 = (s32[16,128]{1,0:T(8,128)}, s32[16,128]{1,0:T(8,128)S(1)}, u32[]{:S(2)}) copy-start(s32[16,128]{1,0:T(8,128)S(1)} %get-tuple-element.17.after_ref.ranges_ref) | copy-start | bytes 24580
  3.2 8.0 %copy-start.3 = (f32[2,4,1440]{2,1,0:T(4,128)S(1)}, f32[2,4,1440]{2,1,0:T(4,128)}, u32[]{:S(2)}) copy-start(f32[2,4,1440]{2,1,0:T(4,128)} %current_ref.1) | copy-start | bytes 138244
  3.2 8.0 %copy-start.4 = (f32[2,4,1440]{2,1,0:T(4,128)S(1)}, f32[2,4,1440]{2,1,0:T(4,128)}, u32[]{:S(2)}) copy-start(f32[2,4,1440]{2,1,0:T(4,128)} %slope_ref.1) | copy-start | bytes 138244
  3.2 8.0 %copy-start.6 = (s32[4,1440]{1,0:T(4,128)S(1)}, s32[4,1440]{1,0:T(4,128)}, u32[]{:S(2)}) copy-start(s32[4,1440]{1,0:T(4,128)} %depth_ref.1) | copy-start | bytes 69124
  3.3 8.0 %copy-start.7 = (f32[64,32]{0,1:T(8,128)S(1)}, f32[64,32]{0,1:T(8,128)}, u32[]{:S(2)}) copy-start(f32[64,32]{0,1:T(8,128)} %param.10) | copy-start | bytes 24580
  4.8 15.2 %collective-permute-start.1 = (bf16[18,16,1536]{2,1,0:T(8,128)(2,1)S(1)}, bf16[18,16,1536]{2,1,0:T(8,128)(2,1)S(1)}, u32[]{:S(2)}, u32[]{:S(2)}) collective-permute-start(bf16[18,16,1536]{2,1,0:T(8,128)(2,1)S(1)} %get-tuple-element.18.top_ref), channel_id=1, source_target_pairs={{1,0},{2,1},{3,2},{5,4},{6,5},{7,6},{9,8},{10,9},{11,10},{13,12},{... | collective-permute-start | bytes 2654216 | tf_op jit(solution)/shard_map/ppermute | solution.py:633
  6.8 14.4 %collective-permute-start = (bf16[18,16,1536]{2,1,0:T(8,128)(2,1)S(1)}, bf16[18,16,1536]{2,1,0:T(8,128)(2,1)S(1)}, u32[]{:S(2)}, u32[]{:S(2)}) collective-permute-start(bf16[18,16,1536]{2,1,0:T(8,128)(2,1)S(1)} %get-tuple-element.19.bottom_ref), channel_id=1, source_target_pairs={{0,1},{1,2},{2,3},{4,5},{5,6},{6,7},{8,9},{9,10},{10,11},{12,13},{... | collective-permute-start | bytes 2654216 | tf_op jit(solution)/shard_map/ppermute | solution.py:632
  25.8 22.8 %collective-permute-start.3 = (s32[1,80,640]{2,1,0:T(8,128)S(1)}, s32[1,80,640]{2,1,0:T(8,128)S(1)}, u32[]{:S(2)}, u32[]{:S(2)}) collective-permute-start(s32[1,80,640]{2,1,0:T(8,128)S(1)} %get-tuple-element.24), channel_id=1, source_target_pairs={{0,20},{4,16},{8,28},{12,24},{16,4},{20,0},{24,12},{28,8},{1,21},{... | collective-permute-start | bytes 614408 | tf_op jit(solution)/shard_map/ppermute | solution.py:671
  28.6 20.0 %collective-permute-start.4 = (s32[1,80,640]{2,1,0:T(8,128)S(1)}, s32[1,80,640]{2,1,0:T(8,128)S(1)}, u32[]{:S(2)}, u32[]{:S(2)}) collective-permute-start(s32[1,80,640]{2,1,0:T(8,128)S(1)} %get-tuple-element.25), channel_id=1, source_target_pairs={{0,24},{4,28},{8,16},{12,20},{16,8},{20,12},{24,0},{28,4},{1,25},{... | collective-permute-start | bytes 614408 | tf_op jit(solution)/shard_map/ppermute | solution.py:671
  30.2 18.4 %collective-permute-start.5 = (s32[1,80,640]{2,1,0:T(8,128)S(1)}, s32[1,80,640]{2,1,0:T(8,128)S(1)}, u32[]{:S(2)}, u32[]{:S(2)}) collective-permute-start(s32[1,80,640]{2,1,0:T(8,128)S(1)} %get-tuple-element.26), channel_id=1, source_target_pairs={{0,28},{4,24},{8,20},{12,16},{16,12},{20,8},{24,4},{28,0},{1,29},{... | collective-permute-start | bytes 614408 | tf_op jit(solution)/shard_map/ppermute | solution.py:671
  31.8 28.1 %collective-permute-start.2 = (s32[1,80,640]{2,1,0:T(8,128)S(1)}, s32[1,80,640]{2,1,0:T(8,128)S(1)}, u32[]{:S(2)}, u32[]{:S(2)}) collective-permute-start(s32[1,80,640]{2,1,0:T(8,128)S(1)} %get-tuple-element.23.after_ref), channel_id=1, source_target_pairs={{0,16},{4,20},{8,24},{12,28},{16,0},{20,4},{24,8},{28,12},{1,17},{... | collective-permute-start | bytes 614408 | tf_op jit(solution)/shard_map/ppermute | solution.py:671
  36.8 24.4 %all-to-all-start = ((s32[4,80,640]{2,1,0:T(8,128)}), s32[4,80,640]{2,1,0:T(8,128)}, u32[]{:S(2)}, u32[]{:S(2)}) async-start(s32[4,80,640]{2,1,0:T(8,128)} %shard_map.86.after_ref), calls=%async_computation | async-start | bytes 1638400 | tf_op jit(solution)/shard_map/all_to_all | solution.py:674
  48.6 11.3 %copy-start.9 = (s32[1,80,640]{2,1,0:T(8,128)}, s32[1,80,640]{2,1,0:T(8,128)S(1)}, u32[]{:S(2)}) copy-start(s32[1,80,640]{2,1,0:T(8,128)S(1)} %collective-permute-done.3.refs_1_) | copy-start | bytes 614404
  48.6 11.3 %copy-start.10 = (s32[1,80,640]{2,1,0:T(8,128)}, s32[1,80,640]{2,1,0:T(8,128)S(1)}, u32[]{:S(2)}) copy-start(s32[1,80,640]{2,1,0:T(8,128)S(1)} %collective-permute-done.4.refs_2_) | copy-start | bytes 614404
  48.7 11.3 %copy-start.11 = (s32[1,80,640]{2,1,0:T(8,128)}, s32[1,80,640]{2,1,0:T(8,128)S(1)}, u32[]{:S(2)}) copy-start(s32[1,80,640]{2,1,0:T(8,128)S(1)} %collective-permute-done.5.refs_3_) | copy-start | bytes 614404
  59.9 0.7 copy-start.12

commit v7 on v6

--- a/solution.py
+++ b/solution.py
@@ -115,9 +115,9 @@
             bottom_ref[j, :, span] = piece[2 * SUBLANES :]
 
 
-def index_kernel(land_ref, counts_ref, cells_ref, ranges_ref, flat):
+def index_kernel(land_ref, cells_ref, ranges_ref, flat):
     chunks = flat.shape[0]
-    rows, lon = land_ref.shape
+    rows, lon = land_ref.shape[0] - 1, land_ref.shape[1]
     per_row = chunks // rows
     tail = lon - (per_row - 1) * LANES
     flat[...] = jnp.ones(flat.shape, I32)
@@ -142,10 +142,10 @@
     chunk_ids = iota((chunks, slots), 0)
     slot_ids = iota((1, slots), 1)
     span_lane = iota((1, LANES), 1)
-    start = jnp.int32(0)
+    start = jnp.zeros((1, 1), I32)
     longest = jnp.zeros((1, 1), F32)
     for c in range(groups):
-        count = counts_ref[0, c]
+        count = land_ref[rows : rows + 1, c : c + 1]
         number = (slot_ids + start).astype(F32)
         passed = (through_column <= number).astype(F32)
         chunk_of = jnp.sum(passed, axis=0, keepdims=True)
@@ -240,15 +240,25 @@
     for j in range(turns):
         trig[0, j], trig[1, j] = signs(part, parts, turns, directions, j)
 
-    def one_chunk(k, carry):
-        span = pl.ds(pl.multiple_of(k * LANES, LANES), LANES)
-        before = pl.ds(pl.multiple_of(((k + chunks - 1) % chunks) * LANES, LANES), LANES)
-        after = pl.ds(pl.multiple_of(((k + 1) % chunks) * LANES, LANES), LANES)
-        for n, ref in enumerate((top_ref, bottom_ref)):
-            wide = jnp.concatenate([ref[:, :, before], ref[:, :, span], ref[:, :, after]], axis=2)
-            wide = wide.reshape(turns * 2 * SUBLANES, 3 * LANES)
-            product = jnp.dot(wide, weights, preferred_element_type=F32)
-            along[n] = product.reshape(turns, 2 * SUBLANES, 2 * LANES)
+    together = along.shape[0]
+
+    def lanes(k):
+        return pl.ds(pl.multiple_of(k * LANES, LANES), LANES)
+
+    def some_chunks(i, carry):
+        for at in range(together):
+            k = i * together + at
+            before, span, after = lanes((k + chunks - 1) % chunks), lanes(k), lanes((k + 1) % chunks)
+            for n, ref in enumerate((top_ref, bottom_ref)):
+                wide = jnp.concatenate([ref[:, :, before], ref[:, :, span], ref[:, :, after]], axis=2)
+                wide = wide.reshape(turns * 2 * SUBLANES, 3 * LANES)
+                product = jnp.dot(wide, weights, preferred_element_type=F32)
+                along[at, n] = product.reshape(turns, 2 * SUBLANES, 2 * LANES)
+        for at in range(together):
+            one_chunk(lanes(i * together + at), at)
+        return carry
+
+    def one_chunk(span, at):
         places = [slice(r * SUBLANES, (r + 1) * SUBLANES) for r in range(rows)]
         sixths = [coef_ref[0, place, span] for place in places]
         currents_y = [coef_ref[1, place, span] for place in places]
@@ -261,15 +271,15 @@
                 pair = ref[j, :, span].astype(F32)
                 centres += [pair[:SUBLANES], pair[SUBLANES:]]
             for r in range(rows):
-                at = slice((r % 2) * SUBLANES, (r % 2 + 1) * SUBLANES)
+                row = slice((r % 2) * SUBLANES, (r % 2 + 1) * SUBLANES)
+                odd, even = along[at, r // 2, j, row, :LANES], along[at, r // 2, j, row, LANES:]
                 speed_x = widened[r] * cos + currents_x[r]
-                moved = speed_x * along[r // 2, j, at, :LANES] + jnp.abs(speed_x) * along[r // 2, j, at, LANES:]
+                moved = speed_x * odd + jnp.abs(speed_x) * even
                 speed_y = sixths[r] * sin + currents_y[r]
                 near = [centres[n] if 0 <= n < rows else 0.0 for n in range(r - 2, r + 3)]
                 out_ref[j, places[r], span] = centres[r] - moved - upwind(speed_y, *near)
-        return carry
-
-    lax.fori_loop(0, chunks, one_chunk, 0)
+
+    lax.fori_loop(0, chunks // together, some_chunks, 0)
 
 
 def pack_kernel(directions, offsets, adv_ref, above_ref, below_ref, coef_ref, cells_ref, ranges_ref, after_ref, *refs):
@@ -509,7 +519,7 @@
 def finish_kernel(freqs, half, *refs):
     far_refs, refs = refs[:half], refs[half:]
     near_ref, grown_near_ref, grown_far_ref, _, counts_ref, out_ref = refs[:6]
-    far_words, near_words, near_values, far_values, ordered, arrivals = refs[6:]
+    far_words, near_words, near_values, far_values, ordered, orders, arrivals = refs[6:]
     groups = 2 * half
     turns = near_values.shape[1]
     each = turns * SUBLANES
@@ -529,8 +539,18 @@
             copy.start()
     scale = power_table(2.0**-EXPONENT_ZERO / STEP_COUNT, 1)
     freq = iota(shape, 0) // (SUBLANES // freqs)
-    square = (LANES, LANES)
-    unit_matrix = (iota(square, 0) == iota(square, 1)).astype(jnp.bfloat16)
+    total = groups * each
+    reach = orders.shape[1]
+    firsts = []
+    for n in range(total // LANES):
+        first = min((n * LANES // each) * each // LANES * LANES, total - reach)
+        firsts.append(first)
+        target = iota((1, LANES), 1) + n * LANES
+        source = sum((target >= each * b).astype(I32) for b in range(1, groups))
+        rest = target - source * each
+        sublane = sum((rest >= turns * b).astype(I32) for b in range(1, SUBLANES))
+        origin = source * each + (rest - sublane * turns) * SUBLANES + sublane - first
+        orders[n] = (iota((reach, LANES), 0) == origin).astype(F32).astype(jnp.bfloat16)
     steps = [jnp.where(side ^ far == 0, jnp.float32(1.0), jnp.float32(1.1 ** (half * freqs))) for far in range(2)]
     for m, span in enumerate(spans):
         for copy in copies[m]:
@@ -556,21 +576,12 @@
                 for j in range(turns):
                     value = far_values[own ^ source, j, :, span] if far else near_values[source, j, :, span]
                     value = jnp.where(occupied, value * factor, 0.0)
-                    ordered[m, side ^ far, pl.ds(source * each + j, SUBLANES, stride=turns), :] = value
+                    ordered[m, side ^ far, source * each + j * SUBLANES : source * each + (j + 1) * SUBLANES, :] = value
         slots = slice(m * LANES, min((m + 1) * LANES, out_ref.shape[0]))
-        for place in range(2):
-            if place == 0:
-                turned = lax.dot_general(
-                    unit_matrix,
-                    ordered[m, place].astype(jnp.bfloat16),
-                    (((1,), (1,)), ((), ())),
-                    preferred_element_type=F32,
-                )
-            else:
-                turned = ordered[m, place].T
-            out_ref[slots, place * half * each : (place + 1) * half * each] = turned[
-                : slots.stop - slots.start
-            ].astype(jnp.bfloat16)
+        turned = jnp.concatenate([ordered[m, place].T for place in range(2)], axis=1).astype(jnp.bfloat16)
+        for n, first in enumerate(firsts):
+            block = jnp.dot(turned[:, first : first + reach], orders[n], preferred_element_type=F32)
+            out_ref[slots, n * LANES : (n + 1) * LANES] = block[: slots.stop - slots.start].astype(jnp.bfloat16)
 
 
 def frequency(index, count):
@@ -607,10 +618,10 @@
             jax.ShapeDtypeStruct((range_rows, LANES), I32),
         ],
         (400_000 * groups * slots, 8 * groups * slots),
-        in_specs=[vmem, smem],
+        in_specs=[vmem],
         out_specs=[vmem, vmem],
         scratch_shapes=[pltpu.VMEM((rows * chunks, LANES), I32)],
-    )(land_mask, block_counts)
+    )(jnp.concatenate([land_mask, jnp.pad(block_counts, ((0, 0), (0, lon - groups)))]))
 
     step = 3
     half = jax.ShapeDtypeStruct((turns, height // 2, padded), jnp.bfloat16)
@@ -643,7 +654,7 @@
         out_specs=[vmem, vmem],
         scratch_shapes=[
             pltpu.VMEM((2, height, padded), F32),
-            pltpu.VMEM((rows // 2, turns, 2 * SUBLANES, 2 * LANES), F32),
+            pltpu.VMEM((3 if chunks % 3 == 0 else 1, rows // 2, turns, 2 * SUBLANES, 2 * LANES), F32),
             pltpu.VMEM((2, turns, SUBLANES, LANES), F32),
         ],
     )(top, bottom, group_speed.T, depth_class, current, depth_slope)
@@ -710,6 +721,7 @@
             pltpu.VMEM((half, turns, SUBLANES, slots), F32),
             pltpu.VMEM((half, turns, SUBLANES, slots), F32),
             pltpu.VMEM((slots // LANES, 2, total // 2, LANES), F32),
+            pltpu.VMEM((total // LANES, 3 * LANES, LANES), jnp.bfloat16),
             pltpu.SemaphoreType.DMA((slots // LANES, half + 3)),
         ],
     )(*far, near, grown_near, grown_far, gate, block_counts)

time: 67.6 us -> 67.4 us (level)
  local copies, waits for them, and re-layouts: 2.23 us -> 0.84 us
  waiting for transfers between devices: 19.7 us -> 18.5 us
  starting transfers between devices: 16.7 us -> 17.7 us
  other arithmetic: 0 us -> 0.76 us
    ppermute x4, waiting for transfers between devices: 14.9 us -> 12.4 us  [body(): lax.ppermute(part, 'comp', [(i, i ^ half + n) for i in range(groups)])]
    pallas_call x1, Pallas kernels: 6.01 us -> 7.77 us  [body(): call(functools.partial(finish_kernel, freqs, half), jax.ShapeDtypeStruct(...]
    unnamed x26 -> x24, local copies, waits for them, and re-layouts: 2.23 us -> 0.84 us
    ppermute x1, waiting for transfers between devices: 3.61 us -> 4.96 us  [body(): below = lax.ppermute(top, 'band', [(j, i) for i, j in down])]
    pallas_call x1, Pallas kernels: 5.13 us -> 3.77 us  [body(): call(functools.partial(advect_kernel, directions, stretch), [jax.ShapeDty...]
    ppermute x4, starting transfers between devices: 6.02 us -> 7.06 us  [body(): lax.ppermute(part, 'comp', [(i, i ^ half + n) for i in range(groups)])]
    concatenate x0 -> x1, other arithmetic: none -> 0.76 us  [body(): jnp.concatenate([land_mask, jnp.pad(block_counts, ((0, 0), (0, lon - grou...]
  transfers between devices with their start and end apart: 7 -> 7, of which waited for: 4 -> 4; matrix products, arithmetic and copies ran while one was open for 0% -> 0% of each run, Pallas kernels for 22% -> 21%
where the time goes in v7:
time: 67.4 us; the launch traced here: 66.8 us
  Pallas kernels  28.6 us (42%)
  waiting for transfers between devices  18.5 us (27%)
  starting transfers between devices  17.7 us (26%)
  local copies, waits for them, and re-layouts  0.84 us (1%)
  other arithmetic  0.76 us (1%)
    ppermute x4, waiting for transfers between devices, body(): lax.ppermute(part, 'comp', [(i, i ^ half + n) for i in range(groups)])  12.4 us
    pallas_call x2, Pallas kernels, body(): call(functools.partial(pack_kernel, directions, tuple(offsets)), [jax.Sha...  9.6 us
    pallas_call x1, Pallas kernels, body(): call(functools.partial(finish_kernel, freqs, half), jax.ShapeDtypeStruct(...  7.77 us
    ppermute x4, starting transfers between devices, body(): lax.ppermute(part, 'comp', [(i, i ^ half + n) for i in range(groups)])  7.06 us
    ppermute x1, waiting for transfers between devices, body(): below = lax.ppermute(top, 'band', [(j, i) for i, j in down])  4.96 us
    ppermute x1, starting transfers between devices, body(): above = lax.ppermute(bottom, 'band', down)  4.46 us
    all_to_all x1, starting transfers between devices, body(): lax.all_to_all(shipped[1][0], 'comp', split_axis=0, concat_axis=0, axis_i...  4.21 us
    pallas_call x1, Pallas kernels, body(): call(functools.partial(grow_kernel, directions), [values, values], LITTLE...  4.11 us
  transfers between devices with their start and end apart: 7, of which 4 were waited for; matrix products, arithmetic and copies ran while one was open for 0% of the time, Pallas kernels for 21%

profile of v7, /device:TPU:1, one launch (start us, length us, event | category | flops | bytes accessed | tf_op | source)
XLA Modules:
  0.0 66.8 jit_solution(10198902201855305142)
XLA Ops:
  0.0 0.8 %pad_add_fusion.land_ref = s32[5,1440]{1,0:T(8,128)S(1)} fusion(s32[1,8]{1,0:T(1,128)} %refs_8_.1, s32[4,1440]{1,0:T(4,128)} %land_ref.1), kind=kLoop, calls=%fused_computation | loop fusion | flops 7200 | bytes 51872 | tf_op jit(solution)/shard_map/concatenate | solution.py:624
  0.8 1.3 %shard_map.82 = (s32[8,8,640]{2,1,0:T(8,128)S(1)}, s32[16,128]{1,0:T(8,128)S(1)}) custom-call(s32[5,1440]{1,0:T(8,128)S(1)} %pad_add_fusion.land_ref), custom_call_target="tpu_custom_call" | custom-call | flops 2048000000 | bytes 40960 | tf_op jit(solution)/shard_map/pallas_call | solution.py:614
  2.1 0.0 copy-start.4
  2.1 0.0 copy-start.5
  2.1 0.0 copy-start.7
  2.1 0.1 copy-done
  2.2 1.5 %shard_map.83 = (bf16[18,16,1536]{2,1,0:T(8,128)(2,1)S(1)}, bf16[18,16,1536]{2,1,0:T(8,128)(2,1)S(1)}) custom-call(bf16[4,2,18,4,1440]{4,3,2,1,0:T(4,128)(2,1)S(1)} %bitcast.3, s32[4,1440]{1,0:T(4,128)S(1)} %copy-done.3, s32[16,128]{1,0:T(8,128)S(1)} %get-tuple-element.17.after_ref.ranges_ref), custom_call_target="tpu_custom_call" | custom-call | flops 7077888 | bytes 3538944 | tf_op jit(solution)/shard_map/pallas_call | solution.py:629
  3.7 2.0 %collective-permute-start.1 = (bf16[18,16,1536]{2,1,0:T(8,128)(2,1)S(1)}, bf16[18,16,1536]{2,1,0:T(8,128)(2,1)S(1)}, u32[]{:S(2)}, u32[]{:S(2)}) collective-permute-start(bf16[18,16,1536]{2,1,0:T(8,128)(2,1)S(1)} %get-tuple-element.18.top_ref), channel_id=1, source_target_pairs={{1,0},{2,1},{3,2},{5,4},{6,5},{7,6},{9,8},{10,9},{11,10},{13,12},{... | collective-permute-start | bytes 2654216 | tf_op jit(solution)/shard_map/ppermute | solution.py:644
  5.7 4.5 %collective-permute-start = (bf16[18,16,1536]{2,1,0:T(8,128)(2,1)S(1)}, bf16[18,16,1536]{2,1,0:T(8,128)(2,1)S(1)}, u32[]{:S(2)}, u32[]{:S(2)}) collective-permute-start(bf16[18,16,1536]{2,1,0:T(8,128)(2,1)S(1)} %get-tuple-element.19.bottom_ref), channel_id=1, source_target_pairs={{0,1},{1,2},{2,3},{4,5},{5,6},{6,7},{8,9},{9,10},{10,11},{12,13},{... | collective-permute-start | bytes 2654216 | tf_op jit(solution)/shard_map/ppermute | solution.py:643
  10.2 3.8 %shard_map.84 = (f32[18,32,1536]{2,1,0:T(8,128)S(1)}, f32[4,32,1536]{2,1,0:T(8,128)S(1)}) custom-call(bf16[18,16,1536]{2,1,0:T(8,128)(2,1)S(1)} %get-tuple-element.18.top_ref, bf16[18,16,1536]{2,1,0:T(8,128)(2,1)S(1)} %get-tuple-element.19.bottom_ref, f32[32,64]{1,0:T(8,128)S(1)} %bitcast.4, s32[4,1440]{1,0:T(4,128)S(1)} %copy-done.6, ...), custom_call_target="tpu_custom_call" | custom-call | flops 88473600 | bytes 7077888 | tf_op jit(solution)/shard_map/pallas_call | solution.py:646
  14.0 5.0 %collective-permute-done.1.below_ref = bf16[18,16,1536]{2,1,0:T(8,128)(2,1)S(1)} collective-permute-done((bf16[18,16,1536]{2,1,0:T(8,128)(2,1)S(1)}, bf16[18,16,1536]{2,1,0:T(8,128)(2,1)S(1)}, u32[]{:S(2)}, u32[]{:S(2)}) %collective-permute-start.1) | collective-permute-done | bytes 884768 | tf_op jit(solution)/shard_map/ppermute | solution.py:644
  19.0 1.2 %collective-permute-done.above_ref = bf16[18,16,1536]{2,1,0:T(8,128)(2,1)S(1)} collective-permute-done((bf16[18,16,1536]{2,1,0:T(8,128)(2,1)S(1)}, bf16[18,16,1536]{2,1,0:T(8,128)(2,1)S(1)}, u32[]{:S(2)}, u32[]{:S(2)}) %collective-permute-start) | collective-permute-done | bytes 884768 | tf_op jit(solution)/shard_map/ppermute | solution.py:643
  20.2 4.1 %shard_map.85 = (s32[1,80,640]{2,1,0:T(8,128)S(1)}, s32[1,80,640]{2,1,0:T(8,128)S(1)}, s32[1,80,640]{2,1,0:T(8,128)S(1)}, s32[1,80,640]{2,1,0:T(8,128)S(1)}) custom-call(f32[18,32,1536]{2,1,0:T(8,128)S(1)} %get-tuple-element.20.adv_ref, bf16[18,16,1536]{2,1,0:T(8,128)(2,1)S(1)} %collective-permute-done.above_ref, ...), custom_call_target="tpu_custom_call" | custom-call | flops 44236800 | bytes 5308416 | tf_op jit(solution)/shard_map/pallas_call | solution.py:667
  24.3 3.8 %collective-permute-start.3 = (s32[1,80,640]{2,1,0:T(8,128)S(1)}, s32[1,80,640]{2,1,0:T(8,128)S(1)}, u32[]{:S(2)}, u32[]{:S(2)}) collective-permute-start(s32[1,80,640]{2,1,0:T(8,128)S(1)} %get-tuple-element.24), channel_id=1, source_target_pairs={{0,20},{4,16},{8,28},{12,24},{16,4},{20,0},{24,12},{28,8},{1,21},{... | collective-permute-start | bytes 614408 | tf_op jit(solution)/shard_map/ppermute | solution.py:682
  28.1 0.6 collective-permute-start.4
  28.7 2.7 %collective-permute-start.5 = (s32[1,80,640]{2,1,0:T(8,128)S(1)}, s32[1,80,640]{2,1,0:T(8,128)S(1)}, u32[]{:S(2)}, u32[]{:S(2)}) collective-permute-start(s32[1,80,640]{2,1,0:T(8,128)S(1)} %get-tuple-element.26), channel_id=1, source_target_pairs={{0,28},{4,24},{8,20},{12,16},{16,12},{20,8},{24,4},{28,0},{1,29},{... | collective-permute-start | bytes 614408 | tf_op jit(solution)/shard_map/ppermute | solution.py:682
  31.3 5.5 %shard_map.86.after_ref = s32[4,80,640]{2,1,0:T(8,128)} custom-call(f32[18,32,1536]{2,1,0:T(8,128)S(1)} %get-tuple-element.20.adv_ref, bf16[18,16,1536]{2,1,0:T(8,128)(2,1)S(1)} %collective-permute-done.above_ref, bf16[18,16,1536]{2,1,0:T(8,128)(2,1)S(1)} %collective-permute-done.1.below_ref, f32[4,32,1536]{2,1,0:T(8,128)S(1)} %get-tuple-element.21.coef_ref, ...), custom_call_target="tpu_custom_call" | custom-call | flops 1000 | bytes 1000 | tf_op jit(solution)/shard_map/pallas_call | solution.py:667
  36.8 4.2 %all-to-all-start = ((s32[4,80,640]{2,1,0:T(8,128)}), s32[4,80,640]{2,1,0:T(8,128)}, u32[]{:S(2)}, u32[]{:S(2)}) async-start(s32[4,80,640]{2,1,0:T(8,128)} %shard_map.86.after_ref), calls=%async_computation | async-start | bytes 1638400 | tf_op jit(solution)/shard_map/all_to_all | solution.py:685
  41.1 4.1 %shard_map.87 = (f32[4,18,8,640]{3,2,1,0:T(8,128)}, f32[4,18,8,640]{3,2,1,0:T(8,128)}) custom-call(f32[2,4,1440]{2,1,0:T(4,128)} %wind_ref.1, s32[8,8,640]{2,1,0:T(8,128)} %copy-done.1, s32[16,128]{1,0:T(8,128)} %copy-done.2, s32[4,80,640]{2,1,0:T(8,128)} %shard_map.86.after_ref), custom_call_target="tpu_custom_call" | custom-call | flops 1000 | bytes 1000 | tf_op jit(solution)/shard_map/pallas_call | solution.py:689
  45.2 1.1 %collective-permute-done.3.refs_1_ = s32[1,80,640]{2,1,0:T(8,128)S(1)} collective-permute-done((s32[1,80,640]{2,1,0:T(8,128)S(1)}, s32[1,80,640]{2,1,0:T(8,128)S(1)}, u32[]{:S(2)}, u32[]{:S(2)}) %collective-permute-start.3) | collective-permute-done | bytes 204832 | tf_op jit(solution)/shard_map/ppermute | solution.py:682
  46.3 11.3 %collective-permute-done.2.refs_0_ = s32[1,80,640]{2,1,0:T(8,128)S(1)} collective-permute-done((s32[1,80,640]{2,1,0:T(8,128)S(1)}, s32[1,80,640]{2,1,0:T(8,128)S(1)}, u32[]{:S(2)}, u32[]{:S(2)}) %collective-permute-start.2) | collective-permute-done | bytes 204832 | tf_op jit(solution)/shard_map/ppermute | solution.py:682
  57.6 0.7 copy-done.11
  58.2 0.6 shard_map.88.refs_7_
  58.8 7.8 %shard_map.89 = bf16[630,1152]{1,0:T(8,128)(2,1)} custom-call(s32[1,80,640]{2,1,0:T(8,128)} %copy-done.11, s32[1,80,640]{2,1,0:T(8,128)} %copy-done.8, s32[1,80,640]{2,1,0:T(8,128)} %copy-done.9, s32[1,80,640]{2,1,0:T(8,128)} %copy-done.10, s32[4,80,640]{2,1,0:T(8,128)} %all-to-all-done.refs_4_, f32[4,18,8,640]{3,2,1,0:T(8,128)} %get-tuple-element.27.refs_5_, ...), custom_call_target="tpu_custom_call" | custom-call | flops 36864000 | bytes 4423680 | tf_op jit(solution)/shard_map/pallas_call | solution.py:711
  (23 shorter events, 0.1 us)
Async XLA Ops:
  0.8 1.5 %copy-start = (bf16[4,36,4,1440]{3,2,1,0:T(4,128)(2,1)S(1)}, bf16[4,36,4,1440]{3,2,1,0:T(4,128)(2,1)}, u32[]{:S(2)}) copy-start(bf16[4,36,4,1440]{3,2,1,0:T(4,128)(2,1)} %param.8) | copy-start | bytes 4976644
  0.8 1.5 %copy-start.3 = (s32[4,1440]{1,0:T(4,128)S(1)}, s32[4,1440]{1,0:T(4,128)}, u32[]{:S(2)}) copy-start(s32[4,1440]{1,0:T(4,128)} %land_ref.1) | copy-start | bytes 69124
  2.0 29.3 %copy-start.1 = (s32[8,8,640]{2,1,0:T(8,128)}, s32[8,8,640]{2,1,0:T(8,128)S(1)}, u32[]{:S(2)}) copy-start(s32[8,8,640]{2,1,0:T(8,128)S(1)} %get-tuple-element.22.cells_ref) | copy-start | bytes 491524
  2.1 29.3 %copy-start.2 = (s32[16,128]{1,0:T(8,128)}, s32[16,128]{1,0:T(8,128)S(1)}, u32[]{:S(2)}) copy-start(s32[16,128]{1,0:T(8,128)S(1)} %get-tuple-element.17.after_ref.ranges_ref) | copy-start | bytes 24580
  2.1 8.1 %copy-start.4 = (f32[2,4,1440]{2,1,0:T(4,128)S(1)}, f32[2,4,1440]{2,1,0:T(4,128)}, u32[]{:S(2)}) copy-start(f32[2,4,1440]{2,1,0:T(4,128)} %current_ref.1) | copy-start | bytes 138244
  2.1 8.1 %copy-start.5 = (f32[2,4,1440]{2,1,0:T(4,128)S(1)}, f32[2,4,1440]{2,1,0:T(4,128)}, u32[]{:S(2)}) copy-start(f32[2,4,1440]{2,1,0:T(4,128)} %slope_ref.1) | copy-start | bytes 138244
  2.1 8.1 %copy-start.6 = (s32[4,1440]{1,0:T(4,128)S(1)}, s32[4,1440]{1,0:T(4,128)}, u32[]{:S(2)}) copy-start(s32[4,1440]{1,0:T(4,128)} %depth_ref.1) | copy-start | bytes 69124
  2.1 8.1 %copy-start.7 = (f32[64,32]{0,1:T(8,128)S(1)}, f32[64,32]{0,1:T(8,128)}, u32[]{:S(2)}) copy-start(f32[64,32]{0,1:T(8,128)} %param.10) | copy-start | bytes 24580
  3.7 15.2 %collective-permute-start.1 = (bf16[18,16,1536]{2,1,0:T(8,128)(2,1)S(1)}, bf16[18,16,1536]{2,1,0:T(8,128)(2,1)S(1)}, u32[]{:S(2)}, u32[]{:S(2)}) collective-permute-start(bf16[18,16,1536]{2,1,0:T(8,128)(2,1)S(1)} %get-tuple-element.18.top_ref), channel_id=1, source_target_pairs={{1,0},{2,1},{3,2},{5,4},{6,5},{7,6},{9,8},{10,9},{11,10},{13,12},{... | collective-permute-start | bytes 2654216 | tf_op jit(solution)/shard_map/ppermute | solution.py:644
  5.7 14.4 %collective-permute-start = (bf16[18,16,1536]{2,1,0:T(8,128)(2,1)S(1)}, bf16[18,16,1536]{2,1,0:T(8,128)(2,1)S(1)}, u32[]{:S(2)}, u32[]{:S(2)}) collective-permute-start(bf16[18,16,1536]{2,1,0:T(8,128)(2,1)S(1)} %get-tuple-element.19.bottom_ref), channel_id=1, source_target_pairs={{0,1},{1,2},{2,3},{4,5},{5,6},{6,7},{8,9},{9,10},{10,11},{12,13},{... | collective-permute-start | bytes 2654216 | tf_op jit(solution)/shard_map/ppermute | solution.py:643
  24.3 22.0 %collective-permute-start.3 = (s32[1,80,640]{2,1,0:T(8,128)S(1)}, s32[1,80,640]{2,1,0:T(8,128)S(1)}, u32[]{:S(2)}, u32[]{:S(2)}) collective-permute-start(s32[1,80,640]{2,1,0:T(8,128)S(1)} %get-tuple-element.24), channel_id=1, source_target_pairs={{0,20},{4,16},{8,28},{12,24},{16,4},{20,0},{24,12},{28,8},{1,21},{... | collective-permute-start | bytes 614408 | tf_op jit(solution)/shard_map/ppermute | solution.py:682
  28.1 18.2 %collective-permute-start.4 = (s32[1,80,640]{2,1,0:T(8,128)S(1)}, s32[1,80,640]{2,1,0:T(8,128)S(1)}, u32[]{:S(2)}, u32[]{:S(2)}) collective-permute-start(s32[1,80,640]{2,1,0:T(8,128)S(1)} %get-tuple-element.25), channel_id=1, source_target_pairs={{0,24},{4,28},{8,16},{12,20},{16,8},{20,12},{24,0},{28,4},{1,25},{... | collective-permute-start | bytes 614408 | tf_op jit(solution)/shard_map/ppermute | solution.py:682
  28.7 17.6 %collective-permute-start.5 = (s32[1,80,640]{2,1,0:T(8,128)S(1)}, s32[1,80,640]{2,1,0:T(8,128)S(1)}, u32[]{:S(2)}, u32[]{:S(2)}) collective-permute-start(s32[1,80,640]{2,1,0:T(8,128)S(1)} %get-tuple-element.26), channel_id=1, source_target_pairs={{0,28},{4,24},{8,20},{12,16},{16,12},{20,8},{24,4},{28,0},{1,29},{... | collective-permute-start | bytes 614408 | tf_op jit(solution)/shard_map/ppermute | solution.py:682
  31.3 26.2 %collective-permute-start.2 = (s32[1,80,640]{2,1,0:T(8,128)S(1)}, s32[1,80,640]{2,1,0:T(8,128)S(1)}, u32[]{:S(2)}, u32[]{:S(2)}) collective-permute-start(s32[1,80,640]{2,1,0:T(8,128)S(1)} %get-tuple-element.23.after_ref), channel_id=1, source_target_pairs={{0,16},{4,20},{8,24},{12,28},{16,0},{20,4},{24,8},{28,12},{1,17},{... | collective-permute-start | bytes 614408 | tf_op jit(solution)/shard_map/ppermute | solution.py:682
  36.8 22.0 %all-to-all-start = ((s32[4,80,640]{2,1,0:T(8,128)}), s32[4,80,640]{2,1,0:T(8,128)}, u32[]{:S(2)}, u32[]{:S(2)}) async-start(s32[4,80,640]{2,1,0:T(8,128)} %shard_map.86.after_ref), calls=%async_computation | async-start | bytes 1638400 | tf_op jit(solution)/shard_map/all_to_all | solution.py:685
  46.3 11.3 %copy-start.8 = (s32[1,80,640]{2,1,0:T(8,128)}, s32[1,80,640]{2,1,0:T(8,128)S(1)}, u32[]{:S(2)}) copy-start(s32[1,80,640]{2,1,0:T(8,128)S(1)} %collective-permute-done.3.refs_1_) | copy-start | bytes 614404
  46.3 11.3 %copy-start.9 = (s32[1,80,640]{2,1,0:T(8,128)}, s32[1,80,640]{2,1,0:T(8,128)S(1)}, u32[]{:S(2)}) copy-start(s32[1,80,640]{2,1,0:T(8,128)S(1)} %collective-permute-done.4.refs_2_) | copy-start | bytes 614404
  46.3 11.3 %copy-start.10 = (s32[1,80,640]{2,1,0:T(8,128)}, s32[1,80,640]{2,1,0:T(8,128)S(1)}, u32[]{:S(2)}) copy-start(s32[1,80,640]{2,1,0:T(8,128)S(1)} %collective-permute-done.5.refs_3_) | copy-start | bytes 614404
  57.6 0.7 %copy-start.11 = (s32[1,80,640]{2,1,0:T(8,128)}, s32[1,80,640]{2,1,0:T(8,128)S(1)}, u32[]{:S(2)}) copy-start(s32[1,80,640]{2,1,0:T(8,128)S(1)} %collective-permute-done.2.refs_0_) | copy-start | bytes 614404

commit v8 on v7

--- a/solution.py
+++ b/solution.py
@@ -74,7 +74,7 @@
     return table
 
 
-def arrange_kernel(x_ref, land_ref, after_ref, top_ref, bottom_ref, scratch):
+def arrange_kernel(x_ref, land_ref, after_ref, bottom_ref, top_ref, scratch):
     freqs, parts, step, rows, lon = x_ref.shape
     chunks = scratch.shape[1]
     tail = lon - (chunks - 1) * LANES
@@ -282,7 +282,7 @@
     lax.fori_loop(0, chunks // together, some_chunks, 0)
 
 
-def pack_kernel(directions, offsets, adv_ref, above_ref, below_ref, coef_ref, cells_ref, ranges_ref, after_ref, *refs):
+def pack_kernel(directions, offsets, adv_ref, below_ref, above_ref, coef_ref, cells_ref, ranges_ref, after_ref, *refs):
     out_refs, (packed, turned_values, trig) = refs[:-3], refs[-3:]
     turns, height, padded = adv_ref.shape
     rows = height // SUBLANES
@@ -539,6 +539,8 @@
             copy.start()
     scale = power_table(2.0**-EXPONENT_ZERO / STEP_COUNT, 1)
     freq = iota(shape, 0) // (SUBLANES // freqs)
+    square = (LANES, LANES)
+    unit_matrix = (iota(square, 0) == iota(square, 1)).astype(jnp.bfloat16)
     total = groups * each
     reach = orders.shape[1]
     firsts = []
@@ -578,7 +580,16 @@
                     value = jnp.where(occupied, value * factor, 0.0)
                     ordered[m, side ^ far, source * each + j * SUBLANES : source * each + (j + 1) * SUBLANES, :] = value
         slots = slice(m * LANES, min((m + 1) * LANES, out_ref.shape[0]))
-        turned = jnp.concatenate([ordered[m, place].T for place in range(2)], axis=1).astype(jnp.bfloat16)
+        turned = [
+            lax.dot_general(
+                unit_matrix,
+                ordered[m, place].astype(jnp.bfloat16),
+                (((1,), (1,)), ((), ())),
+                preferred_element_type=F32,
+            ).astype(jnp.bfloat16)
+            for place in range(2)
+        ]
+        turned = jnp.concatenate(turned, axis=1)
         for n, first in enumerate(firsts):
             block = jnp.dot(turned[:, first : first + reach], orders[n], preferred_element_type=F32)
             out_ref[slots, n * LANES : (n + 1) * LANES] = block[: slots.stop - slots.start].astype(jnp.bfloat16)
@@ -626,7 +637,7 @@
     step = 3
     half = jax.ShapeDtypeStruct((turns, height // 2, padded), jnp.bfloat16)
     half_spec = pl.BlockSpec((step, height // 2, padded), lambda i: (i, 0, 0))
-    top, bottom = call(
+    bottom, top = call(
         arrange_kernel,
         [half, half],
         (4 * hbm, 2 * hbm),
@@ -640,8 +651,8 @@
         scratch_shapes=[pltpu.VMEM((step, chunks, height, LANES), F32)],
     )(spectra.reshape(freqs, parts, turns, rows, lon), land_mask, ranges)
     down = [(i, i + 1) for i in range(bands - 1)]
+    below = lax.ppermute(top, "band", [(j, i) for i, j in down])
     above = lax.ppermute(bottom, "band", down)
-    below = lax.ppermute(top, "band", [(j, i) for i, j in down])
 
     advected, coefs = call(
         functools.partial(advect_kernel, directions, stretch),
@@ -675,7 +686,7 @@
                     pltpu.VMEM((6 if chunks % 6 == 0 else 1, turns, SUBLANES, LANES), F32),
                     pltpu.VMEM((2, turns, SUBLANES, LANES), F32),
                 ],
-            )(advected, above, below, coefs, cells, ranges, after)
+            )(advected, below, above, coefs, cells, ranges, after)
         )
         after = shipped[0][0]
     far = [
@@ -713,7 +724,7 @@
         jax.ShapeDtypeStruct((slot_count, total), jnp.bfloat16),
         (50 * total * slots, 6 * total * slots),
         vmem=WHOLE_VMEM,
-        in_specs=[anywhere] * (half + 4) + [smem],
+        in_specs=[anywhere] * (half + 3) + [vmem, smem],
         out_specs=vmem,
         scratch_shapes=[
             pltpu.VMEM((half,) + block, I32),

time: 67.4 us -> 67.6 us (level)
  waiting for transfers between devices: 18.5 us -> 20.4 us
  starting transfers between devices: 17.7 us -> 16.7 us
    ppermute x4, waiting for transfers between devices: 12.4 us -> 14.3 us  [body(): lax.ppermute(part, 'comp', [(i, i ^ half + n) for i in range(groups)])]
    ppermute x4, starting transfers between devices: 7.06 us -> 6.02 us  [body(): lax.ppermute(part, 'comp', [(i, i ^ half + n) for i in range(groups)])]
  transfers between devices with their start and end apart: 7 -> 7, of which waited for: 4 -> 4; matrix products, arithmetic and copies ran while one was open for 0% -> 0% of each run, Pallas kernels for 21% -> 20%
where the time goes in v8:
time: 67.6 us; the launch traced here: 67.3 us
  Pallas kernels  28.3 us (42%)
  waiting for transfers between devices  20.4 us (30%)
  starting transfers between devices  16.7 us (25%)
  local copies, waits for them, and re-layouts  0.84 us (1%)
  other arithmetic  0.76 us (1%)
    ppermute x4, waiting for transfers between devices, body(): lax.ppermute(part, 'comp', [(i, i ^ half + n) for i in range(groups)])  14.3 us
    pallas_call x2, Pallas kernels, body(): call(functools.partial(pack_kernel, directions, tuple(offsets)), [jax.Sha...  9.62 us
    pallas_call x1, Pallas kernels, body(): call(functools.partial(finish_kernel, freqs, half), jax.ShapeDtypeStruct(...  7.74 us
    ppermute x4, starting transfers between devices, body(): lax.ppermute(part, 'comp', [(i, i ^ half + n) for i in range(groups)])  6.02 us
    ppermute x1, waiting for transfers between devices, body(): below = lax.ppermute(top, 'band', [(j, i) for i, j in down])  4.93 us
    ppermute x1, starting transfers between devices, body(): above = lax.ppermute(bottom, 'band', down)  4.46 us
    all_to_all x1, starting transfers between devices, body(): lax.all_to_all(shipped[1][0], 'comp', split_axis=0, concat_axis=0, axis_i...  4.21 us
    pallas_call x1, Pallas kernels, body(): call(functools.partial(advect_kernel, directions, stretch), [jax.ShapeDty...  3.8 us
  transfers between devices with their start and end apart: 7, of which 4 were waited for; matrix products, arithmetic and copies ran while one was open for 0% of the time, Pallas kernels for 20%

profile of v8, /device:TPU:1, one launch (start us, length us, event | category | flops | bytes accessed | tf_op | source)
XLA Modules:
  0.0 67.3 jit_solution(13316169564790083859)
XLA Ops:
  0.0 0.8 %pad_add_fusion.land_ref = s32[5,1440]{1,0:T(8,128)S(1)} fusion(s32[1,8]{1,0:T(1,128)} %refs_8_.1, s32[4,1440]{1,0:T(4,128)} %land_ref.1), kind=kLoop, calls=%fused_computation | loop fusion | flops 7200 | bytes 51872 | tf_op jit(solution)/shard_map/concatenate | solution.py:635
  0.8 0.0 copy-start.3
  0.8 1.3 %shard_map.82 = (s32[8,8,640]{2,1,0:T(8,128)S(1)}, s32[16,128]{1,0:T(8,128)S(1)}) custom-call(s32[5,1440]{1,0:T(8,128)S(1)} %pad_add_fusion.land_ref), custom_call_target="tpu_custom_call" | custom-call | flops 2048000000 | bytes 40960 | tf_op jit(solution)/shard_map/pallas_call | solution.py:625
  2.1 0.0 copy-start.6
  2.1 0.0 copy-start.7
  2.1 0.1 copy-done
  2.2 1.5 %shard_map.83 = (bf16[18,16,1536]{2,1,0:T(8,128)(2,1)S(1)}, bf16[18,16,1536]{2,1,0:T(8,128)(2,1)S(1)}) custom-call(bf16[4,2,18,4,1440]{4,3,2,1,0:T(4,128)(2,1)S(1)} %bitcast.3, s32[4,1440]{1,0:T(4,128)S(1)} %copy-done.3, s32[16,128]{1,0:T(8,128)S(1)} %get-tuple-element.17.after_ref.ranges_ref), custom_call_target="tpu_custom_call" | custom-call | flops 7077888 | bytes 3538944 | tf_op jit(solution)/shard_map/pallas_call | solution.py:640
  3.7 2.0 %collective-permute-start = (bf16[18,16,1536]{2,1,0:T(8,128)(2,1)S(1)}, bf16[18,16,1536]{2,1,0:T(8,128)(2,1)S(1)}, u32[]{:S(2)}, u32[]{:S(2)}) collective-permute-start(bf16[18,16,1536]{2,1,0:T(8,128)(2,1)S(1)} %get-tuple-element.18.top_ref), channel_id=1, source_target_pairs={{1,0},{2,1},{3,2},{5,4},{6,5},{7,6},{9,8},{10,9},{11,10},{13,12},{... | collective-permute-start | bytes 2654216 | tf_op jit(solution)/shard_map/ppermute | solution.py:654
  5.7 4.5 %collective-permute-start.1 = (bf16[18,16,1536]{2,1,0:T(8,128)(2,1)S(1)}, bf16[18,16,1536]{2,1,0:T(8,128)(2,1)S(1)}, u32[]{:S(2)}, u32[]{:S(2)}) collective-permute-start(bf16[18,16,1536]{2,1,0:T(8,128)(2,1)S(1)} %get-tuple-element.19.bottom_ref), channel_id=1, source_target_pairs={{0,1},{1,2},{2,3},{4,5},{5,6},{6,7},{8,9},{9,10},{10,11},{12,13},{... | collective-permute-start | bytes 2654216 | tf_op jit(solution)/shard_map/ppermute | solution.py:655
  10.2 3.8 %shard_map.84 = (f32[18,32,1536]{2,1,0:T(8,128)S(1)}, f32[4,32,1536]{2,1,0:T(8,128)S(1)}) custom-call(bf16[18,16,1536]{2,1,0:T(8,128)(2,1)S(1)} %get-tuple-element.18.top_ref, bf16[18,16,1536]{2,1,0:T(8,128)(2,1)S(1)} %get-tuple-element.19.bottom_ref, f32[32,64]{1,0:T(8,128)S(1)} %bitcast.4, s32[4,1440]{1,0:T(4,128)S(1)} %copy-done.6, ...), custom_call_target="tpu_custom_call" | custom-call | flops 88473600 | bytes 7077888 | tf_op jit(solution)/shard_map/pallas_call | solution.py:657
  14.0 4.9 %collective-permute-done.below_ref = bf16[18,16,1536]{2,1,0:T(8,128)(2,1)S(1)} collective-permute-done((bf16[18,16,1536]{2,1,0:T(8,128)(2,1)S(1)}, bf16[18,16,1536]{2,1,0:T(8,128)(2,1)S(1)}, u32[]{:S(2)}, u32[]{:S(2)}) %collective-permute-start) | collective-permute-done | bytes 884768 | tf_op jit(solution)/shard_map/ppermute | solution.py:654
  19.0 1.2 %collective-permute-done.1.above_ref = bf16[18,16,1536]{2,1,0:T(8,128)(2,1)S(1)} collective-permute-done((bf16[18,16,1536]{2,1,0:T(8,128)(2,1)S(1)}, bf16[18,16,1536]{2,1,0:T(8,128)(2,1)S(1)}, u32[]{:S(2)}, u32[]{:S(2)}) %collective-permute-start.1) | collective-permute-done | bytes 884768 | tf_op jit(solution)/shard_map/ppermute | solution.py:655
  20.2 4.6 %shard_map.85 = (s32[1,80,640]{2,1,0:T(8,128)S(1)}, s32[1,80,640]{2,1,0:T(8,128)S(1)}, s32[1,80,640]{2,1,0:T(8,128)S(1)}, s32[1,80,640]{2,1,0:T(8,128)S(1)}) custom-call(f32[18,32,1536]{2,1,0:T(8,128)S(1)} %get-tuple-element.20.adv_ref, bf16[18,16,1536]{2,1,0:T(8,128)(2,1)S(1)} %collective-permute-done.below_ref, ...), custom_call_target="tpu_custom_call" | custom-call | flops 44236800 | bytes 5308416 | tf_op jit(solution)/shard_map/pallas_call | solution.py:678
  24.8 2.8 %collective-permute-start.3 = (s32[1,80,640]{2,1,0:T(8,128)S(1)}, s32[1,80,640]{2,1,0:T(8,128)S(1)}, u32[]{:S(2)}, u32[]{:S(2)}) collective-permute-start(s32[1,80,640]{2,1,0:T(8,128)S(1)} %get-tuple-element.24), channel_id=1, source_target_pairs={{0,20},{4,16},{8,28},{12,24},{16,4},{20,0},{24,12},{28,8},{1,21},{... | collective-permute-start | bytes 614408 | tf_op jit(solution)/shard_map/ppermute | solution.py:693
  27.6 1.6 %collective-permute-start.4 = (s32[1,80,640]{2,1,0:T(8,128)S(1)}, s32[1,80,640]{2,1,0:T(8,128)S(1)}, u32[]{:S(2)}, u32[]{:S(2)}) collective-permute-start(s32[1,80,640]{2,1,0:T(8,128)S(1)} %get-tuple-element.25), channel_id=1, source_target_pairs={{0,24},{4,28},{8,16},{12,20},{16,8},{20,12},{24,0},{28,4},{1,25},{... | collective-permute-start | bytes 614408 | tf_op jit(solution)/shard_map/ppermute | solution.py:693
  29.2 1.6 %collective-permute-start.5 = (s32[1,80,640]{2,1,0:T(8,128)S(1)}, s32[1,80,640]{2,1,0:T(8,128)S(1)}, u32[]{:S(2)}, u32[]{:S(2)}) collective-permute-start(s32[1,80,640]{2,1,0:T(8,128)S(1)} %get-tuple-element.26), channel_id=1, source_target_pairs={{0,28},{4,24},{8,20},{12,16},{16,12},{20,8},{24,4},{28,0},{1,29},{... | collective-permute-start | bytes 614408 | tf_op jit(solution)/shard_map/ppermute | solution.py:693
  30.8 5.0 %shard_map.86.after_ref = s32[4,80,640]{2,1,0:T(8,128)} custom-call(f32[18,32,1536]{2,1,0:T(8,128)S(1)} %get-tuple-element.20.adv_ref, bf16[18,16,1536]{2,1,0:T(8,128)(2,1)S(1)} %collective-permute-done.below_ref, bf16[18,16,1536]{2,1,0:T(8,128)(2,1)S(1)} %collective-permute-done.1.above_ref, f32[4,32,1536]{2,1,0:T(8,128)S(1)} %get-tuple-element.21.coef_ref, ...), custom_call_target="tpu_custom_call" | custom-call | flops 1000 | bytes 1000 | tf_op jit(solution)/shard_map/pallas_call | solution.py:678
  35.8 4.2 %all-to-all-start = ((s32[4,80,640]{2,1,0:T(8,128)}), s32[4,80,640]{2,1,0:T(8,128)}, u32[]{:S(2)}, u32[]{:S(2)}) async-start(s32[4,80,640]{2,1,0:T(8,128)} %shard_map.86.after_ref), calls=%async_computation | async-start | bytes 1638400 | tf_op jit(solution)/shard_map/all_to_all | solution.py:696
  40.0 3.8 %shard_map.87 = (f32[4,18,8,640]{3,2,1,0:T(8,128)}, f32[4,18,8,640]{3,2,1,0:T(8,128)}) custom-call(f32[2,4,1440]{2,1,0:T(4,128)} %wind_ref.1, s32[8,8,640]{2,1,0:T(8,128)} %copy-done.1, s32[16,128]{1,0:T(8,128)} %copy-done.2, s32[4,80,640]{2,1,0:T(8,128)} %shard_map.86.after_ref), custom_call_target="tpu_custom_call" | custom-call | flops 1000 | bytes 1000 | tf_op jit(solution)/shard_map/pallas_call | solution.py:700
  43.8 2.5 %collective-permute-done.3.refs_1_ = s32[1,80,640]{2,1,0:T(8,128)S(1)} collective-permute-done((s32[1,80,640]{2,1,0:T(8,128)S(1)}, s32[1,80,640]{2,1,0:T(8,128)S(1)}, u32[]{:S(2)}, u32[]{:S(2)}) %collective-permute-start.3) | collective-permute-done | bytes 204832 | tf_op jit(solution)/shard_map/ppermute | solution.py:693
  46.4 11.8 %collective-permute-done.2.refs_0_ = s32[1,80,640]{2,1,0:T(8,128)S(1)} collective-permute-done((s32[1,80,640]{2,1,0:T(8,128)S(1)}, s32[1,80,640]{2,1,0:T(8,128)S(1)}, u32[]{:S(2)}, u32[]{:S(2)}) %collective-permute-start.2) | collective-permute-done | bytes 204832 | tf_op jit(solution)/shard_map/ppermute | solution.py:693
  58.1 0.7 copy-done.11
  58.8 0.6 shard_map.88.refs_7_
  59.4 7.7 %shard_map.89 = bf16[630,1152]{1,0:T(8,128)(2,1)} custom-call(s32[1,80,640]{2,1,0:T(8,128)} %copy-done.11, s32[1,80,640]{2,1,0:T(8,128)} %copy-done.8, s32[1,80,640]{2,1,0:T(8,128)} %copy-done.9, s32[1,80,640]{2,1,0:T(8,128)} %copy-done.10, s32[4,80,640]{2,1,0:T(8,128)} %all-to-all-done.refs_4_, f32[4,18,8,640]{3,2,1,0:T(8,128)} %get-tuple-element.27.refs_5_, ...), custom_call_target="tpu_custom_call" | custom-call | flops 36864000 | bytes 4423680 | tf_op jit(solution)/shard_map/pallas_call | solution.py:722
  (23 shorter events, 0.1 us)
Async XLA Ops:
  0.8 1.5 %copy-start = (bf16[4,36,4,1440]{3,2,1,0:T(4,128)(2,1)S(1)}, bf16[4,36,4,1440]{3,2,1,0:T(4,128)(2,1)}, u32[]{:S(2)}) copy-start(bf16[4,36,4,1440]{3,2,1,0:T(4,128)(2,1)} %param.8) | copy-start | bytes 4976644
  0.8 1.5 %copy-start.3 = (s32[4,1440]{1,0:T(4,128)S(1)}, s32[4,1440]{1,0:T(4,128)}, u32[]{:S(2)}) copy-start(s32[4,1440]{1,0:T(4,128)} %land_ref.1) | copy-start | bytes 69124
  2.0 28.8 %copy-start.1 = (s32[8,8,640]{2,1,0:T(8,128)}, s32[8,8,640]{2,1,0:T(8,128)S(1)}, u32[]{:S(2)}) copy-start(s32[8,8,640]{2,1,0:T(8,128)S(1)} %get-tuple-element.22.cells_ref) | copy-start | bytes 491524
  2.1 28.8 %copy-start.2 = (s32[16,128]{1,0:T(8,128)}, s32[16,128]{1,0:T(8,128)S(1)}, u32[]{:S(2)}) copy-start(s32[16,128]{1,0:T(8,128)S(1)} %get-tuple-element.17.after_ref.ranges_ref) | copy-start | bytes 24580
  2.1 8.1 %copy-start.4 = (f32[2,4,1440]{2,1,0:T(4,128)S(1)}, f32[2,4,1440]{2,1,0:T(4,128)}, u32[]{:S(2)}) copy-start(f32[2,4,1440]{2,1,0:T(4,128)} %current_ref.1) | copy-start | bytes 138244
  2.1 8.1 %copy-start.5 = (f32[2,4,1440]{2,1,0:T(4,128)S(1)}, f32[2,4,1440]{2,1,0:T(4,128)}, u32[]{:S(2)}) copy-start(f32[2,4,1440]{2,1,0:T(4,128)} %slope_ref.1) | copy-start | bytes 138244
  2.1 8.1 %copy-start.6 = (s32[4,1440]{1,0:T(4,128)S(1)}, s32[4,1440]{1,0:T(4,128)}, u32[]{:S(2)}) copy-start(s32[4,1440]{1,0:T(4,128)} %depth_ref.1) | copy-start | bytes 69124
  2.1 8.1 %copy-start.7 = (f32[64,32]{0,1:T(8,128)S(1)}, f32[64,32]{0,1:T(8,128)}, u32[]{:S(2)}) copy-start(f32[64,32]{0,1:T(8,128)} %param.10) | copy-start | bytes 24580
  3.7 15.2 %collective-permute-start = (bf16[18,16,1536]{2,1,0:T(8,128)(2,1)S(1)}, bf16[18,16,1536]{2,1,0:T(8,128)(2,1)S(1)}, u32[]{:S(2)}, u32[]{:S(2)}) collective-permute-start(bf16[18,16,1536]{2,1,0:T(8,128)(2,1)S(1)} %get-tuple-element.18.top_ref), channel_id=1, source_target_pairs={{1,0},{2,1},{3,2},{5,4},{6,5},{7,6},{9,8},{10,9},{11,10},{13,12},{... | collective-permute-start | bytes 2654216 | tf_op jit(solution)/shard_map/ppermute | solution.py:654
  5.7 14.4 %collective-permute-start.1 = (bf16[18,16,1536]{2,1,0:T(8,128)(2,1)S(1)}, bf16[18,16,1536]{2,1,0:T(8,128)(2,1)S(1)}, u32[]{:S(2)}, u32[]{:S(2)}) collective-permute-start(bf16[18,16,1536]{2,1,0:T(8,128)(2,1)S(1)} %get-tuple-element.19.bottom_ref), channel_id=1, source_target_pairs={{0,1},{1,2},{2,3},{4,5},{5,6},{6,7},{8,9},{9,10},{10,11},{12,13},{... | collective-permute-start | bytes 2654216 | tf_op jit(solution)/shard_map/ppermute | solution.py:655
  24.8 21.5 %collective-permute-start.3 = (s32[1,80,640]{2,1,0:T(8,128)S(1)}, s32[1,80,640]{2,1,0:T(8,128)S(1)}, u32[]{:S(2)}, u32[]{:S(2)}) collective-permute-start(s32[1,80,640]{2,1,0:T(8,128)S(1)} %get-tuple-element.24), channel_id=1, source_target_pairs={{0,20},{4,16},{8,28},{12,24},{16,4},{20,0},{24,12},{28,8},{1,21},{... | collective-permute-start | bytes 614408 | tf_op jit(solution)/shard_map/ppermute | solution.py:693
  27.6 18.7 %collective-permute-start.4 = (s32[1,80,640]{2,1,0:T(8,128)S(1)}, s32[1,80,640]{2,1,0:T(8,128)S(1)}, u32[]{:S(2)}, u32[]{:S(2)}) collective-permute-start(s32[1,80,640]{2,1,0:T(8,128)S(1)} %get-tuple-element.25), channel_id=1, source_target_pairs={{0,24},{4,28},{8,16},{12,20},{16,8},{20,12},{24,0},{28,4},{1,25},{... | collective-permute-start | bytes 614408 | tf_op jit(solution)/shard_map/ppermute | solution.py:693
  29.2 17.2 %collective-permute-start.5 = (s32[1,80,640]{2,1,0:T(8,128)S(1)}, s32[1,80,640]{2,1,0:T(8,128)S(1)}, u32[]{:S(2)}, u32[]{:S(2)}) collective-permute-start(s32[1,80,640]{2,1,0:T(8,128)S(1)} %get-tuple-element.26), channel_id=1, source_target_pairs={{0,28},{4,24},{8,20},{12,16},{16,12},{20,8},{24,4},{28,0},{1,29},{... | collective-permute-start | bytes 614408 | tf_op jit(solution)/shard_map/ppermute | solution.py:693
  30.8 27.3 %collective-permute-start.2 = (s32[1,80,640]{2,1,0:T(8,128)S(1)}, s32[1,80,640]{2,1,0:T(8,128)S(1)}, u32[]{:S(2)}, u32[]{:S(2)}) collective-permute-start(s32[1,80,640]{2,1,0:T(8,128)S(1)} %get-tuple-element.23.after_ref), channel_id=1, source_target_pairs={{0,16},{4,20},{8,24},{12,28},{16,0},{20,4},{24,8},{28,12},{1,17},{... | collective-permute-start | bytes 614408 | tf_op jit(solution)/shard_map/ppermute | solution.py:693
  35.8 23.6 %all-to-all-start = ((s32[4,80,640]{2,1,0:T(8,128)}), s32[4,80,640]{2,1,0:T(8,128)}, u32[]{:S(2)}, u32[]{:S(2)}) async-start(s32[4,80,640]{2,1,0:T(8,128)} %shard_map.86.after_ref), calls=%async_computation | async-start | bytes 1638400 | tf_op jit(solution)/shard_map/all_to_all | solution.py:696
  46.3 11.8 %copy-start.8 = (s32[1,80,640]{2,1,0:T(8,128)}, s32[1,80,640]{2,1,0:T(8,128)S(1)}, u32[]{:S(2)}) copy-start(s32[1,80,640]{2,1,0:T(8,128)S(1)} %collective-permute-done.3.refs_1_) | copy-start | bytes 614404
  46.3 11.8 %copy-start.9 = (s32[1,80,640]{2,1,0:T(8,128)}, s32[1,80,640]{2,1,0:T(8,128)S(1)}, u32[]{:S(2)}) copy-start(s32[1,80,640]{2,1,0:T(8,128)S(1)} %collective-permute-done.4.refs_2_) | copy-start | bytes 614404
  46.3 11.8 %copy-start.10 = (s32[1,80,640]{2,1,0:T(8,128)}, s32[1,80,640]{2,1,0:T(8,128)S(1)}, u32[]{:S(2)}) copy-start(s32[1,80,640]{2,1,0:T(8,128)S(1)} %collective-permute-done.5.refs_3_) | copy-start | bytes 614404
  58.1 0.7 %copy-start.11 = (s32[1,80,640]{2,1,0:T(8,128)}, s32[1,80,640]{2,1,0:T(8,128)S(1)}, u32[]{:S(2)}) copy-start(s32[1,80,640]{2,1,0:T(8,128)S(1)} %collective-permute-done.2.refs_0_) | copy-start | bytes 614404

commit v9 on v8

--- a/solution.py
+++ b/solution.py
@@ -519,7 +519,7 @@
 def finish_kernel(freqs, half, *refs):
     far_refs, refs = refs[:half], refs[half:]
     near_ref, grown_near_ref, grown_far_ref, _, counts_ref, out_ref = refs[:6]
-    far_words, near_words, near_values, far_values, ordered, orders, arrivals = refs[6:]
+    far_words, near_words, near_values, far_values, ordered, arrivals = refs[6:]
     groups = 2 * half
     turns = near_values.shape[1]
     each = turns * SUBLANES
@@ -541,18 +541,6 @@
     freq = iota(shape, 0) // (SUBLANES // freqs)
     square = (LANES, LANES)
     unit_matrix = (iota(square, 0) == iota(square, 1)).astype(jnp.bfloat16)
-    total = groups * each
-    reach = orders.shape[1]
-    firsts = []
-    for n in range(total // LANES):
-        first = min((n * LANES // each) * each // LANES * LANES, total - reach)
-        firsts.append(first)
-        target = iota((1, LANES), 1) + n * LANES
-        source = sum((target >= each * b).astype(I32) for b in range(1, groups))
-        rest = target - source * each
-        sublane = sum((rest >= turns * b).astype(I32) for b in range(1, SUBLANES))
-        origin = source * each + (rest - sublane * turns) * SUBLANES + sublane - first
-        orders[n] = (iota((reach, LANES), 0) == origin).astype(F32).astype(jnp.bfloat16)
     steps = [jnp.where(side ^ far == 0, jnp.float32(1.0), jnp.float32(1.1 ** (half * freqs))) for far in range(2)]
     for m, span in enumerate(spans):
         for copy in copies[m]:
@@ -578,21 +566,21 @@
                 for j in range(turns):
                     value = far_values[own ^ source, j, :, span] if far else near_values[source, j, :, span]
                     value = jnp.where(occupied, value * factor, 0.0)
-                    ordered[m, side ^ far, source * each + j * SUBLANES : source * each + (j + 1) * SUBLANES, :] = value
+                    ordered[m, side ^ far, pl.ds(source * each + j, SUBLANES, stride=turns), :] = value
         slots = slice(m * LANES, min((m + 1) * LANES, out_ref.shape[0]))
-        turned = [
-            lax.dot_general(
-                unit_matrix,
-                ordered[m, place].astype(jnp.bfloat16),
-                (((1,), (1,)), ((), ())),
-                preferred_element_type=F32,
-            ).astype(jnp.bfloat16)
-            for place in range(2)
-        ]
-        turned = jnp.concatenate(turned, axis=1)
-        for n, first in enumerate(firsts):
-            block = jnp.dot(turned[:, first : first + reach], orders[n], preferred_element_type=F32)
-            out_ref[slots, n * LANES : (n + 1) * LANES] = block[: slots.stop - slots.start].astype(jnp.bfloat16)
+        for place in range(2):
+            if place == 0:
+                turned = lax.dot_general(
+                    unit_matrix,
+                    ordered[m, place].astype(jnp.bfloat16),
+                    (((1,), (1,)), ((), ())),
+                    preferred_element_type=F32,
+                )
+            else:
+                turned = ordered[m, place].T
+            out_ref[slots, place * half * each : (place + 1) * half * each] = turned[
+                : slots.stop - slots.start
+            ].astype(jnp.bfloat16)
 
 
 def frequency(index, count):
@@ -732,7 +720,6 @@
             pltpu.VMEM((half, turns, SUBLANES, slots), F32),
             pltpu.VMEM((half, turns, SUBLANES, slots), F32),
             pltpu.VMEM((slots // LANES, 2, total // 2, LANES), F32),
-            pltpu.VMEM((total // LANES, 3 * LANES, LANES), jnp.bfloat16),
             pltpu.SemaphoreType.DMA((slots // LANES, half + 3)),
         ],
     )(*far, near, grown_near, grown_far, gate, block_counts)

time: 67.6 us -> 66 us (0.976)
  Pallas kernels: 28.3 us -> 26.9 us
    pallas_call x1, Pallas kernels: 7.74 us -> 6.14 us  [body(): call(functools.partial(finish_kernel, freqs, half), jax.ShapeDtypeStruct(...]
where the time goes in v9:
time: 66 us; the launch traced here: 65.7 us
  Pallas kernels  26.9 us (41%)
  waiting for transfers between devices  20.2 us (31%)
  starting transfers between devices  16.7 us (25%)
  local copies, waits for them, and re-layouts  0.84 us (1%)
  other arithmetic  0.76 us (1%)
    ppermute x4, waiting for transfers between devices, body(): lax.ppermute(part, 'comp', [(i, i ^ half + n) for i in range(groups)])  14.1 us
    pallas_call x2, Pallas kernels, body(): call(functools.partial(pack_kernel, directions, tuple(offsets)), [jax.Sha...  9.61 us
    pallas_call x1, Pallas kernels, body(): call(functools.partial(finish_kernel, freqs, half), jax.ShapeDtypeStruct(...  6.14 us
    ppermute x4, starting transfers between devices, body(): lax.ppermute(part, 'comp', [(i, i ^ half + n) for i in range(groups)])  6.02 us
    ppermute x1, waiting for transfers between devices, body(): below = lax.ppermute(top, 'band', [(j, i) for i, j in down])  4.93 us
    ppermute x1, starting transfers between devices, body(): above = lax.ppermute(bottom, 'band', down)  4.46 us
    all_to_all x1, starting transfers between devices, body(): lax.all_to_all(shipped[1][0], 'comp', split_axis=0, concat_axis=0, axis_i...  4.21 us
    pallas_call x1, Pallas kernels, body(): call(functools.partial(grow_kernel, directions), [values, values], LITTLE...  3.95 us
  transfers between devices with their start and end apart: 7, of which 4 were waited for; matrix products, arithmetic and copies ran while one was open for 0% of the time, Pallas kernels for 20%

profile of v9, /device:TPU:1, one launch (start us, length us, event | category | flops | bytes accessed | tf_op | source)
XLA Modules:
  0.0 65.7 jit_solution(527048611151334685)
XLA Ops:
  0.0 0.8 %pad_add_fusion.land_ref = s32[5,1440]{1,0:T(8,128)S(1)} fusion(s32[1,8]{1,0:T(1,128)} %refs_8_.1, s32[4,1440]{1,0:T(4,128)} %land_ref.1), kind=kLoop, calls=%fused_computation | loop fusion | flops 7200 | bytes 51872 | tf_op jit(solution)/shard_map/concatenate | solution.py:623
  0.8 0.0 copy-start.3
  0.8 1.3 %shard_map.82 = (s32[8,8,640]{2,1,0:T(8,128)S(1)}, s32[16,128]{1,0:T(8,128)S(1)}) custom-call(s32[5,1440]{1,0:T(8,128)S(1)} %pad_add_fusion.land_ref), custom_call_target="tpu_custom_call" | custom-call | flops 2048000000 | bytes 40960 | tf_op jit(solution)/shard_map/pallas_call | solution.py:613
  2.1 0.0 copy-start.4
  2.1 0.0 copy-start.7
  2.1 0.1 copy-done
  2.2 1.5 %shard_map.83 = (bf16[18,16,1536]{2,1,0:T(8,128)(2,1)S(1)}, bf16[18,16,1536]{2,1,0:T(8,128)(2,1)S(1)}) custom-call(bf16[4,2,18,4,1440]{4,3,2,1,0:T(4,128)(2,1)S(1)} %bitcast.3, s32[4,1440]{1,0:T(4,128)S(1)} %copy-done.3, s32[16,128]{1,0:T(8,128)S(1)} %get-tuple-element.17.after_ref.ranges_ref), custom_call_target="tpu_custom_call" | custom-call | flops 7077888 | bytes 3538944 | tf_op jit(solution)/shard_map/pallas_call | solution.py:628
  3.7 2.0 %collective-permute-start = (bf16[18,16,1536]{2,1,0:T(8,128)(2,1)S(1)}, bf16[18,16,1536]{2,1,0:T(8,128)(2,1)S(1)}, u32[]{:S(2)}, u32[]{:S(2)}) collective-permute-start(bf16[18,16,1536]{2,1,0:T(8,128)(2,1)S(1)} %get-tuple-element.18.top_ref), channel_id=1, source_target_pairs={{1,0},{2,1},{3,2},{5,4},{6,5},{7,6},{9,8},{10,9},{11,10},{13,12},{... | collective-permute-start | bytes 2654216 | tf_op jit(solution)/shard_map/ppermute | solution.py:642
  5.7 4.5 %collective-permute-start.1 = (bf16[18,16,1536]{2,1,0:T(8,128)(2,1)S(1)}, bf16[18,16,1536]{2,1,0:T(8,128)(2,1)S(1)}, u32[]{:S(2)}, u32[]{:S(2)}) collective-permute-start(bf16[18,16,1536]{2,1,0:T(8,128)(2,1)S(1)} %get-tuple-element.19.bottom_ref), channel_id=1, source_target_pairs={{0,1},{1,2},{2,3},{4,5},{5,6},{6,7},{8,9},{9,10},{10,11},{12,13},{... | collective-permute-start | bytes 2654216 | tf_op jit(solution)/shard_map/ppermute | solution.py:643
  10.2 3.8 %shard_map.84 = (f32[18,32,1536]{2,1,0:T(8,128)S(1)}, f32[4,32,1536]{2,1,0:T(8,128)S(1)}) custom-call(bf16[18,16,1536]{2,1,0:T(8,128)(2,1)S(1)} %get-tuple-element.18.top_ref, bf16[18,16,1536]{2,1,0:T(8,128)(2,1)S(1)} %get-tuple-element.19.bottom_ref, f32[32,64]{1,0:T(8,128)S(1)} %bitcast.4, s32[4,1440]{1,0:T(4,128)S(1)} %copy-done.6, ...), custom_call_target="tpu_custom_call" | custom-call | flops 88473600 | bytes 7077888 | tf_op jit(solution)/shard_map/pallas_call | solution.py:645
  14.0 4.9 %collective-permute-done.below_ref = bf16[18,16,1536]{2,1,0:T(8,128)(2,1)S(1)} collective-permute-done((bf16[18,16,1536]{2,1,0:T(8,128)(2,1)S(1)}, bf16[18,16,1536]{2,1,0:T(8,128)(2,1)S(1)}, u32[]{:S(2)}, u32[]{:S(2)}) %collective-permute-start) | collective-permute-done | bytes 884768 | tf_op jit(solution)/shard_map/ppermute | solution.py:642
  19.0 1.2 %collective-permute-done.1.above_ref = bf16[18,16,1536]{2,1,0:T(8,128)(2,1)S(1)} collective-permute-done((bf16[18,16,1536]{2,1,0:T(8,128)(2,1)S(1)}, bf16[18,16,1536]{2,1,0:T(8,128)(2,1)S(1)}, u32[]{:S(2)}, u32[]{:S(2)}) %collective-permute-start.1) | collective-permute-done | bytes 884768 | tf_op jit(solution)/shard_map/ppermute | solution.py:643
  20.2 4.6 %shard_map.85 = (s32[1,80,640]{2,1,0:T(8,128)S(1)}, s32[1,80,640]{2,1,0:T(8,128)S(1)}, s32[1,80,640]{2,1,0:T(8,128)S(1)}, s32[1,80,640]{2,1,0:T(8,128)S(1)}) custom-call(f32[18,32,1536]{2,1,0:T(8,128)S(1)} %get-tuple-element.20.adv_ref, bf16[18,16,1536]{2,1,0:T(8,128)(2,1)S(1)} %collective-permute-done.below_ref, ...), custom_call_target="tpu_custom_call" | custom-call | flops 44236800 | bytes 5308416 | tf_op jit(solution)/shard_map/pallas_call | solution.py:666
  24.8 2.8 %collective-permute-start.3 = (s32[1,80,640]{2,1,0:T(8,128)S(1)}, s32[1,80,640]{2,1,0:T(8,128)S(1)}, u32[]{:S(2)}, u32[]{:S(2)}) collective-permute-start(s32[1,80,640]{2,1,0:T(8,128)S(1)} %get-tuple-element.24), channel_id=1, source_target_pairs={{0,20},{4,16},{8,28},{12,24},{16,4},{20,0},{24,12},{28,8},{1,21},{... | collective-permute-start | bytes 614408 | tf_op jit(solution)/shard_map/ppermute | solution.py:681
  27.6 1.6 %collective-permute-start.4 = (s32[1,80,640]{2,1,0:T(8,128)S(1)}, s32[1,80,640]{2,1,0:T(8,128)S(1)}, u32[]{:S(2)}, u32[]{:S(2)}) collective-permute-start(s32[1,80,640]{2,1,0:T(8,128)S(1)} %get-tuple-element.25), channel_id=1, source_target_pairs={{0,24},{4,28},{8,16},{12,20},{16,8},{20,12},{24,0},{28,4},{1,25},{... | collective-permute-start | bytes 614408 | tf_op jit(solution)/shard_map/ppermute | solution.py:681
  29.2 1.6 %collective-permute-start.5 = (s32[1,80,640]{2,1,0:T(8,128)S(1)}, s32[1,80,640]{2,1,0:T(8,128)S(1)}, u32[]{:S(2)}, u32[]{:S(2)}) collective-permute-start(s32[1,80,640]{2,1,0:T(8,128)S(1)} %get-tuple-element.26), channel_id=1, source_target_pairs={{0,28},{4,24},{8,20},{12,16},{16,12},{20,8},{24,4},{28,0},{1,29},{... | collective-permute-start | bytes 614408 | tf_op jit(solution)/shard_map/ppermute | solution.py:681
  30.8 5.0 %shard_map.86.after_ref = s32[4,80,640]{2,1,0:T(8,128)} custom-call(f32[18,32,1536]{2,1,0:T(8,128)S(1)} %get-tuple-element.20.adv_ref, bf16[18,16,1536]{2,1,0:T(8,128)(2,1)S(1)} %collective-permute-done.below_ref, bf16[18,16,1536]{2,1,0:T(8,128)(2,1)S(1)} %collective-permute-done.1.above_ref, f32[4,32,1536]{2,1,0:T(8,128)S(1)} %get-tuple-element.21.coef_ref, ...), custom_call_target="tpu_custom_call" | custom-call | flops 1000 | bytes 1000 | tf_op jit(solution)/shard_map/pallas_call | solution.py:666
  35.8 4.2 %all-to-all-start = ((s32[4,80,640]{2,1,0:T(8,128)}), s32[4,80,640]{2,1,0:T(8,128)}, u32[]{:S(2)}, u32[]{:S(2)}) async-start(s32[4,80,640]{2,1,0:T(8,128)} %shard_map.86.after_ref), calls=%async_computation | async-start | bytes 1638400 | tf_op jit(solution)/shard_map/all_to_all | solution.py:684
  40.0 4.0 %shard_map.87 = (f32[4,18,8,640]{3,2,1,0:T(8,128)}, f32[4,18,8,640]{3,2,1,0:T(8,128)}) custom-call(f32[2,4,1440]{2,1,0:T(4,128)} %wind_ref.1, s32[8,8,640]{2,1,0:T(8,128)} %copy-done.1, s32[16,128]{1,0:T(8,128)} %copy-done.2, s32[4,80,640]{2,1,0:T(8,128)} %shard_map.86.after_ref), custom_call_target="tpu_custom_call" | custom-call | flops 1000 | bytes 1000 | tf_op jit(solution)/shard_map/pallas_call | solution.py:688
  44.0 2.3 %collective-permute-done.3.refs_1_ = s32[1,80,640]{2,1,0:T(8,128)S(1)} collective-permute-done((s32[1,80,640]{2,1,0:T(8,128)S(1)}, s32[1,80,640]{2,1,0:T(8,128)S(1)}, u32[]{:S(2)}, u32[]{:S(2)}) %collective-permute-start.3) | collective-permute-done | bytes 204832 | tf_op jit(solution)/shard_map/ppermute | solution.py:681
  46.4 11.8 %collective-permute-done.2.refs_0_ = s32[1,80,640]{2,1,0:T(8,128)S(1)} collective-permute-done((s32[1,80,640]{2,1,0:T(8,128)S(1)}, s32[1,80,640]{2,1,0:T(8,128)S(1)}, u32[]{:S(2)}, u32[]{:S(2)}) %collective-permute-start.2) | collective-permute-done | bytes 204832 | tf_op jit(solution)/shard_map/ppermute | solution.py:681
  58.1 0.7 %copy-done.11 = s32[1,80,640]{2,1,0:T(8,128)} copy-done((s32[1,80,640]{2,1,0:T(8,128)}, s32[1,80,640]{2,1,0:T(8,128)S(1)}, u32[]{:S(2)}) %copy-start.11) | copy-done | bytes 204824
  58.8 0.6 shard_map.88.refs_7_
  59.4 6.1 %shard_map.89 = bf16[630,1152]{1,0:T(8,128)(2,1)} custom-call(s32[1,80,640]{2,1,0:T(8,128)} %copy-done.11, s32[1,80,640]{2,1,0:T(8,128)} %copy-done.8, s32[1,80,640]{2,1,0:T(8,128)} %copy-done.9, s32[1,80,640]{2,1,0:T(8,128)} %copy-done.10, s32[4,80,640]{2,1,0:T(8,128)} %all-to-all-done.refs_4_, f32[4,18,8,640]{3,2,1,0:T(8,128)} %get-tuple-element.27.refs_5_, ...), custom_call_target="tpu_custom_call" | custom-call | flops 36864000 | bytes 4423680 | tf_op jit(solution)/shard_map/pallas_call | solution.py:710
  (23 shorter events, 0.1 us)
Async XLA Ops:
  0.8 1.5 %copy-start = (bf16[4,36,4,1440]{3,2,1,0:T(4,128)(2,1)S(1)}, bf16[4,36,4,1440]{3,2,1,0:T(4,128)(2,1)}, u32[]{:S(2)}) copy-start(bf16[4,36,4,1440]{3,2,1,0:T(4,128)(2,1)} %param.8) | copy-start | bytes 4976644
  0.8 1.5 %copy-start.3 = (s32[4,1440]{1,0:T(4,128)S(1)}, s32[4,1440]{1,0:T(4,128)}, u32[]{:S(2)}) copy-start(s32[4,1440]{1,0:T(4,128)} %land_ref.1) | copy-start | bytes 69124
  2.0 28.8 %copy-start.1 = (s32[8,8,640]{2,1,0:T(8,128)}, s32[8,8,640]{2,1,0:T(8,128)S(1)}, u32[]{:S(2)}) copy-start(s32[8,8,640]{2,1,0:T(8,128)S(1)} %get-tuple-element.22.cells_ref) | copy-start | bytes 491524
  2.1 28.8 %copy-start.2 = (s32[16,128]{1,0:T(8,128)}, s32[16,128]{1,0:T(8,128)S(1)}, u32[]{:S(2)}) copy-start(s32[16,128]{1,0:T(8,128)S(1)} %get-tuple-element.17.after_ref.ranges_ref) | copy-start | bytes 24580
  2.1 8.1 %copy-start.4 = (f32[2,4,1440]{2,1,0:T(4,128)S(1)}, f32[2,4,1440]{2,1,0:T(4,128)}, u32[]{:S(2)}) copy-start(f32[2,4,1440]{2,1,0:T(4,128)} %current_ref.1) | copy-start | bytes 138244
  2.1 8.1 %copy-start.5 = (f32[2,4,1440]{2,1,0:T(4,128)S(1)}, f32[2,4,1440]{2,1,0:T(4,128)}, u32[]{:S(2)}) copy-start(f32[2,4,1440]{2,1,0:T(4,128)} %slope_ref.1) | copy-start | bytes 138244
  2.1 8.1 %copy-start.6 = (s32[4,1440]{1,0:T(4,128)S(1)}, s32[4,1440]{1,0:T(4,128)}, u32[]{:S(2)}) copy-start(s32[4,1440]{1,0:T(4,128)} %depth_ref.1) | copy-start | bytes 69124
  2.1 8.1 %copy-start.7 = (f32[64,32]{0,1:T(8,128)S(1)}, f32[64,32]{0,1:T(8,128)}, u32[]{:S(2)}) copy-start(f32[64,32]{0,1:T(8,128)} %param.10) | copy-start | bytes 24580
  3.7 15.2 %collective-permute-start = (bf16[18,16,1536]{2,1,0:T(8,128)(2,1)S(1)}, bf16[18,16,1536]{2,1,0:T(8,128)(2,1)S(1)}, u32[]{:S(2)}, u32[]{:S(2)}) collective-permute-start(bf16[18,16,1536]{2,1,0:T(8,128)(2,1)S(1)} %get-tuple-element.18.top_ref), channel_id=1, source_target_pairs={{1,0},{2,1},{3,2},{5,4},{6,5},{7,6},{9,8},{10,9},{11,10},{13,12},{... | collective-permute-start | bytes 2654216 | tf_op jit(solution)/shard_map/ppermute | solution.py:642
  5.7 14.4 %collective-permute-start.1 = (bf16[18,16,1536]{2,1,0:T(8,128)(2,1)S(1)}, bf16[18,16,1536]{2,1,0:T(8,128)(2,1)S(1)}, u32[]{:S(2)}, u32[]{:S(2)}) collective-permute-start(bf16[18,16,1536]{2,1,0:T(8,128)(2,1)S(1)} %get-tuple-element.19.bottom_ref), channel_id=1, source_target_pairs={{0,1},{1,2},{2,3},{4,5},{5,6},{6,7},{8,9},{9,10},{10,11},{12,13},{... | collective-permute-start | bytes 2654216 | tf_op jit(solution)/shard_map/ppermute | solution.py:643
  24.8 21.5 %collective-permute-start.3 = (s32[1,80,640]{2,1,0:T(8,128)S(1)}, s32[1,80,640]{2,1,0:T(8,128)S(1)}, u32[]{:S(2)}, u32[]{:S(2)}) collective-permute-start(s32[1,80,640]{2,1,0:T(8,128)S(1)} %get-tuple-element.24), channel_id=1, source_target_pairs={{0,20},{4,16},{8,28},{12,24},{16,4},{20,0},{24,12},{28,8},{1,21},{... | collective-permute-start | bytes 614408 | tf_op jit(solution)/shard_map/ppermute | solution.py:681
  27.6 18.7 %collective-permute-start.4 = (s32[1,80,640]{2,1,0:T(8,128)S(1)}, s32[1,80,640]{2,1,0:T(8,128)S(1)}, u32[]{:S(2)}, u32[]{:S(2)}) collective-permute-start(s32[1,80,640]{2,1,0:T(8,128)S(1)} %get-tuple-element.25), channel_id=1, source_target_pairs={{0,24},{4,28},{8,16},{12,20},{16,8},{20,12},{24,0},{28,4},{1,25},{... | collective-permute-start | bytes 614408 | tf_op jit(solution)/shard_map/ppermute | solution.py:681
  29.2 17.2 %collective-permute-start.5 = (s32[1,80,640]{2,1,0:T(8,128)S(1)}, s32[1,80,640]{2,1,0:T(8,128)S(1)}, u32[]{:S(2)}, u32[]{:S(2)}) collective-permute-start(s32[1,80,640]{2,1,0:T(8,128)S(1)} %get-tuple-element.26), channel_id=1, source_target_pairs={{0,28},{4,24},{8,20},{12,16},{16,12},{20,8},{24,4},{28,0},{1,29},{... | collective-permute-start | bytes 614408 | tf_op jit(solution)/shard_map/ppermute | solution.py:681
  30.8 27.3 %collective-permute-start.2 = (s32[1,80,640]{2,1,0:T(8,128)S(1)}, s32[1,80,640]{2,1,0:T(8,128)S(1)}, u32[]{:S(2)}, u32[]{:S(2)}) collective-permute-start(s32[1,80,640]{2,1,0:T(8,128)S(1)} %get-tuple-element.23.after_ref), channel_id=1, source_target_pairs={{0,16},{4,20},{8,24},{12,28},{16,0},{20,4},{24,8},{28,12},{1,17},{... | collective-permute-start | bytes 614408 | tf_op jit(solution)/shard_map/ppermute | solution.py:681
  35.8 23.6 %all-to-all-start = ((s32[4,80,640]{2,1,0:T(8,128)}), s32[4,80,640]{2,1,0:T(8,128)}, u32[]{:S(2)}, u32[]{:S(2)}) async-start(s32[4,80,640]{2,1,0:T(8,128)} %shard_map.86.after_ref), calls=%async_computation | async-start | bytes 1638400 | tf_op jit(solution)/shard_map/all_to_all | solution.py:684
  46.3 11.8 %copy-start.8 = (s32[1,80,640]{2,1,0:T(8,128)}, s32[1,80,640]{2,1,0:T(8,128)S(1)}, u32[]{:S(2)}) copy-start(s32[1,80,640]{2,1,0:T(8,128)S(1)} %collective-permute-done.3.refs_1_) | copy-start | bytes 614404
  46.3 11.8 %copy-start.9 = (s32[1,80,640]{2,1,0:T(8,128)}, s32[1,80,640]{2,1,0:T(8,128)S(1)}, u32[]{:S(2)}) copy-start(s32[1,80,640]{2,1,0:T(8,128)S(1)} %collective-permute-done.4.refs_2_) | copy-start | bytes 614404
  46.3 11.8 %copy-start.10 = (s32[1,80,640]{2,1,0:T(8,128)}, s32[1,80,640]{2,1,0:T(8,128)S(1)}, u32[]{:S(2)}) copy-start(s32[1,80,640]{2,1,0:T(8,128)S(1)} %collective-permute-done.5.refs_3_) | copy-start | bytes 614404
  58.1 0.7 %copy-start.11 = (s32[1,80,640]{2,1,0:T(8,128)}, s32[1,80,640]{2,1,0:T(8,128)S(1)}, u32[]{:S(2)}) copy-start(s32[1,80,640]{2,1,0:T(8,128)S(1)} %collective-permute-done.2.refs_0_) | copy-start | bytes 614404

commit v10 on v9

--- a/solution.py
+++ b/solution.py
@@ -661,12 +661,15 @@
     half = groups // 2
     block = (words * SUBLANES, slots)
     after, shipped = ranges, []
-    for offsets, outputs in ((range(half, groups), [(1,) + block] * half), (range(half), [(half,) + block])):
+    pair = half // 2
+    for offsets in (range(half, half + pair), range(half + pair, groups), range(half)):
+        last = len(offsets) == half
+        outputs = [(half,) + block] if last else [(1,) + block] * pair
         shipped.append(
             call(
                 functools.partial(pack_kernel, directions, tuple(offsets)),
                 [jax.ShapeDtypeStruct(shape, I32) for shape in outputs],
-                (25 * hbm, 3 * hbm) if len(outputs) > 1 else LITTLE,
+                LITTLE if shipped else (12 * hbm, 2 * hbm),
                 in_specs=[vmem] * 5 + [smem, anywhere],
                 out_specs=[vmem] * len(outputs),
                 scratch_shapes=[
@@ -676,12 +679,13 @@
                 ],
             )(advected, below, above, coefs, cells, ranges, after)
         )
-        after = shipped[0][0]
+        after = shipped[-1][0]
     far = [
-        lax.ppermute(part, "comp", [(i, i ^ (half + n)) for i in range(groups)]) for n, part in enumerate(shipped[0])
+        lax.ppermute(part, "comp", [(i, i ^ (half + n)) for i in range(groups)])
+        for n, part in enumerate(shipped[0] + shipped[1])
     ]
     halves = [list(range(half)), list(range(half, groups))]
-    near = lax.all_to_all(shipped[1][0], "comp", split_axis=0, concat_axis=0, axis_index_groups=halves, tiled=True)
+    near = lax.all_to_all(shipped[2][0], "comp", split_axis=0, concat_axis=0, axis_index_groups=halves, tiled=True)
 
     total = total_freqs * directions
     values = jax.ShapeDtypeStruct((half, turns, SUBLANES, slots), F32)
@@ -696,7 +700,7 @@
             pltpu.VMEM((rows * chunks, SUBLANES, LANES), F32),
             pltpu.VMEM((2, SUBLANES, slots), F32),
         ],
-    )(wind, cells, ranges, shipped[1][0])
+    )(wind, cells, ranges, shipped[2][0])
 
     gate = call(
         gate_kernel,

time: 66 us -> 63.6 us (0.964)
  waiting for transfers between devices: 20.2 us -> 14.3 us
  Pallas kernels: 26.9 us -> 28.5 us
  starting transfers between devices: 16.7 us -> 18 us
  local copies, waits for them, and re-layouts: 0.84 us -> 1.62 us
    ppermute x4, waiting for transfers between devices: 14.1 us -> 2.65 us  [body(): lax.ppermute(part, 'comp', [(i, i ^ half + n) for i in range(groups)])]
    all_to_all x1, waiting for transfers between devices: 0.01 us -> 5.53 us  [body(): lax.all_to_all(shipped[2][0], 'comp', split_axis=0, concat_axis=0, axis_i...]
    pallas_call x2 -> x3, Pallas kernels: 9.61 us -> 11.1 us  [body(): call(functools.partial(pack_kernel, directions, tuple(offsets)), [jax.Sha...]
    ppermute x4, starting transfers between devices: 6.02 us -> 7.36 us  [body(): lax.ppermute(part, 'comp', [(i, i ^ half + n) for i in range(groups)])]
    unnamed x24, local copies, waits for them, and re-layouts: 0.84 us -> 1.62 us
  transfers between devices with their start and end apart: 7 -> 7, of which waited for: 4 -> 4; matrix products, arithmetic and copies ran while one was open for 0% -> 0% of each run, Pallas kernels for 20% -> 27%
where the time goes in v10:
time: 63.6 us; the launch traced here: 63.5 us
  Pallas kernels  28.5 us (45%)
  starting transfers between devices  18 us (28%)
  waiting for transfers between devices  14.3 us (22%)
  local copies, waits for them, and re-layouts  1.62 us (3%)
  other arithmetic  0.76 us (1%)
    pallas_call x3, Pallas kernels, body(): call(functools.partial(pack_kernel, directions, tuple(offsets)), [jax.Sha...  11.1 us
    ppermute x4, starting transfers between devices, body(): lax.ppermute(part, 'comp', [(i, i ^ half + n) for i in range(groups)])  7.36 us
    pallas_call x1, Pallas kernels, body(): call(functools.partial(finish_kernel, freqs, half), jax.ShapeDtypeStruct(...  6.14 us
    all_to_all x1, waiting for transfers between devices, body(): lax.all_to_all(shipped[2][0], 'comp', split_axis=0, concat_axis=0, axis_i...  5.53 us
    ppermute x1, waiting for transfers between devices, body(): below = lax.ppermute(top, 'band', [(j, i) for i, j in down])  4.93 us
    ppermute x1, starting transfers between devices, body(): above = lax.ppermute(bottom, 'band', down)  4.46 us
    all_to_all x1, starting transfers between devices, body(): lax.all_to_all(shipped[2][0], 'comp', split_axis=0, concat_axis=0, axis_i...  4.2 us
    pallas_call x1, Pallas kernels, body(): call(functools.partial(grow_kernel, directions), [values, values], LITTLE...  4.1 us
  transfers between devices with their start and end apart: 7, of which 4 were waited for; matrix products, arithmetic and copies ran while one was open for 0% of the time, Pallas kernels for 27%

profile of v10, /device:TPU:1, one launch (start us, length us, event | category | flops | bytes accessed | tf_op | source)
XLA Modules:
  0.0 63.5 jit_solution(1603714897691200141)
XLA Ops:
  0.0 0.8 %pad_add_fusion.land_ref = s32[5,1440]{1,0:T(8,128)S(1)} fusion(s32[1,8]{1,0:T(1,128)} %refs_8_.1, s32[4,1440]{1,0:T(4,128)} %land_ref.1), kind=kLoop, calls=%fused_computation | loop fusion | flops 7200 | bytes 51872 | tf_op jit(solution)/shard_map/concatenate | solution.py:623
  0.8 1.3 %shard_map.82 = (s32[8,8,640]{2,1,0:T(8,128)S(1)}, s32[16,128]{1,0:T(8,128)S(1)}) custom-call(s32[5,1440]{1,0:T(8,128)S(1)} %pad_add_fusion.land_ref), custom_call_target="tpu_custom_call" | custom-call | flops 2048000000 | bytes 40960 | tf_op jit(solution)/shard_map/pallas_call | solution.py:613
  2.1 0.1 copy-done.1
  2.2 1.5 %shard_map.83 = (bf16[18,16,1536]{2,1,0:T(8,128)(2,1)S(1)}, bf16[18,16,1536]{2,1,0:T(8,128)(2,1)S(1)}) custom-call(bf16[4,2,18,4,1440]{4,3,2,1,0:T(4,128)(2,1)S(1)} %bitcast.3, s32[4,1440]{1,0:T(4,128)S(1)} %copy-done.3, s32[16,128]{1,0:T(8,128)S(1)} %get-tuple-element.17.after_ref.ranges_ref), custom_call_target="tpu_custom_call" | custom-call | flops 7077888 | bytes 3538944 | tf_op jit(solution)/shard_map/pallas_call | solution.py:628
  3.7 2.0 %collective-permute-start = (bf16[18,16,1536]{2,1,0:T(8,128)(2,1)S(1)}, bf16[18,16,1536]{2,1,0:T(8,128)(2,1)S(1)}, u32[]{:S(2)}, u32[]{:S(2)}) collective-permute-start(bf16[18,16,1536]{2,1,0:T(8,128)(2,1)S(1)} %get-tuple-element.18.top_ref), channel_id=1, source_target_pairs={{1,0},{2,1},{3,2},{5,4},{6,5},{7,6},{9,8},{10,9},{11,10},{13,12},{... | collective-permute-start | bytes 2654216 | tf_op jit(solution)/shard_map/ppermute | solution.py:642
  5.7 4.5 %collective-permute-start.1 = (bf16[18,16,1536]{2,1,0:T(8,128)(2,1)S(1)}, bf16[18,16,1536]{2,1,0:T(8,128)(2,1)S(1)}, u32[]{:S(2)}, u32[]{:S(2)}) collective-permute-start(bf16[18,16,1536]{2,1,0:T(8,128)(2,1)S(1)} %get-tuple-element.19.bottom_ref), channel_id=1, source_target_pairs={{0,1},{1,2},{2,3},{4,5},{5,6},{6,7},{8,9},{9,10},{10,11},{12,13},{... | collective-permute-start | bytes 2654216 | tf_op jit(solution)/shard_map/ppermute | solution.py:643
  10.2 3.8 %shard_map.84 = (f32[18,32,1536]{2,1,0:T(8,128)S(1)}, f32[4,32,1536]{2,1,0:T(8,128)S(1)}) custom-call(bf16[18,16,1536]{2,1,0:T(8,128)(2,1)S(1)} %get-tuple-element.18.top_ref, bf16[18,16,1536]{2,1,0:T(8,128)(2,1)S(1)} %get-tuple-element.19.bottom_ref, f32[32,64]{1,0:T(8,128)S(1)} %bitcast.4, s32[4,1440]{1,0:T(4,128)S(1)} %copy-done.6, ...), custom_call_target="tpu_custom_call" | custom-call | flops 88473600 | bytes 7077888 | tf_op jit(solution)/shard_map/pallas_call | solution.py:645
  14.0 4.9 %collective-permute-done.below_ref = bf16[18,16,1536]{2,1,0:T(8,128)(2,1)S(1)} collective-permute-done((bf16[18,16,1536]{2,1,0:T(8,128)(2,1)S(1)}, bf16[18,16,1536]{2,1,0:T(8,128)(2,1)S(1)}, u32[]{:S(2)}, u32[]{:S(2)}) %collective-permute-start) | collective-permute-done | bytes 884768 | tf_op jit(solution)/shard_map/ppermute | solution.py:642
  19.0 1.2 %collective-permute-done.1.above_ref = bf16[18,16,1536]{2,1,0:T(8,128)(2,1)S(1)} collective-permute-done((bf16[18,16,1536]{2,1,0:T(8,128)(2,1)S(1)}, bf16[18,16,1536]{2,1,0:T(8,128)(2,1)S(1)}, u32[]{:S(2)}, u32[]{:S(2)}) %collective-permute-start.1) | collective-permute-done | bytes 884768 | tf_op jit(solution)/shard_map/ppermute | solution.py:643
  20.2 2.4 %shard_map.85 = (s32[1,80,640]{2,1,0:T(8,128)S(1)}, s32[1,80,640]{2,1,0:T(8,128)S(1)}) custom-call(f32[18,32,1536]{2,1,0:T(8,128)S(1)} %get-tuple-element.20.adv_ref, bf16[18,16,1536]{2,1,0:T(8,128)(2,1)S(1)} %collective-permute-done.below_ref, bf16[18,16,1536]{2,1,0:T(8,128)(2,1)S(1)} %collective-permute-done.1.above_ref, ...), custom_call_target="tpu_custom_call" | custom-call | flops 21233664 | bytes 3538944 | tf_op jit(solution)/shard_map/pallas_call | solution.py:669
  22.6 4.0 %collective-permute-start.3 = (s32[1,80,640]{2,1,0:T(8,128)S(1)}, s32[1,80,640]{2,1,0:T(8,128)S(1)}, u32[]{:S(2)}, u32[]{:S(2)}) collective-permute-start(s32[1,80,640]{2,1,0:T(8,128)S(1)} %get-tuple-element.24), channel_id=1, source_target_pairs={{0,20},{4,16},{8,28},{12,24},{16,4},{20,0},{24,12},{28,8},{1,21},{... | collective-permute-start | bytes 614408 | tf_op jit(solution)/shard_map/ppermute | solution.py:684
  26.5 3.0 %shard_map.86 = (s32[1,80,640]{2,1,0:T(8,128)S(1)}, s32[1,80,640]{2,1,0:T(8,128)S(1)}) custom-call(f32[18,32,1536]{2,1,0:T(8,128)S(1)} %get-tuple-element.20.adv_ref, bf16[18,16,1536]{2,1,0:T(8,128)(2,1)S(1)} %collective-permute-done.below_ref, bf16[18,16,1536]{2,1,0:T(8,128)(2,1)S(1)} %collective-permute-done.1.above_ref, ...), custom_call_target="tpu_custom_call" | custom-call | flops 1000 | bytes 1000 | tf_op jit(solution)/shard_map/pallas_call | solution.py:669
  29.5 3.3 %collective-permute-start.5 = (s32[1,80,640]{2,1,0:T(8,128)S(1)}, s32[1,80,640]{2,1,0:T(8,128)S(1)}, u32[]{:S(2)}, u32[]{:S(2)}) collective-permute-start(s32[1,80,640]{2,1,0:T(8,128)S(1)} %get-tuple-element.26), channel_id=1, source_target_pairs={{0,28},{4,24},{8,20},{12,16},{16,12},{20,8},{24,4},{28,0},{1,29},{... | collective-permute-start | bytes 614408 | tf_op jit(solution)/shard_map/ppermute | solution.py:684
  32.8 0.1 collective-permute-start.4
  33.0 5.7 %shard_map.87.after_ref = s32[4,80,640]{2,1,0:T(8,128)} custom-call(f32[18,32,1536]{2,1,0:T(8,128)S(1)} %get-tuple-element.20.adv_ref, bf16[18,16,1536]{2,1,0:T(8,128)(2,1)S(1)} %collective-permute-done.below_ref, bf16[18,16,1536]{2,1,0:T(8,128)(2,1)S(1)} %collective-permute-done.1.above_ref, f32[4,32,1536]{2,1,0:T(8,128)S(1)} %get-tuple-element.21.coef_ref, ...), custom_call_target="tpu_custom_call" | custom-call | flops 1000 | bytes 1000 | tf_op jit(solution)/shard_map/pallas_call | solution.py:669
  38.6 4.2 %all-to-all-start = ((s32[4,80,640]{2,1,0:T(8,128)}), s32[4,80,640]{2,1,0:T(8,128)}, u32[]{:S(2)}, u32[]{:S(2)}) async-start(s32[4,80,640]{2,1,0:T(8,128)} %shard_map.87.after_ref), calls=%async_computation | async-start | bytes 1638400 | tf_op jit(solution)/shard_map/all_to_all | solution.py:688
  42.9 4.1 %shard_map.88 = (f32[4,18,8,640]{3,2,1,0:T(8,128)}, f32[4,18,8,640]{3,2,1,0:T(8,128)}) custom-call(f32[2,4,1440]{2,1,0:T(4,128)} %wind_ref.1, s32[8,8,640]{2,1,0:T(8,128)} %copy-done, s32[16,128]{1,0:T(8,128)} %copy-done.2, s32[4,80,640]{2,1,0:T(8,128)} %shard_map.87.after_ref), custom_call_target="tpu_custom_call" | custom-call | flops 1000 | bytes 1000 | tf_op jit(solution)/shard_map/pallas_call | solution.py:692
  47.0 2.6 %collective-permute-done.2.refs_0_ = s32[1,80,640]{2,1,0:T(8,128)S(1)} collective-permute-done((s32[1,80,640]{2,1,0:T(8,128)S(1)}, s32[1,80,640]{2,1,0:T(8,128)S(1)}, u32[]{:S(2)}, u32[]{:S(2)}) %collective-permute-start.2) | collective-permute-done | bytes 204832 | tf_op jit(solution)/shard_map/ppermute | solution.py:684
  49.6 0.6 %copy-done.9 = s32[1,80,640]{2,1,0:T(8,128)} copy-done((s32[1,80,640]{2,1,0:T(8,128)}, s32[1,80,640]{2,1,0:T(8,128)S(1)}, u32[]{:S(2)}) %copy-start.9) | copy-done | bytes 204824
  50.3 0.1 copy-done.10
  50.4 0.7 %copy-done.11 = s32[1,80,640]{2,1,0:T(8,128)} copy-done((s32[1,80,640]{2,1,0:T(8,128)}, s32[1,80,640]{2,1,0:T(8,128)S(1)}, u32[]{:S(2)}) %copy-start.11) | copy-done | bytes 204824
  51.1 0.6 shard_map.89.refs_7_
  51.7 5.5 %all-to-all-done.refs_4_ = s32[4,80,640]{2,1,0:T(8,128)} async-done(((s32[4,80,640]{2,1,0:T(8,128)}), s32[4,80,640]{2,1,0:T(8,128)}, u32[]{:S(2)}, u32[]{:S(2)}) %all-to-all-start) | async-done | bytes 819232 | tf_op jit(solution)/shard_map/all_to_all | solution.py:688
  57.2 6.1 %shard_map.90 = bf16[630,1152]{1,0:T(8,128)(2,1)} custom-call(s32[1,80,640]{2,1,0:T(8,128)} %copy-done.9, s32[1,80,640]{2,1,0:T(8,128)} %copy-done.8, s32[1,80,640]{2,1,0:T(8,128)} %copy-done.11, s32[1,80,640]{2,1,0:T(8,128)} %copy-done.10, s32[4,80,640]{2,1,0:T(8,128)} %all-to-all-done.refs_4_, f32[4,18,8,640]{3,2,1,0:T(8,128)} %get-tuple-element.27.refs_5_, ...), custom_call_target="tpu_custom_call" | custom-call | flops 36864000 | bytes 4423680 | tf_op jit(solution)/shard_map/pallas_call | solution.py:714
  (24 shorter events, 0.1 us)
Async XLA Ops:
  0.8 1.5 %copy-start.1 = (bf16[4,36,4,1440]{3,2,1,0:T(4,128)(2,1)S(1)}, bf16[4,36,4,1440]{3,2,1,0:T(4,128)(2,1)}, u32[]{:S(2)}) copy-start(bf16[4,36,4,1440]{3,2,1,0:T(4,128)(2,1)} %param.8) | copy-start | bytes 4976644
  0.8 1.5 %copy-start.3 = (s32[4,1440]{1,0:T(4,128)S(1)}, s32[4,1440]{1,0:T(4,128)}, u32[]{:S(2)}) copy-start(s32[4,1440]{1,0:T(4,128)} %land_ref.1) | copy-start | bytes 69124
  2.0 30.9 %copy-start = (s32[8,8,640]{2,1,0:T(8,128)}, s32[8,8,640]{2,1,0:T(8,128)S(1)}, u32[]{:S(2)}) copy-start(s32[8,8,640]{2,1,0:T(8,128)S(1)} %get-tuple-element.22.cells_ref) | copy-start | bytes 491524
  2.1 30.9 %copy-start.2 = (s32[16,128]{1,0:T(8,128)}, s32[16,128]{1,0:T(8,128)S(1)}, u32[]{:S(2)}) copy-start(s32[16,128]{1,0:T(8,128)S(1)} %get-tuple-element.17.after_ref.ranges_ref) | copy-start | bytes 24580
  2.1 8.1 %copy-start.4 = (f32[2,4,1440]{2,1,0:T(4,128)S(1)}, f32[2,4,1440]{2,1,0:T(4,128)}, u32[]{:S(2)}) copy-start(f32[2,4,1440]{2,1,0:T(4,128)} %current_ref.1) | copy-start | bytes 138244
  2.1 8.1 %copy-start.5 = (f32[2,4,1440]{2,1,0:T(4,128)S(1)}, f32[2,4,1440]{2,1,0:T(4,128)}, u32[]{:S(2)}) copy-start(f32[2,4,1440]{2,1,0:T(4,128)} %slope_ref.1) | copy-start | bytes 138244
  2.1 8.1 %copy-start.6 = (s32[4,1440]{1,0:T(4,128)S(1)}, s32[4,1440]{1,0:T(4,128)}, u32[]{:S(2)}) copy-start(s32[4,1440]{1,0:T(4,128)} %depth_ref.1) | copy-start | bytes 69124
  2.1 8.1 %copy-start.7 = (f32[64,32]{0,1:T(8,128)S(1)}, f32[64,32]{0,1:T(8,128)}, u32[]{:S(2)}) copy-start(f32[64,32]{0,1:T(8,128)} %param.10) | copy-start | bytes 24580
  3.7 15.2 %collective-permute-start = (bf16[18,16,1536]{2,1,0:T(8,128)(2,1)S(1)}, bf16[18,16,1536]{2,1,0:T(8,128)(2,1)S(1)}, u32[]{:S(2)}, u32[]{:S(2)}) collective-permute-start(bf16[18,16,1536]{2,1,0:T(8,128)(2,1)S(1)} %get-tuple-element.18.top_ref), channel_id=1, source_target_pairs={{1,0},{2,1},{3,2},{5,4},{6,5},{7,6},{9,8},{10,9},{11,10},{13,12},{... | collective-permute-start | bytes 2654216 | tf_op jit(solution)/shard_map/ppermute | solution.py:642
  5.7 14.4 %collective-permute-start.1 = (bf16[18,16,1536]{2,1,0:T(8,128)(2,1)S(1)}, bf16[18,16,1536]{2,1,0:T(8,128)(2,1)S(1)}, u32[]{:S(2)}, u32[]{:S(2)}) collective-permute-start(bf16[18,16,1536]{2,1,0:T(8,128)(2,1)S(1)} %get-tuple-element.19.bottom_ref), channel_id=1, source_target_pairs={{0,1},{1,2},{2,3},{4,5},{5,6},{6,7},{8,9},{9,10},{10,11},{12,13},{... | collective-permute-start | bytes 2654216 | tf_op jit(solution)/shard_map/ppermute | solution.py:643
  22.6 24.4 %collective-permute-start.3 = (s32[1,80,640]{2,1,0:T(8,128)S(1)}, s32[1,80,640]{2,1,0:T(8,128)S(1)}, u32[]{:S(2)}, u32[]{:S(2)}) collective-permute-start(s32[1,80,640]{2,1,0:T(8,128)S(1)} %get-tuple-element.24), channel_id=1, source_target_pairs={{0,20},{4,16},{8,28},{12,24},{16,4},{20,0},{24,12},{28,8},{1,21},{... | collective-permute-start | bytes 614408 | tf_op jit(solution)/shard_map/ppermute | solution.py:684
  26.5 23.1 %collective-permute-start.2 = (s32[1,80,640]{2,1,0:T(8,128)S(1)}, s32[1,80,640]{2,1,0:T(8,128)S(1)}, u32[]{:S(2)}, u32[]{:S(2)}) collective-permute-start(s32[1,80,640]{2,1,0:T(8,128)S(1)} %get-tuple-element.23.after_ref), channel_id=1, source_target_pairs={{0,16},{4,20},{8,24},{12,28},{16,0},{20,4},{24,8},{28,12},{1,17},{... | collective-permute-start | bytes 614408 | tf_op jit(solution)/shard_map/ppermute | solution.py:684
  29.5 20.1 %collective-permute-start.5 = (s32[1,80,640]{2,1,0:T(8,128)S(1)}, s32[1,80,640]{2,1,0:T(8,128)S(1)}, u32[]{:S(2)}, u32[]{:S(2)}) collective-permute-start(s32[1,80,640]{2,1,0:T(8,128)S(1)} %get-tuple-element.26), channel_id=1, source_target_pairs={{0,28},{4,24},{8,20},{12,16},{16,12},{20,8},{24,4},{28,0},{1,29},{... | collective-permute-start | bytes 614408 | tf_op jit(solution)/shard_map/ppermute | solution.py:684
  32.8 16.8 %collective-permute-start.4 = (s32[1,80,640]{2,1,0:T(8,128)S(1)}, s32[1,80,640]{2,1,0:T(8,128)S(1)}, u32[]{:S(2)}, u32[]{:S(2)}) collective-permute-start(s32[1,80,640]{2,1,0:T(8,128)S(1)} %get-tuple-element.25.after_ref), channel_id=1, source_target_pairs={{0,24},{4,28},{8,16},{12,20},{16,8},{20,12},{24,0},{28,4},{1,25},{... | collective-permute-start | bytes 614408 | tf_op jit(solution)/shard_map/ppermute | solution.py:684
  38.6 18.6 %all-to-all-start = ((s32[4,80,640]{2,1,0:T(8,128)}), s32[4,80,640]{2,1,0:T(8,128)}, u32[]{:S(2)}, u32[]{:S(2)}) async-start(s32[4,80,640]{2,1,0:T(8,128)} %shard_map.87.after_ref), calls=%async_computation | async-start | bytes 1638400 | tf_op jit(solution)/shard_map/all_to_all | solution.py:688
  47.0 2.7 %copy-start.8 = (s32[1,80,640]{2,1,0:T(8,128)}, s32[1,80,640]{2,1,0:T(8,128)S(1)}, u32[]{:S(2)}) copy-start(s32[1,80,640]{2,1,0:T(8,128)S(1)} %collective-permute-done.3.refs_1_) | copy-start | bytes 614404
  49.6 0.7 %copy-start.9 = (s32[1,80,640]{2,1,0:T(8,128)}, s32[1,80,640]{2,1,0:T(8,128)S(1)}, u32[]{:S(2)}) copy-start(s32[1,80,640]{2,1,0:T(8,128)S(1)} %collective-permute-done.2.refs_0_) | copy-start | bytes 614404
  49.6 0.8 %copy-start.10 = (s32[1,80,640]{2,1,0:T(8,128)}, s32[1,80,640]{2,1,0:T(8,128)S(1)}, u32[]{:S(2)}) copy-start(s32[1,80,640]{2,1,0:T(8,128)S(1)} %collective-permute-done.5.refs_3_) | copy-start | bytes 614404
  50.4 0.7 %copy-start.11 = (s32[1,80,640]{2,1,0:T(8,128)}, s32[1,80,640]{2,1,0:T(8,128)S(1)}, u32[]{:S(2)}) copy-start(s32[1,80,640]{2,1,0:T(8,128)S(1)} %collective-permute-done.4.refs_2_) | copy-start | bytes 614404
